TPU v7x, 256 devices: a whole 4x4x8 slice. The times are simulated.
256 devices in a mesh: rep: 2 (over y_lo), dp: 16 (over z, core), tensor: 8 (over x, y_hi).
Axes of the slice: x: 4, y: 4 (y_hi: 2, y_lo: 2; y = y_hi * 2 + y_lo), z: 8, core: 2. Of those that a mesh axis runs over, the one named last changes fastest.
Arguments:
- z_act: bfloat16 [4096, 8192], P(('rep', 'dp'), 'tensor'), may hold values from -6 to 6
- x_act: bfloat16 [4096, 8192], P(('rep', 'dp'), 'tensor'), may hold values from -6 to 6
- b_act: bfloat16 [4096, 1024], P(('rep', 'dp'), 'tensor'), may hold values from -6 to 6
- c_act: bfloat16 [4096, 1024], P(('rep', 'dp'), 'tensor'), may hold values from -6 to 6
- dt_act: bfloat16 [4096, 128], P(('rep', 'dp'), 'tensor'), may hold values from -6 to 6
- segment: int32 [4096], P(('rep', 'dp')), may hold values from 0 to 15, as said below
- counts: int32 [32], P(('rep', 'dp')), may hold values from 32 to 128, as said below
- conv_x: float32 [4, 8192], P(None, 'tensor'), may hold values from -3 to 3
- conv_b: float32 [4, 1024], P(None, 'tensor'), may hold values from -3 to 3
- conv_c: float32 [4, 1024], P(None, 'tensor'), may hold values from -3 to 3
- a_log: float32 [128], P('tensor'), may hold values from -3 to 1.5
- dt_bias: float32 [128], P('tensor'), may hold values from -6 to -2
- d_skip: float32 [128], P('tensor'), may hold values from 0.5 to 1.5
- norm_gain: float32 [8192], P('tensor'), may hold values from 0.5 to 1.5
- w_out: bfloat16 [4096, 8192], P('dp', 'tensor'), may hold values from -0.0625 to 0.0625
- d_out: bfloat16 [4096, 4096], P(('rep', 'dp', 'tensor')), may hold values from -24 to 24
Outputs:
- grad_z: bfloat16 [4096, 8192], P(('rep', 'dp'), 'tensor')
- grad_x: bfloat16 [4096, 8192], P(('rep', 'dp'), 'tensor')
- grad_b: bfloat16 [4096, 1024], P(('rep', 'dp'), 'tensor')
- grad_c: bfloat16 [4096, 1024], P(('rep', 'dp'), 'tensor')
- grad_dt: bfloat16 [4096, 128], P(('rep', 'dp'), 'tensor')
- grad_conv_x: float32 [4, 8192], P(None, 'tensor')
- grad_conv_b: float32 [4, 1024], P(None, 'tensor')
- grad_conv_c: float32 [4, 1024], P(None, 'tensor')
- grad_a_log: float32 [128], P('tensor')
- grad_dt_bias: float32 [128], P('tensor')
- grad_d_skip: float32 [128], P('tensor')
- grad_norm_gain: float32 [8192], P('tensor')
- grad_w_out: float32 [4096, 8192], P('dp', 'tensor')
Inputs may be any that keep to these rules, and one draw needn't show every extreme that they name: counts[j] is the number of live slots of shard j; some shard has exactly 128. Within each shard segment starts at 0 and never falls along the slots.
All inputs are finite; a program needn't handle non-finite values.
Results may differ from a plain program's by a relative error of at most 0.0055.
Values may be sent and summed in bfloat16 or wider, within the bound.
No kernel may reach another device: no remote copies, remote signals or barrier semaphores. Data moves between devices by JAX's collectives and lax.ppermute only.
A program may use at most 128 MiB of HBM per device.

v0:
```python
import jax
import jax.numpy as jnp
from jax import lax
from jax.sharding import PartitionSpec as P

HDIM = 64
NST = 128
SPAN = 128
KCONV = 4


def conv_doc(values, taps, segment):
    length = values.shape[0]
    summed = jnp.zeros_like(values)
    for offset in range(KCONV):
        tap_index = KCONV - 1 - offset
        if offset == 0:
            shifted = values
            same_doc = segment == segment
        else:
            shifted = jnp.pad(values, ((offset, 0), (0, 0)))[:length]
            prior_seg = jnp.pad(segment, (offset, 0), constant_values=-1)[:length]
            same_doc = prior_seg == segment
        summed = summed + taps[tap_index][None, :] * jnp.where(
            same_doc[:, None], shifted, jnp.zeros_like(shifted)
        )
    return jax.nn.silu(summed)


def span_step(carry, inputs):
    ssm_state, prior_seg = carry
    x_blk, b_blk, c_blk, dt_blk, la_blk, seg_blk = inputs
    head_count = x_blk.shape[1]
    per_group = head_count // b_blk.shape[1]
    highest = lax.Precision.HIGHEST
    cumul = jnp.cumsum(la_blk, axis=0)
    positions = jnp.arange(seg_blk.shape[0])
    causal = (positions[:, None] >= positions[None, :]) & (seg_blk[:, None] == seg_blk[None, :])
    log_gap = cumul.T[:, :, None] - cumul.T[:, None, :]
    decay_mat = jnp.exp(jnp.where(causal[None], log_gap, -1e30))
    scores = jnp.einsum("tgn,sgn->gts", c_blk, b_blk, precision=highest)
    scores = jnp.repeat(scores, per_group, axis=0)
    weights = scores * decay_mat * dt_blk.T[:, None, :]
    intra_out = jnp.einsum("hts,shp->thp", weights, x_blk, precision=highest)
    keep_rows = (seg_blk == prior_seg).astype(cumul.dtype)
    c_heads = jnp.repeat(c_blk, per_group, axis=1)
    b_heads = jnp.repeat(b_blk, per_group, axis=1)
    inter_out = jnp.einsum("thn,hpn->thp", c_heads, ssm_state, precision=highest)
    inter_out = inter_out * (jnp.exp(cumul) * keep_rows[:, None])[:, :, None]
    last_seg = seg_blk[-1]
    tail_weight = (
        jnp.exp(cumul[-1][None, :] - cumul)
        * dt_blk
        * (seg_blk == last_seg).astype(cumul.dtype)[:, None]
    )
    fresh_state = jnp.einsum("sh,shp,shn->hpn", tail_weight, x_blk, b_heads, precision=highest)
    keep_state = (last_seg == prior_seg).astype(cumul.dtype)
    carried = keep_state * jnp.exp(cumul[-1])[:, None, None] * ssm_state
    return ((carried + fresh_state, last_seg), intra_out + inter_out)


def mixer_forward(
    z_act,
    x_act,
    b_act,
    c_act,
    dt_act,
    conv_x,
    conv_b,
    conv_c,
    a_log,
    dt_bias,
    d_skip,
    norm_gain,
    segment,
):
    length = x_act.shape[0]
    head_count = dt_act.shape[1]
    groups = b_act.shape[1] // NST
    x_conv = conv_doc(x_act.astype(jnp.float32), conv_x, segment)
    b_conv = conv_doc(b_act.astype(jnp.float32), conv_b, segment)
    c_conv = conv_doc(c_act.astype(jnp.float32), conv_c, segment)
    dt_step = jax.nn.softplus(dt_act.astype(jnp.float32) + dt_bias[None, :])
    log_decay = dt_step * (-jnp.exp(a_log))[None, :]
    blocks = length // SPAN
    span_inputs = (
        x_conv.reshape(blocks, SPAN, head_count, HDIM),
        b_conv.reshape(blocks, SPAN, groups, NST),
        c_conv.reshape(blocks, SPAN, groups, NST),
        dt_step.reshape(blocks, SPAN, head_count),
        log_decay.reshape(blocks, SPAN, head_count),
        segment.reshape(blocks, SPAN),
    )
    initial = (jnp.zeros((head_count, HDIM, NST), jnp.float32), jnp.array(-1, jnp.int32))
    final_state, outputs = lax.scan(span_step, initial, span_inputs)
    ssm_out = outputs.reshape(length, head_count, HDIM) + d_skip[None, :, None] * x_conv.reshape(
        length, head_count, HDIM
    )
    gated_out = ssm_out.reshape(length, head_count * HDIM) * jax.nn.silu(z_act.astype(jnp.float32))
    grouped = gated_out.reshape(length, groups, -1)
    inv_rms = lax.rsqrt(jnp.mean(grouped * grouped, axis=-1, keepdims=True) + 1e-05)
    return (grouped * inv_rms).reshape(length, head_count * HDIM) * norm_gain[None, :]


def body(
    z_act,
    x_act,
    b_act,
    c_act,
    dt_act,
    segment,
    counts,
    conv_x,
    conv_b,
    conv_c,
    a_log,
    dt_bias,
    d_skip,
    norm_gain,
    w_out,
    d_out,
):
    length = z_act.shape[0]
    live_rows = jnp.arange(length) < counts[0]
    gathered = lax.all_gather(d_out, "tensor", axis=0, tiled=True)
    masked = jnp.where(live_rows[:, None], gathered, jnp.zeros_like(gathered))
    params = (conv_x, conv_b, conv_c, a_log, dt_bias, d_skip, norm_gain)

    def forward(activations, weights):
        return mixer_forward(
            activations[0],
            activations[1],
            activations[2],
            activations[3],
            activations[4],
            weights[0],
            weights[1],
            weights[2],
            weights[3],
            weights[4],
            weights[5],
            weights[6],
            segment,
        )

    normed, pullback = jax.vjp(forward, (z_act, x_act, b_act, c_act, dt_act), params)
    normed_b = normed.astype(jnp.bfloat16)
    dy_block = masked
    upstream = jnp.dot(
        dy_block,
        lax.all_gather(w_out, "dp", axis=0, tiled=True),
        preferred_element_type=jnp.float32,
    )
    act_grads, param_grads = pullback(upstream)
    sums = lax.psum(
        (
            param_grads[0],
            param_grads[1],
            param_grads[2],
            param_grads[3],
            param_grads[4],
            param_grads[5],
            param_grads[6],
        ),
        ("rep", "dp"),
    )
    dy_block = masked
    shares = lax.psum_scatter(
        lax.dot_general(
            dy_block, normed_b, (((0,), (0,)), ((), ())), preferred_element_type=jnp.float32
        ),
        "dp",
        scatter_dimension=0,
        tiled=True,
    )
    weight_grad = lax.psum(shares, "rep")
    return (
        act_grads[0],
        act_grads[1],
        act_grads[2],
        act_grads[3],
        act_grads[4],
        sums[0],
        sums[1],
        sums[2],
        sums[3],
        sums[4],
        sums[5],
        sums[6],
        weight_grad,
    )


def solution(mesh):
    in_specs = (
        P(("rep", "dp"), "tensor"),
        P(("rep", "dp"), "tensor"),
        P(("rep", "dp"), "tensor"),
        P(("rep", "dp"), "tensor"),
        P(("rep", "dp"), "tensor"),
        P(("rep", "dp")),
        P(("rep", "dp")),
        P(None, "tensor"),
        P(None, "tensor"),
        P(None, "tensor"),
        P("tensor"),
        P("tensor"),
        P("tensor"),
        P("tensor"),
        P("dp", "tensor"),
        P(("rep", "dp", "tensor"), None),
    )
    out_specs = (
        P(("rep", "dp"), "tensor"),
        P(("rep", "dp"), "tensor"),
        P(("rep", "dp"), "tensor"),
        P(("rep", "dp"), "tensor"),
        P(("rep", "dp"), "tensor"),
        P(None, "tensor"),
        P(None, "tensor"),
        P(None, "tensor"),
        P("tensor"),
        P("tensor"),
        P("tensor"),
        P("tensor"),
        P("dp", "tensor"),
    )
    return jax.shard_map(body, mesh=mesh, in_specs=in_specs, out_specs=out_specs, check_vma=False)
```

profile of v0, /device:TPU:2, one launch (start us, length us, event | category | flops | bytes accessed | tf_op | source)
XLA Modules:
  0.0 347.0 jit_solution(9510845905680853121)
XLA Ops:
  16.4 1.5 compare_convert_fusion
  22.5 2.9 multiply_reduce_fusion.2
  25.4 1.4 fusion.90
  27.1 2.1 convolution_bitcast_fusion.2
  29.3 2.2 fusion.1
  32.9 34.1 %all-gather.3.cloned.1.call-done = bf16[128,4096]{1,0:T(8,128)(2,1)} async-done(((bf16[16,4096]{1,0:T(8,128)(2,1)}), bf16[128,4096]{1,0:T(8,128)(2,1)}) %all-gather.3.cloned.1.call-update) | async-done | bytes 1048592 | tf_op jit(solution)/shard_map/all_gather | solution.py:125
  67.0 9.4 %fusion.41 = f32[4096,1024]{1,0:T(8,128)} fusion(bf16[128,4096]{1,0:T(8,128)(2,1)} %all-gather.3.cloned.1.call-done, pred[128]{0:T(512)(128)(4,1)S(1)} %iota_compare_fusion.1, f32[128,1024]{1,0:T(8,128)S(1)} %get-tuple-element.294, f32[128]{0:T(128)S(1)} %fusion.81, f32[1024]{0:T(1024)} %param.29), kind=kOutput, calls=%fused_computation.81 | convolution fusion | flops 1074659328 | bytes 18354816 | tf_op jit(solution)/shard_map/dot_general | solution.py:169
  77.7 46.2 %all-gather.5.cloned.1.call-done = bf16[4096,1024]{1,0:T(8,128)(2,1)} async-done(((bf16[256,1024]{1,0:T(8,128)(2,1)}), bf16[4096,1024]{1,0:T(8,128)(2,1)}) %all-gather.5.cloned.1.call-update) | async-done | bytes 8388624 | tf_op jit(solution)/shard_map/all_gather | solution.py:151
  123.9 5.8 %multiply_reduce_fusion.3 = (f32[1024]{0:T(1024)}, f32[128]{0:T(128)S(1)}, f32[128,1024]{1,0:T(8,128)S(1)}) fusion(f32[128,1024]{1,0:T(8,128)S(1)} %get-tuple-element.294, f32[128]{0:T(128)S(1)} %fusion.81, f32[1024]{0:T(1024)S(1)} %copy-done.14, bf16[4096,1024]{1,0:T(8,128)(2,1)} %all-gather.5.cloned.1.call-done, ...), kind=kOutput, calls=%fused_computation.49 | convolution fusion | flops 1075051392 | bytes 10495104 | tf_op jit(solution)/shard_map/dot_general | solution.py:149
  129.7 2.5 multiply_reduce_fusion.4
  135.0 4.0 %fusion.7 = (f32[16,128]{1,0:T(8,128)S(1)}, f32[16,128]{1,0:T(8,128)S(1)}, f32[16,128]{1,0:T(8,128)S(1)}, f32[128,128]{1,0:T(8,128)}) fusion(f32[16,128]{1,0:T(8,128)} %copy-done.22, f32[16,128]{1,0:T(8,128)} %copy-done.21, f32[128,128]{1,0:T(8,128)} %copy-done.37, pred[128,128]{1,0:T(8,128)(4,1)} %copy-done.13, f32[16,64,128]{2,1,0:T(8,128)S(1)} %bitcast.89, ...), kind=kOutput, calls=%fused_computation.24 | convolution fusion | flops 204711936 | bytes 1236992 | tf_op jit(solution)/shard_map/transpose(jvp())/while/body/eval_jaxpr/hts,shp->thp/dot_general | solution.py:44
  141.1 2.0 fusion.98
  143.1 3.3 fusion
  146.4 1.3 copy.108
  147.7 1.7 convolution_bitcast_fusion.5
  149.4 1.7 convolution_bitcast_fusion.4
  152.2 1.9 multiply_reduce_fusion.19
  154.2 1.3 multiply_reduce_fusion.8
  156.1 69.4 %reduce-scatter.2.cloned.1.call-done = f32[256,1024]{1,0:T(8,128)} async-done(((f32[4096,1024]{1,0:T(8,128)}), f32[256,1024]{1,0:T(8,128)}) %reduce-scatter.2.cloned.1.call-update) | async-done | bytes 1048592 | tf_op jit(solution)/shard_map/reduce_scatter | solution.py:168
  226.2 106.8 %all-reduce.35 = (f32[4,1024]{1,0:T(4,128)}, f32[4,128]{1,0:T(4,128)}, f32[4,128]{1,0:T(4,128)}, f32[16]{0:T(128)}, f32[16]{0:T(128)}, /*index=5*/f32[16]{0:T(128)}, f32[1024]{0:T(1024)}) all-reduce(f32[4,1024]{1,0:T(4,128)S(1)} %pad_add_fusion, ...), channel_id=1, replica_groups=mesh['rep'=2,'dp'=16,'tensor'=8] {'rep','dp'}, use_global_device_ids=true, to_apply=%region_14.15 | all-reduce | flops 6192 | bytes 49536 | tf_op jit(solution)/shard_map/psum | solution.py:155
  333.0 1.3 fusion.66
  334.3 1.3 fusion.62
  336.5 1.6 fusion.14
  338.1 2.3 copy.119
  (125 shorter events, 24.1 us)
Async XLA Ops:
  7.2 24.6 %copy-start.2 = (bf16[128,1024]{1,0:T(8,128)(2,1)S(1)}, bf16[128,1024]{1,0:T(8,128)(2,1)}, u32[]{:S(2)}) copy-start(bf16[128,1024]{1,0:T(8,128)(2,1)} %param.16) | copy-start | bytes 786436
  7.2 59.8 %all-gather.3.cloned.1.call-start = ((), (), s32[]{:S(2)}) async-start(), calls=%async_computation.1 | async-start | bytes 1179648 | tf_op jit(solution)/shard_map/all_gather | solution.py:125
  7.9 115.9 %all-gather.5.cloned.1.call-start = ((), (), s32[]{:S(2)}) async-start(), calls=%async_computation.2 | async-start | bytes 8912896 | tf_op jit(solution)/shard_map/all_gather | solution.py:151
  8.7 216.8 %reduce-scatter.2.cloned.1.call-start = ((), (), s32[]{:S(2)}) async-start(), calls=%async_computation.3 | async-start | bytes 17825792 | tf_op jit(solution)/shard_map/reduce_scatter | solution.py:168
  13.9 17.6 %copy-start.21 = (f32[16,128]{1,0:T(8,128)}, f32[16,128]{1,0:T(8,128)S(1)}, u32[]{:S(2)}) copy-start(f32[16,128]{1,0:T(8,128)S(1)} %copy.101) | copy-start | bytes 24580
  17.9 7.4 %copy-start.16 = (pred[128]{0:T(512)(128)(4,1)}, pred[128]{0:T(512)(128)(4,1)S(1)}, u32[]{:S(2)}) copy-start(pred[128]{0:T(512)(128)(4,1)S(1)} %get-tuple-element.331) | copy-start | bytes 388
  17.9 7.4 %copy-start.17 = (pred[128]{0:T(512)(128)(4,1)}, pred[128]{0:T(512)(128)(4,1)S(1)}, u32[]{:S(2)}) copy-start(pred[128]{0:T(512)(128)(4,1)S(1)} %get-tuple-element.332) | copy-start | bytes 388
  18.0 13.5 %copy-start.18 = (pred[128]{0:T(512)(128)(4,1)}, pred[128]{0:T(512)(128)(4,1)S(1)}, u32[]{:S(2)}) copy-start(pred[128]{0:T(512)(128)(4,1)S(1)} %get-tuple-element.334) | copy-start | bytes 388
  18.0 13.5 %copy-start.19 = (f32[128]{0:T(128)}, f32[128]{0:T(128)S(1)}, u32[]{:S(2)}) copy-start(f32[128]{0:T(128)S(1)} %get-tuple-element.330) | copy-start | bytes 1540
  18.0 13.5 %copy-start.25 = (f32[128]{0:T(128)}, f32[128]{0:T(128)S(1)}, u32[]{:S(2)}) copy-start(f32[128]{0:T(128)S(1)} %get-tuple-element.333) | copy-start | bytes 1540
  20.6 8.6 %copy-start.23 = (f32[128]{0:T(128)}, f32[128]{0:T(128)S(1)}, u32[]{:S(2)}) copy-start(f32[128]{0:T(128)S(1)} %get-tuple-element.320) | copy-start | bytes 1540
  20.6 8.6 %copy-start.24 = (f32[128]{0:T(128)}, f32[128]{0:T(128)S(1)}, u32[]{:S(2)}) copy-start(f32[128]{0:T(128)S(1)} %get-tuple-element.342) | copy-start | bytes 1540
  20.6 8.6 %copy-start.29 = (f32[128]{0:T(128)}, f32[128]{0:T(128)S(1)}, u32[]{:S(2)}) copy-start(f32[128]{0:T(128)S(1)} %get-tuple-element.323) | copy-start | bytes 1540
  20.6 8.6 %copy-start.30 = (f32[128]{0:T(128)}, f32[128]{0:T(128)S(1)}, u32[]{:S(2)}) copy-start(f32[128]{0:T(128)S(1)} %get-tuple-element.339) | copy-start | bytes 1540
  20.6 8.6 %copy-start.31 = (f32[128]{0:T(128)}, f32[128]{0:T(128)S(1)}, u32[]{:S(2)}) copy-start(f32[128]{0:T(128)S(1)} %get-tuple-element.340) | copy-start | bytes 1540
  20.6 8.6 %copy-start.32 = (f32[128]{0:T(128)}, f32[128]{0:T(128)S(1)}, u32[]{:S(2)}) copy-start(f32[128]{0:T(128)S(1)} %get-tuple-element.341) | copy-start | bytes 1540
  21.4 7.8 %copy-start.20 = (f32[16]{0:T(128)}, f32[16]{0:T(128)S(1)}, u32[]{:S(2)}) copy-start(f32[16]{0:T(128)S(1)} %get-tuple-element.316) | copy-start | bytes 196
  22.2 9.3 %copy-start.13 = (pred[128,128]{1,0:T(8,128)(4,1)}, pred[128,128]{1,0:T(8,128)(4,1)S(1)}, u32[]{:S(2)}) copy-start(pred[128,128]{1,0:T(8,128)(4,1)S(1)} %fusion.73) | copy-start | bytes 49156
  32.9 91.0 %copy-start.26 = (f32[128]{0:T(128)}, f32[128]{0:T(128)S(1)}, u32[]{:S(2)}) copy-start(f32[128]{0:T(128)S(1)} %fusion.81) | copy-start | bytes 1540
  76.4 47.5 %copy-start.14 = (f32[1024]{0:T(1024)S(1)}, f32[1024]{0:T(1024)}, u32[]{:S(2)}) copy-start(f32[1024]{0:T(1024)} %param.29) | copy-start | bytes 12292
  76.4 261.8 %all-reduce.38.cloned.1.call-start = ((), (), s32[]{:S(2)}) async-start(), calls=%async_computation.4 | async-start | bytes 2097152 | tf_op jit(solution)/shard_map/psum | solution.py:176
  129.7 24.5 %copy-start.1 = (bf16[128,1024]{1,0:T(8,128)(2,1)S(1)}, bf16[128,1024]{1,0:T(8,128)(2,1)}, u32[]{:S(2)}) copy-start(bf16[128,1024]{1,0:T(8,128)(2,1)} %param.17) | copy-start | bytes 786436
  143.1 12.3 %copy-start.36 = (f32[16]{0:T(128)S(1)}, f32[16]{0:T(128)}, u32[]{:S(2)}) copy-start(f32[16]{0:T(128)} %get-tuple-element.314) | copy-start | bytes 196
  143.1 83.1 %copy-start.33 = (f32[16]{0:T(128)S(1)}, f32[16]{0:T(128)}, u32[]{:S(2)}) copy-start(f32[16]{0:T(128)} %get-tuple-element.288) | copy-start | bytes 196
  (18 other events, 64.2 us)
Sparse Core Ops, SparseCore 0:
  10.7 56.2 all-gather.2
  68.8 55.0 all-gather.4
  126.4 99.0 reduce-scatter.1
  228.0 50.4 all-reduce.37
where the time goes:
time: 348 us; the launch traced here: 347 us
  waiting for transfers between devices  151 us (43%)
  blocking collectives  107 us (31%)
  matrix products  36.3 us (10%)
  other arithmetic  26.5 us (8%)
  between operations  15 us (4%)
  local copies, waits for them, and re-layouts  10.9 us (3%)
    psum x1, blocking collectives, body(): lax.psum((param_grads[0], param_grads[1], param_grads[2], param_grads[3],...  107 us
    reduce_scatter x1, waiting for transfers between devices, body(): lax.psum_scatter(lax.dot_general(dy_block, normed_b, (((0,), (0,)), ((),...  69.4 us
    all_gather x1, waiting for transfers between devices, body(): lax.all_gather(w_out, 'dp', axis=0, tiled=True)  46.2 us
    all_gather x1, waiting for transfers between devices, body(): gathered = lax.all_gather(d_out, 'tensor', axis=0, tiled=True)  34.1 us
    dot_general x3, matrix products, span_step(): intra_out = jnp.einsum('hts,shp->thp', weights, x_blk, precision=highest)  9.46 us
    dot_general x1, matrix products, body(): lax.dot_general(dy_block, normed_b, (((0,), (0,)), ((), ())), preferred_e...  9.39 us
  transfers between devices with their start and end apart: 4, of which 3 were waited for; matrix products, arithmetic and copies ran while one was open for 20% of the time, Pallas kernels for 0%

commit v1 on v0

v1 whole, which is shorter than its diff:
```python
import jax
import jax.numpy as jnp
from jax import lax
from jax.experimental import pallas as pl
from jax.experimental.pallas import tpu as pltpu
from jax.sharding import PartitionSpec as P

HDIM = 64
LANES = 128
KCONV = 4
EPS = 1e-05
F32 = jnp.float32
BF16 = jnp.bfloat16
VMEM_LIMIT = 48 * 1024 * 1024


def split2(value):
    high = value.astype(BF16)
    low = (value - high.astype(F32)).astype(BF16)
    return high, low


def split3(value):
    high = value.astype(BF16)
    rest = value - high.astype(F32)
    middle = rest.astype(BF16)
    low = (rest - middle.astype(F32)).astype(BF16)
    return high, middle, low


def dot_nn(left, right):
    left_h, left_l = split2(left)
    right_h, right_l = split2(right)
    return jnp.dot(
        jnp.concatenate([left_h, left_h, left_l], axis=1),
        jnp.concatenate([right_h, right_l, right_h], axis=0),
        preferred_element_type=F32,
    )


def dot_nt(left, right):
    left_h, left_l = split2(left)
    right_h, right_l = split2(right)
    return lax.dot_general(
        jnp.concatenate([left_h, left_h, left_l], axis=1),
        jnp.concatenate([right_h, right_l, right_h], axis=1),
        (((1,), (1,)), ((), ())),
        preferred_element_type=F32,
    )


def dot_exact(left_pieces, right):
    total = jnp.dot(left_pieces[0], right, preferred_element_type=F32)
    for piece in left_pieces[1:]:
        total = total + jnp.dot(piece, right, preferred_element_type=F32)
    return total


def sigmoid(value):
    return 1.0 / (1.0 + jnp.exp(-value))


def iota(axis, shape=(LANES, LANES)):
    return lax.broadcasted_iota(jnp.int32, shape, axis)


def shift_masks(seg_row):
    seg_cols = jnp.broadcast_to(seg_row.astype(F32), (LANES, LANES))
    seg_rows = seg_cols.T
    rows = iota(0)
    masks = []
    for offset in range(1, KCONV):
        prior = pltpu.roll(seg_rows, offset, 0)
        masks.append(jnp.where((rows >= offset) & (prior == seg_rows), 1.0, 0.0).astype(F32))
    return seg_rows, seg_cols, masks


def conv_silu(values, taps, masks):
    summed = taps[KCONV - 1 : KCONV] * values
    for offset in range(1, KCONV):
        shifted = pltpu.roll(values, offset, 0) * masks[offset - 1]
        summed = summed + taps[KCONV - 1 - offset : KCONV - offset] * shifted
    sig = sigmoid(summed)
    return summed * sig, sig * (1.0 + summed * (1.0 - sig))


def conv_back(cotangent, values, taps, masks):
    result = taps[KCONV - 1 : KCONV] * cotangent
    tap_grads = [None] * KCONV
    tap_grads[KCONV - 1] = jnp.sum(cotangent * values, axis=0, keepdims=True)
    for offset in range(1, KCONV):
        moved = pltpu.roll(cotangent * masks[offset - 1], LANES - offset, 0)
        result = result + taps[KCONV - 1 - offset : KCONV - offset] * moved
        tap_grads[KCONV - 1 - offset] = jnp.sum(moved * values, axis=0, keepdims=True)
    return result, tap_grads


def head_expander(heads):
    shape = (heads, heads * HDIM)
    return jnp.where(iota(1, shape) // HDIM == iota(0, shape), 1.0, 0.0).astype(BF16)


def two_halves(value):
    left = iota(1) < HDIM
    zero = jnp.zeros_like(value)
    return jnp.concatenate([jnp.where(left, value, zero), jnp.where(left, zero, value)], axis=0)


def forward_kernel(
    count_ref, z_ref, x_ref, b_ref, c_ref, dt_ref, seg_ref, cx_ref, cb_ref, cc_ref, al_ref, bias_ref, skip_ref, gain_ref,
    norm_ref, xc_ref, dsx_ref, ssm_ref, gate_ref, dgate_ref, bcc_ref, small_ref, cumt_ref, rms_ref,
):
    heads = dt_ref.shape[1]
    tiles = x_ref.shape[1] // LANES
    seg_rows, seg_cols, masks = shift_masks(seg_ref[...])
    rows, cols = iota(0), iota(1)
    causal = (rows >= cols) & (seg_rows == seg_cols)

    b_conv, b_slope = conv_silu(b_ref[...].astype(F32), cb_ref[...], masks)
    c_conv, c_slope = conv_silu(c_ref[...].astype(F32), cc_ref[...], masks)
    bcc_ref[0] = b_conv
    bcc_ref[1] = c_conv
    bcc_ref[2] = b_slope
    bcc_ref[3] = c_slope
    scores = dot_nt(c_conv, b_conv)
    bcc_ref[4] = scores.T

    raw = dt_ref[...].astype(F32) + bias_ref[...]
    step = jnp.maximum(raw, 0.0) + jnp.log1p(jnp.exp(-jnp.abs(raw)))
    decay = -jnp.exp(al_ref[...]) * step
    lower = jnp.where(rows >= cols, 1.0, 0.0).astype(BF16)
    cumul = sum(jnp.dot(lower, piece, preferred_element_type=F32) for piece in split3(decay))
    cumul_t = cumul.T
    cumt_ref[...] = cumul_t
    small_ref[0] = step
    small_ref[1] = decay
    small_ref[2] = cumul
    small_ref[3] = sigmoid(raw)

    expander = head_expander(heads)
    step_wide = dot_exact(split3(step), expander)
    skip_wide = dot_exact(split3(jnp.broadcast_to(skip_ref[...], (8, heads))), expander)

    squares = jnp.zeros((LANES, LANES), F32)
    for tile in range(tiles):
        span = slice(tile * LANES, (tile + 1) * LANES)
        x_conv, x_slope = conv_silu(x_ref[:, span].astype(F32), cx_ref[:, span], masks)
        xc_ref[:, span] = x_conv
        dsx_ref[:, span] = x_slope
        pieces = []
        for head in (2 * tile, 2 * tile + 1):
            gap = cumul[:, head : head + 1] - cumul_t[head : head + 1, :]
            pieces.append(scores * jnp.exp(jnp.where(causal, gap, -1e30)))
        weights = jnp.concatenate(pieces, axis=1)
        ssm = dot_nn(weights, two_halves(step_wide[:, span] * x_conv))
        ssm = ssm + skip_wide[0:1, span] * x_conv
        ssm_ref[:, span] = ssm
        z_tile = z_ref[:, span].astype(F32)
        sig = sigmoid(z_tile)
        gate = z_tile * sig
        gate_ref[:, span] = gate
        dgate_ref[:, span] = sig * (1.0 + z_tile * (1.0 - sig))
        gated = ssm * gate
        squares = squares + gated * gated
    mean = jnp.sum(squares, axis=1, keepdims=True) / (tiles * LANES)
    inv = lax.rsqrt(jnp.broadcast_to(mean, (LANES, LANES)) + EPS)
    rms_ref[...] = inv
    alive = jnp.where(rows < count_ref[0], 1.0, 0.0).astype(F32)
    for tile in range(tiles):
        span = slice(tile * LANES, (tile + 1) * LANES)
        normed = ssm_ref[:, span] * gate_ref[:, span] * inv * gain_ref[:, span]
        norm_ref[:, span] = (normed * alive).astype(BF16)


def backward_kernel(
    count_ref, up_ref, x_ref, b_ref, c_ref, seg_ref, cx_ref, cb_ref, cc_ref, al_ref, skip_ref, gain_ref,
    xc_ref, dsx_ref, ssm_ref, gate_ref, dgate_ref, bcc_ref, small_ref, cumt_ref, rms_ref,
    gz_ref, gx_ref, gb_ref, gc_ref, gdt_ref, par_ref,
):
    heads = small_ref.shape[2]
    tiles = x_ref.shape[1] // LANES
    seg_rows, seg_cols, masks = shift_masks(seg_ref[...])
    rows, cols = iota(0), iota(1)
    causal_t = (cols >= rows) & (seg_rows == seg_cols)
    alive = jnp.where(rows < count_ref[0], 1.0, 0.0).astype(F32)
    inv = rms_ref[...]
    scores_t = bcc_ref[4]
    step, decay, cumul, slope = small_ref[0], small_ref[1], small_ref[2], small_ref[3]
    cumul_t = cumt_ref[...]
    expander = head_expander(heads)
    step_wide = dot_exact(split3(step), expander)
    skip_wide = dot_exact(split3(jnp.broadcast_to(skip_ref[...], (8, heads))), expander)

    dots = jnp.zeros((LANES, LANES), F32)
    for tile in range(tiles):
        span = slice(tile * LANES, (tile + 1) * LANES)
        upstream = up_ref[:, span] * alive
        gated = ssm_ref[:, span] * gate_ref[:, span]
        product = upstream * gated
        dots = dots + product * gain_ref[:, span]
        par_ref[32 + tile : 33 + tile, :] = jnp.sum(product * inv, axis=0, keepdims=True)
    mean = jnp.sum(dots, axis=1, keepdims=True) / (tiles * LANES)
    pull = jnp.broadcast_to(mean, (LANES, LANES)) * inv * inv * inv

    before = jnp.where(rows > cols, 1.0, 0.0).astype(BF16)
    before = jnp.concatenate([before, before], axis=1)
    after = jnp.where(cols >= rows, 1.0, 0.0).astype(F32)
    score_grad = jnp.zeros((LANES, LANES), F32)
    sums = jnp.zeros((LANES, LANES), F32)
    for tile in range(tiles):
        span = slice(tile * LANES, (tile + 1) * LANES)
        x_conv = xc_ref[:, span]
        ssm = ssm_ref[:, span]
        gate = gate_ref[:, span]
        d_gated = inv * (up_ref[:, span] * alive) * gain_ref[:, span] - ssm * gate * pull
        gz_ref[:, span] = (d_gated * ssm * dgate_ref[:, span]).astype(BF16)
        d_ssm = d_gated * gate
        x_step = step_wide[:, span] * x_conv
        d_weights = dot_nt(two_halves(x_step), d_ssm)
        pieces = []
        for which in range(2):
            head = 2 * tile + which
            gap = cumul_t[head : head + 1, :] - cumul[:, head : head + 1]
            fade = jnp.exp(jnp.where(causal_t, gap, -1e30))
            d_weight = d_weights[which * LANES : (which + 1) * LANES, :] * fade
            score_grad = score_grad + d_weight
            pieces.append((scores_t * fade, d_weight * scores_t))
        d_xstep = dot_nn(
            jnp.concatenate([pieces[0][0], pieces[1][0]], axis=1), two_halves(d_ssm)
        )
        gaps_h, gaps_l = split2(jnp.concatenate([pieces[0][1], pieces[1][1]], axis=1))
        gaps = jnp.dot(
            before, jnp.concatenate([gaps_h, gaps_l], axis=0), preferred_element_type=F32
        )
        terms = (
            gaps[:, :LANES] * after,
            gaps[:, LANES:] * after,
            d_xstep * x_conv,
            d_ssm * x_conv,
        )
        pickers = (
            jnp.where(cols == 2 * tile, 1.0, 0.0),
            jnp.where(cols == 2 * tile + 1, 1.0, 0.0),
            jnp.where(cols == heads + 2 * tile + rows // HDIM, 1.0, 0.0),
            jnp.where(cols == 2 * heads + 2 * tile + rows // HDIM, 1.0, 0.0),
        )
        left, right = [], []
        for term, picker in zip(terms, pickers):
            term_h, term_l = split2(term)
            left += [term_h, term_l]
            right += [picker.astype(BF16)] * 2
        sums = sums + jnp.dot(
            jnp.concatenate(left, axis=1),
            jnp.concatenate(right, axis=0),
            preferred_element_type=F32,
        )
        d_conv = skip_wide[0:1, span] * d_ssm + step_wide[:, span] * d_xstep
        x_grad, tap_grads = conv_back(
            d_conv * dsx_ref[:, span], x_ref[:, span].astype(F32), cx_ref[:, span], masks
        )
        gx_ref[:, span] = x_grad.astype(BF16)
        for tap in range(KCONV):
            par_ref[tap * tiles + tile : tap * tiles + tile + 1, :] = tap_grads[tap]

    d_decay = sums[:, 0:heads]
    d_step = sums[:, heads : 2 * heads] - jnp.exp(al_ref[...]) * d_decay
    d_raw = d_step * slope
    gdt_ref[...] = d_raw.astype(BF16)
    par_ref[48:49, 0:heads] = jnp.sum(d_decay * decay, axis=0, keepdims=True)
    par_ref[49:50, 0:heads] = jnp.sum(d_raw, axis=0, keepdims=True)
    par_ref[50:51, 0:heads] = jnp.sum(sums[:, 2 * heads : 3 * heads], axis=0, keepdims=True)

    b_conv, c_conv = bcc_ref[0], bcc_ref[1]
    b_grad, tap_grads = conv_back(
        dot_nn(score_grad, c_conv) * bcc_ref[2], b_ref[...].astype(F32), cb_ref[...], masks
    )
    gb_ref[...] = b_grad.astype(BF16)
    for tap in range(KCONV):
        par_ref[40 + tap : 41 + tap, :] = tap_grads[tap]
    c_grad, tap_grads = conv_back(
        dot_nn(score_grad.T, b_conv) * bcc_ref[3], c_ref[...].astype(F32), cc_ref[...], masks
    )
    gc_ref[...] = c_grad.astype(BF16)
    for tap in range(KCONV):
        par_ref[44 + tap : 45 + tap, :] = tap_grads[tap]


def unpack_kernel(par_ref, cx_ref, cb_ref, cc_ref, al_ref, bias_ref, skip_ref, gain_ref):
    heads = al_ref.shape[1]
    tiles = cx_ref.shape[1] // LANES
    total = par_ref[...]
    for tap in range(KCONV):
        for tile in range(tiles):
            cx_ref[tap : tap + 1, tile * LANES : (tile + 1) * LANES] = total[
                tap * tiles + tile : tap * tiles + tile + 1
            ]
    for tile in range(tiles):
        gain_ref[:, tile * LANES : (tile + 1) * LANES] = total[32 + tile : 33 + tile]
    cb_ref[...] = total[40:44]
    cc_ref[...] = total[44:48]
    al_ref[...] = total[48:49, 0:heads]
    bias_ref[...] = total[49:50, 0:heads]
    skip_ref[...] = total[50:51, 0:heads]


def call(kernel, operands, outs, flops, smem_first=True):
    vmem = pl.BlockSpec(memory_space=pltpu.VMEM)
    specs = [vmem] * len(operands)
    if smem_first:
        specs[0] = pl.BlockSpec(memory_space=pltpu.SMEM)
    size = sum(a.size * a.dtype.itemsize for a in operands) + sum(
        a.size * a.dtype.itemsize for a in outs
    )
    return pl.pallas_call(
        kernel,
        out_shape=outs,
        in_specs=specs,
        out_specs=[vmem] * len(outs),
        compiler_params=pltpu.CompilerParams(vmem_limit_bytes=VMEM_LIMIT),
        cost_estimate=pl.CostEstimate(flops=flops, bytes_accessed=size, transcendentals=0),
    )(*operands)


def shape(dims, dtype=F32):
    return jax.ShapeDtypeStruct(dims, dtype)


def swap(value, axis, bit, size):
    return lax.ppermute(value, axis, [(i, i ^ bit) for i in range(size)])


def gather_tensor(block, axis):
    me = lax.axis_index("tensor")
    held = jnp.expand_dims(block, axis)
    for bit in (1, 2, 4):
        other = swap(held, "tensor", bit, 8)
        first = (me & bit) == 0
        held = jnp.concatenate(
            [jnp.where(first, held, other), jnp.where(first, other, held)], axis=axis
        )
    return held


def body(
    z_act, x_act, b_act, c_act, dt_act, segment, counts,
    conv_x, conv_b, conv_c, a_log, dt_bias, d_skip, norm_gain, w_out, d_out,
):
    length, width = z_act.shape
    heads = dt_act.shape[1]
    features = d_out.shape[1]
    dp = lax.axis_size("dp")
    seg_row = segment.reshape(1, length)
    a_log, dt_bias, d_skip = (v.reshape(1, heads) for v in (a_log, dt_bias, d_skip))
    gain = norm_gain.reshape(1, width)

    w_all = lax.all_gather(w_out, "dp", axis=0, tiled=True)

    own = d_out.shape[0]
    rows = gather_tensor(d_out, 0).reshape(length, features)
    pieces = d_out.reshape(own, dp, features // dp).transpose(1, 0, 2)
    pieces = lax.all_to_all(pieces, "dp", 0, 0, tiled=False)
    columns = gather_tensor(pieces, 1).reshape(dp * length, features // dp)

    wide = shape((length, width))
    normed, *saved = call(
        forward_kernel,
        (counts, z_act, x_act, b_act, c_act, dt_act, seg_row, conv_x, conv_b, conv_c, a_log, dt_bias, d_skip, gain),
        [
            shape((length, width), BF16), wide, wide, wide, wide, wide,
            shape((5, LANES, LANES)), shape((4, length, heads)), shape((heads, length)), shape((LANES, LANES)),
        ],
        300_000_000,
    )
    normed_all = lax.all_gather(normed, "dp", axis=0, tiled=True)

    upstream = jnp.dot(rows, w_all, preferred_element_type=F32)
    *act_grads, packed = call(
        backward_kernel,
        (counts, upstream, x_act, b_act, c_act, seg_row, conv_x, conv_b, conv_c, a_log, d_skip, gain, *saved),
        [
            shape((length, width), BF16), shape((length, width), BF16), shape((length, LANES), BF16),
            shape((length, LANES), BF16), shape((length, heads), BF16), shape((56, LANES)),
        ],
        600_000_000,
    )
    packed = packed + swap(packed, "dp", 1, dp)
    packed = packed + swap(packed, "rep", 1, 2)
    for bit in (2, 4, 8):
        packed = packed + swap(packed, "dp", bit, dp)
    sums = call(
        unpack_kernel,
        (packed,),
        [
            shape(conv_x.shape), shape(conv_b.shape), shape(conv_c.shape),
            shape((1, heads)), shape((1, heads)), shape((1, heads)), shape((1, width)),
        ],
        1000,
        smem_first=False,
    )

    share = lax.dot_general(
        columns, normed_all, (((0,), (0,)), ((), ())), preferred_element_type=F32
    ).astype(BF16)
    weight_grad = share.astype(F32) + swap(share, "rep", 1, 2).astype(F32)
    return (
        *act_grads,
        sums[0], sums[1], sums[2],
        sums[3].reshape(heads), sums[4].reshape(heads), sums[5].reshape(heads), sums[6].reshape(width),
        weight_grad,
    )


def solution(mesh):
    tokens = P(("rep", "dp"), "tensor")
    shards = P(("rep", "dp"))
    taps = P(None, "tensor")
    per_head = P("tensor")
    weight = P("dp", "tensor")
    in_specs = (
        *([tokens] * 5), shards, shards, *([taps] * 3), *([per_head] * 4),
        weight, P(("rep", "dp", "tensor"), None),
    )
    out_specs = (*([tokens] * 5), *([taps] * 3), *([per_head] * 4), weight)
    return jax.shard_map(body, mesh=mesh, in_specs=in_specs, out_specs=out_specs, check_vma=False)
```

time: 348 us -> 165 us (0.47)
  blocking collectives: 107 us -> 0 us
  waiting for transfers between devices: 151 us -> 81.5 us
  matrix products: 36.3 us -> 9.76 us
  starting transfers between devices: 0.34 us -> 24.7 us
  other arithmetic: 26.5 us -> 11.5 us
  Pallas kernels: 0 us -> 8.06 us
    psum x1 -> x0, blocking collectives: 107 us -> none  [body(): lax.psum((param_grads[0], param_grads[1], param_grads[2], param_grads[3],...]
    reduce_scatter x1 -> x0, waiting for transfers between devices: 69.4 us -> none  [body(): lax.psum_scatter(lax.dot_general(dy_block, normed_b, (((0,), (0,)), ((),...]
    all_gather x2, waiting for transfers between devices: 80.3 us -> 31.3 us  [the longest x1 31.3 us: body(): w_all = lax.all_gather(w_out, 'dp', axis=0, tiled=True)]
    ppermute x0 -> x12, waiting for transfers between devices: none -> 40.4 us  [swap(): return lax.ppermute(value, axis, [(i, i ^ bit) for i in range(size)])]
    dot_general x12 -> x2, matrix products: 36.3 us -> 9.76 us  [the longest x1 5.03 us: body(): upstream = jnp.dot(rows, w_all, preferred_element_type=F32)]
    ppermute x0 -> x12, starting transfers between devices: none -> 16 us  [swap(): return lax.ppermute(value, axis, [(i, i ^ bit) for i in range(size)])]
    unnamed x77 -> x63, local copies, waits for them, and re-layouts: 2.97 us -> 13.4 us
    reduce_sum x7 -> x0, other arithmetic: 10.1 us -> none  [the longest x2 3.16 us: mixer_forward(): d_skip[None, :, None] * x_conv.reshape(length, head_count, HDIM)]
  transfers between devices with their start and end apart: 4 -> 15, of which waited for: 3 -> 11; matrix products, arithmetic and copies ran while one was open for 20% -> 14% of each run, Pallas kernels for 0% -> 3%
where the time goes in v1:
time: 165 us
  waiting for transfers between devices  81.5 us (49%)
  starting transfers between devices  24.7 us (15%)
  between operations  15 us (9%)
  local copies, waits for them, and re-layouts  14.1 us (9%)
  other arithmetic  11.5 us (7%)
  matrix products  9.76 us (6%)
  Pallas kernels  8.06 us (5%)
    ppermute x12, waiting for transfers between devices, swap(): return lax.ppermute(value, axis, [(i, i ^ bit) for i in range(size)])  40.4 us
    all_gather x1, waiting for transfers between devices, body(): w_all = lax.all_gather(w_out, 'dp', axis=0, tiled=True)  31.3 us
    ppermute x12, starting transfers between devices, swap(): return lax.ppermute(value, axis, [(i, i ^ bit) for i in range(size)])  16 us
    unnamed x63, local copies, waits for them, and re-layouts  13.4 us
    all_to_all x1, waiting for transfers between devices, body(): pieces = lax.all_to_all(pieces, 'dp', 0, 0, tiled=False)  9.12 us
    all_to_all x1, starting transfers between devices, body(): pieces = lax.all_to_all(pieces, 'dp', 0, 0, tiled=False)  8.62 us
    pallas_call x3, Pallas kernels, call(): pl.pallas_call(kernel, out_shape=outs, in_specs=specs, out_specs=[vmem] *...  8.06 us
    select_n x6, other arithmetic, gather_tensor(): jnp.where(first, held, other)  5.34 us
  transfers between devices with their start and end apart: 15, of which 11 were waited for; matrix products, arithmetic and copies ran while one was open for 14% of the time, Pallas kernels for 3%

profile of v1, /device:TPU:2, one launch (start us, length us, event | category | flops | bytes accessed | tf_op | source)
XLA Modules:
  0.0 164.6 jit_solution(7860638561540268538)
XLA Ops:
  17.5 2.5 %shard_map.255 = (bf16[128,1024]{1,0:T(8,128)(2,1)}, f32[128,1024]{1,0:T(8,128)S(1)}, f32[128,1024]{1,0:T(8,128)S(1)}, f32[128,1024]{1,0:T(8,128)S(1)}, f32[128,...) custom-call(s32[1]{0:T(128)S(6)} %copy.40.count_ref, ...), custom_call_target="tpu_custom_call" | custom-call | flops 300000000 | bytes 3936964 | tf_op jit(solution)/shard_map/pallas_call | solution.py:314
  21.4 3.3 %collective-permute-start = (bf16[1,16,4096]{2,1,0:T(8,128)(2,1)}, bf16[1,16,4096]{2,1,0:T(8,128)(2,1)}, u32[]{:S(2)}, u32[]{:S(2)}) collective-permute-start(bf16[1,16,4096]{2,1,0:T(8,128)(2,1)} %bitcast.36), channel_id=1, source_target_pairs={{0,1},{1,0},{2,3},{3,2},{4,5},{5,4},{6,7},{7,6},{8,9},{9,8},{10,11... | collective-permute-start | bytes 393224 | tf_op jit(solution)/shard_map/ppermute | solution.py:329
  26.4 8.6 %all-to-all-start = ((bf16[16,16,256]{2,1,0:T(8,128)(2,1)}), bf16[16,16,256]{2,1,0:T(8,128)(2,1)}, u32[]{:S(2)}, u32[]{:S(2)}) async-start(bf16[16,16,256]{2,1,0:T(8,128)(2,1)} %copy.37), calls=%async_computation | async-start | bytes 262144 | tf_op jit(solution)/shard_map/all_to_all | solution.py:361
  36.0 9.1 %all-to-all-done = bf16[16,16,256]{2,1,0:T(8,128)(2,1)} async-done(((bf16[16,16,256]{2,1,0:T(8,128)(2,1)}), bf16[16,16,256]{2,1,0:T(8,128)(2,1)}, u32[]{:S(2)}, u32[]{:S(2)}) %all-to-all-start) | async-done | bytes 131104 | tf_op jit(solution)/shard_map/all_to_all | solution.py:361
  45.8 7.1 %collective-permute-done.8 = bf16[16,1,16,256]{3,2,1,0:T(8,128)(2,1)S(1)} collective-permute-done((bf16[16,1,16,256]{3,2,1,0:T(8,128)(2,1)}, bf16[16,1,16,256]{3,2,1,0:T(8,128)(2,1)S(1)}, u32[]{:S(2)}, u32[]{:S(2)}) %collective-permute-start.8) | collective-permute-done | bytes 131104 | tf_op jit(solution)/shard_map/ppermute | solution.py:329
  57.8 2.4 %collective-permute-start.2 = (bf16[4,16,4096]{2,1,0:T(8,128)(2,1)}, bf16[4,16,4096]{2,1,0:T(8,128)(2,1)}, u32[]{:S(2)}, u32[]{:S(2)}) collective-permute-start(bf16[4,16,4096]{2,1,0:T(8,128)(2,1)} %pad_maximum_fusion.2), channel_id=1, source_target_pairs={{0,4},{1,5},{2,6},{3,7},{4,0},{5,1},{6,2},{7,3},{8,12},{9,13},{10,... | collective-permute-start | bytes 1572872 | tf_op jit(solution)/shard_map/ppermute | solution.py:329
  60.2 3.2 %collective-permute-done.9 = bf16[16,2,16,256]{3,2,1,0:T(8,128)(2,1)} collective-permute-done((bf16[16,2,16,256]{3,2,1,0:T(8,128)(2,1)}, bf16[16,2,16,256]{3,2,1,0:T(8,128)(2,1)}, u32[]{:S(2)}, u32[]{:S(2)}) %collective-permute-start.9) | collective-permute-done | bytes 262176 | tf_op jit(solution)/shard_map/ppermute | solution.py:329
  64.6 3.0 %collective-permute-start.10 = (bf16[16,4,16,256]{3,2,1,0:T(8,128)(2,1)S(1)}, bf16[16,4,16,256]{3,2,1,0:T(8,128)(2,1)S(1)}, u32[]{:S(2)}, u32[]{:S(2)}) collective-permute-start(bf16[16,4,16,256]{3,2,1,0:T(8,128)(2,1)S(1)} %pad_maximum_fusion.3), channel_id=1, source_target_pairs={{0,4},{1,5},{2,6},{3,7},{4,0},{5,1},{6,2},{7,3},{8,12},{9,13},{10,... | collective-permute-start | bytes 1572872 | tf_op jit(solution)/shard_map/ppermute | solution.py:329
  67.6 8.8 %collective-permute-done.2 = bf16[4,16,4096]{2,1,0:T(8,128)(2,1)} collective-permute-done((bf16[4,16,4096]{2,1,0:T(8,128)(2,1)}, bf16[4,16,4096]{2,1,0:T(8,128)(2,1)}, u32[]{:S(2)}, u32[]{:S(2)}) %collective-permute-start.2) | collective-permute-done | bytes 524320 | tf_op jit(solution)/shard_map/ppermute | solution.py:329
  76.4 1.2 broadcast_select_fusion.3
  78.6 7.7 %collective-permute-done.10 = bf16[16,4,16,256]{3,2,1,0:T(8,128)(2,1)S(1)} collective-permute-done((bf16[16,4,16,256]{3,2,1,0:T(8,128)(2,1)S(1)}, bf16[16,4,16,256]{3,2,1,0:T(8,128)(2,1)S(1)}, u32[]{:S(2)}, u32[]{:S(2)}) %collective-permute-start.10) | collective-permute-done | bytes 524320 | tf_op jit(solution)/shard_map/ppermute | solution.py:329
  87.5 4.7 %convolution_convert_fusion = bf16[256,1024]{1,0:T(8,128)(2,1)} fusion(bf16[2048,256]{1,0:T(8,128)(2,1)} %bitcast.35, bf16[2048,1024]{1,0:T(8,128)(2,1)} %all-gather.5.cloned.1.call-done), kind=kOutput, calls=%fused_computation | convolution fusion | flops 1074003968 | bytes 5767168 | tf_op jit(solution)/shard_map/dot_general | solution.py:401
  92.5 31.3 %all-gather.3.cloned.1.call-done = bf16[4096,1024]{1,0:T(8,128)(2,1)} async-done(((bf16[256,1024]{1,0:T(8,128)(2,1)}), bf16[4096,1024]{1,0:T(8,128)(2,1)}) %all-gather.3.cloned.1.call-update) | async-done | bytes 8388624 | tf_op jit(solution)/shard_map/all_gather | solution.py:356
  123.9 5.0 %fusion.up_ref = f32[128,1024]{1,0:T(8,128)S(1)} fusion(bf16[128,4096]{1,0:T(8,128)(2,1)} %bitcast.34, bf16[4096,1024]{1,0:T(8,128)(2,1)} %all-gather.3.cloned.1.call-done), kind=kOutput, calls=%fused_computation.20 | convolution fusion | flops 1073741824 | bytes 9961472 | tf_op jit(solution)/shard_map/dot_general | solution.py:376
  129.0 4.9 %shard_map.256 = (bf16[128,1024]{1,0:T(8,128)(2,1)}, bf16[128,1024]{1,0:T(8,128)(2,1)}, bf16[128,128]{1,0:T(8,128)(2,1)}, bf16[128,128]{1,0:T(8,128)(2,1)}, bf16...) custom-call(s32[1]{0:T(128)S(6)} %copy.40.count_ref, f32[128,1024]{1,0:T(8,128)S(1)} %fusion.up_ref, ...), custom_call_target="tpu_custom_call" | custom-call | flops 600000000 | bytes 4555396 | tf_op jit(solution)/shard_map/pallas_call | solution.py:314
  135.1 1.5 collective-permute-start.4
  136.6 2.4 %collective-permute-done.4 = f32[56,128]{1,0:T(8,128)S(1)} collective-permute-done((f32[56,128]{1,0:T(8,128)S(1)}, f32[56,128]{1,0:T(8,128)S(1)}, u32[]{:S(2)}, u32[]{:S(2)}) %collective-permute-start.4) | collective-permute-done | bytes 28704 | tf_op jit(solution)/shard_map/ppermute | solution.py:329
  139.0 3.9 %collective-permute-done.5 = f32[56,128]{1,0:T(8,128)S(1)} collective-permute-done((f32[56,128]{1,0:T(8,128)S(1)}, f32[56,128]{1,0:T(8,128)S(1)}, u32[]{:S(2)}, u32[]{:S(2)}) %collective-permute-start.5) | collective-permute-done | bytes 28704 | tf_op jit(solution)/shard_map/ppermute | solution.py:329
  142.9 1.5 collective-permute-start.6
  144.3 3.6 %collective-permute-done.6 = f32[56,128]{1,0:T(8,128)S(1)} collective-permute-done((f32[56,128]{1,0:T(8,128)S(1)}, f32[56,128]{1,0:T(8,128)S(1)}, u32[]{:S(2)}, u32[]{:S(2)}) %collective-permute-start.6) | collective-permute-done | bytes 28704 | tf_op jit(solution)/shard_map/ppermute | solution.py:329
  147.9 2.7 %collective-permute-start.7 = (f32[56,128]{1,0:T(8,128)S(1)}, f32[56,128]{1,0:T(8,128)S(1)}, u32[]{:S(2)}, u32[]{:S(2)}) collective-permute-start(f32[56,128]{1,0:T(8,128)S(1)} %add.21), channel_id=1, source_target_pairs={{0,64},{8,72},{16,80},{24,88},{32,96},{40,104},{48,112},{56,120},{... | collective-permute-start | bytes 86024 | tf_op jit(solution)/shard_map/ppermute | solution.py:329
  150.6 2.3 %convert_add_fusion = f32[256,1024]{1,0:T(8,128)} fusion(bf16[256,1024]{1,0:T(8,128)(2,1)} %collective-permute-done.11, bf16[256,1024]{1,0:T(8,128)(2,1)} %convolution_convert_fusion), kind=kLoop, calls=%fused_computation.3 | loop fusion | flops 786432 | bytes 2097152 | tf_op jit(solution)/shard_map/add | solution.py:404
  153.0 2.7 %collective-permute-done.7 = f32[56,128]{1,0:T(8,128)S(1)} collective-permute-done((f32[56,128]{1,0:T(8,128)S(1)}, f32[56,128]{1,0:T(8,128)S(1)}, u32[]{:S(2)}, u32[]{:S(2)}) %collective-permute-start.7) | collective-permute-done | bytes 28704 | tf_op jit(solution)/shard_map/ppermute | solution.py:329
  155.7 1.4 copy.38
  (95 shorter events, 24.8 us)
Async XLA Ops:
  7.2 80.3 %all-gather.5.cloned.1.call-start = ((), (), s32[]{:S(2)}) async-start(), calls=%async_computation.2 | async-start | bytes 4456448 | tf_op jit(solution)/shard_map/all_gather | solution.py:374
  20.7 103.1 %all-gather.3.cloned.1.call-start = ((), (), s32[]{:S(2)}) async-start(), calls=%async_computation.1 | async-start | bytes 8912896 | tf_op jit(solution)/shard_map/all_gather | solution.py:356
  21.4 13.6 %collective-permute-start = (bf16[1,16,4096]{2,1,0:T(8,128)(2,1)}, bf16[1,16,4096]{2,1,0:T(8,128)(2,1)}, u32[]{:S(2)}, u32[]{:S(2)}) collective-permute-start(bf16[1,16,4096]{2,1,0:T(8,128)(2,1)} %bitcast.36), channel_id=1, source_target_pairs={{0,1},{1,0},{2,3},{3,2},{4,5},{5,4},{6,7},{7,6},{8,9},{9,8},{10,11... | collective-permute-start | bytes 393224 | tf_op jit(solution)/shard_map/ppermute | solution.py:329
  26.4 18.8 %all-to-all-start = ((bf16[16,16,256]{2,1,0:T(8,128)(2,1)}), bf16[16,16,256]{2,1,0:T(8,128)(2,1)}, u32[]{:S(2)}, u32[]{:S(2)}) async-start(bf16[16,16,256]{2,1,0:T(8,128)(2,1)} %copy.37), calls=%async_computation | async-start | bytes 262144 | tf_op jit(solution)/shard_map/all_to_all | solution.py:361
  36.0 19.2 %copy-start.28 = (bf16[1,16,4096]{2,1,0:T(8,128)(2,1)}, bf16[1,16,4096]{2,1,0:T(8,128)(2,1)S(1)}, u32[]{:S(2)}) copy-start(bf16[1,16,4096]{2,1,0:T(8,128)(2,1)S(1)} %get-tuple-element.121) | copy-start | bytes 393220
  36.0 19.2 %copy-start.29 = (bf16[1,16,4096]{2,1,0:T(8,128)(2,1)}, bf16[1,16,4096]{2,1,0:T(8,128)(2,1)S(1)}, u32[]{:S(2)}) copy-start(bf16[1,16,4096]{2,1,0:T(8,128)(2,1)S(1)} %get-tuple-element.122) | copy-start | bytes 393220
  45.2 7.8 %collective-permute-start.8 = (bf16[16,1,16,256]{3,2,1,0:T(8,128)(2,1)}, bf16[16,1,16,256]{3,2,1,0:T(8,128)(2,1)S(1)}, u32[]{:S(2)}, u32[]{:S(2)}) collective-permute-start(bf16[16,1,16,256]{3,2,1,0:T(8,128)(2,1)} %bitcast.12), channel_id=1, source_target_pairs={{0,1},{1,0},{2,3},{3,2},{4,5},{5,4},{6,7},{7,6},{8,9},{9,8},{10,11... | collective-permute-start | bytes 393224 | tf_op jit(solution)/shard_map/ppermute | solution.py:329
  45.2 10.0 %collective-permute-start.1 = (bf16[2,16,4096]{2,1,0:T(8,128)(2,1)S(1)}, bf16[2,16,4096]{2,1,0:T(8,128)(2,1)S(1)}, u32[]{:S(2)}, u32[]{:S(2)}) collective-permute-start(bf16[2,16,4096]{2,1,0:T(8,128)(2,1)S(1)} %pad_maximum_fusion.4), channel_id=1, source_target_pairs={{0,2},{1,3},{2,0},{3,1},{4,6},{5,7},{6,4},{7,5},{8,10},{9,11},{10,... | collective-permute-start | bytes 786440 | tf_op jit(solution)/shard_map/ppermute | solution.py:329
  54.7 8.7 %collective-permute-start.9 = (bf16[16,2,16,256]{3,2,1,0:T(8,128)(2,1)}, bf16[16,2,16,256]{3,2,1,0:T(8,128)(2,1)}, u32[]{:S(2)}, u32[]{:S(2)}) collective-permute-start(bf16[16,2,16,256]{3,2,1,0:T(8,128)(2,1)} %pad_maximum_fusion.5), channel_id=1, source_target_pairs={{0,2},{1,3},{2,0},{3,1},{4,6},{5,7},{6,4},{7,5},{8,10},{9,11},{10,... | collective-permute-start | bytes 786440 | tf_op jit(solution)/shard_map/ppermute | solution.py:329
  57.8 18.5 %collective-permute-start.2 = (bf16[4,16,4096]{2,1,0:T(8,128)(2,1)}, bf16[4,16,4096]{2,1,0:T(8,128)(2,1)}, u32[]{:S(2)}, u32[]{:S(2)}) collective-permute-start(bf16[4,16,4096]{2,1,0:T(8,128)(2,1)} %pad_maximum_fusion.2), channel_id=1, source_target_pairs={{0,4},{1,5},{2,6},{3,7},{4,0},{5,1},{6,2},{7,3},{8,12},{9,13},{10,... | collective-permute-start | bytes 1572872 | tf_op jit(solution)/shard_map/ppermute | solution.py:329
  64.6 21.7 %collective-permute-start.10 = (bf16[16,4,16,256]{3,2,1,0:T(8,128)(2,1)S(1)}, bf16[16,4,16,256]{3,2,1,0:T(8,128)(2,1)S(1)}, u32[]{:S(2)}, u32[]{:S(2)}) collective-permute-start(bf16[16,4,16,256]{3,2,1,0:T(8,128)(2,1)S(1)} %pad_maximum_fusion.3), channel_id=1, source_target_pairs={{0,4},{1,5},{2,6},{3,7},{4,0},{5,1},{6,2},{7,3},{8,12},{9,13},{10,... | collective-permute-start | bytes 1572872 | tf_op jit(solution)/shard_map/ppermute | solution.py:329
  92.2 36.7 %copy-start.1 = (bf16[128,1024]{1,0:T(8,128)(2,1)S(1)}, bf16[128,1024]{1,0:T(8,128)(2,1)}, u32[]{:S(2)}) copy-start(bf16[128,1024]{1,0:T(8,128)(2,1)} %x_ref.3) | copy-start | bytes 786436
  92.2 36.7 %copy-start.8 = (f32[4,1024]{1,0:T(4,128)S(1)}, f32[4,1024]{1,0:T(4,128)}, u32[]{:S(2)}) copy-start(f32[4,1024]{1,0:T(4,128)} %cx_ref.3) | copy-start | bytes 49156
  92.2 58.4 %collective-permute-start.11 = (bf16[256,1024]{1,0:T(8,128)(2,1)}, bf16[256,1024]{1,0:T(8,128)(2,1)}, u32[]{:S(2)}, u32[]{:S(2)}) collective-permute-start(bf16[256,1024]{1,0:T(8,128)(2,1)} %convolution_convert_fusion), channel_id=1, source_target_pairs={{0,128},{128,0},{1,129},{129,1},{2,130},{130,2},{3,131},{131,3},{4... | collective-permute-start | bytes 1572872 | tf_op jit(solution)/shard_map/ppermute | solution.py:329
  123.8 5.2 %copy-start.14 = (f32[4,128]{1,0:T(4,128)S(1)}, f32[4,128]{1,0:T(4,128)}, u32[]{:S(2)}) copy-start(f32[4,128]{1,0:T(4,128)} %cb_ref.3) | copy-start | bytes 6148
  123.8 5.2 %copy-start.16 = (f32[4,128]{1,0:T(4,128)S(1)}, f32[4,128]{1,0:T(4,128)}, u32[]{:S(2)}) copy-start(f32[4,128]{1,0:T(4,128)} %cc_ref.3) | copy-start | bytes 6148
  123.8 5.2 %copy-start.18 = (s32[128]{0:T(128)S(1)}, s32[128]{0:T(128)}, u32[]{:S(2)}) copy-start(s32[128]{0:T(128)} %param.21) | copy-start | bytes 1540
  123.8 5.2 %copy-start.20 = (f32[16]{0:T(128)S(1)}, f32[16]{0:T(128)}, u32[]{:S(2)}) copy-start(f32[16]{0:T(128)} %param.26) | copy-start | bytes 196
  133.9 19.1 %copy-start.2 = (bf16[128,16]{1,0:T(8,128)(2,1)}, bf16[128,16]{1,0:T(8,128)(2,1)S(1)}, u32[]{:S(2)}) copy-start(bf16[128,16]{1,0:T(8,128)(2,1)S(1)} %get-tuple-element.102) | copy-start | bytes 12292
  133.9 1.2 collective-permute-start.3
  135.1 3.9 %collective-permute-start.4 = (f32[56,128]{1,0:T(8,128)S(1)}, f32[56,128]{1,0:T(8,128)S(1)}, u32[]{:S(2)}, u32[]{:S(2)}) collective-permute-start(f32[56,128]{1,0:T(8,128)S(1)} %add.18), channel_id=1, source_target_pairs={{0,128},{128,0},{1,129},{129,1},{2,130},{130,2},{3,131},{131,3},{4... | collective-permute-start | bytes 86024 | tf_op jit(solution)/shard_map/ppermute | solution.py:329
  139.0 3.9 %collective-permute-start.5 = (f32[56,128]{1,0:T(8,128)S(1)}, f32[56,128]{1,0:T(8,128)S(1)}, u32[]{:S(2)}, u32[]{:S(2)}) collective-permute-start(f32[56,128]{1,0:T(8,128)S(1)} %add.19), channel_id=1, source_target_pairs={{0,16},{8,24},{16,0},{24,8},{32,48},{40,56},{48,32},{56,40},{64,80... | collective-permute-start | bytes 86024 | tf_op jit(solution)/shard_map/ppermute | solution.py:329
  142.9 5.1 %collective-permute-start.6 = (f32[56,128]{1,0:T(8,128)S(1)}, f32[56,128]{1,0:T(8,128)S(1)}, u32[]{:S(2)}, u32[]{:S(2)}) collective-permute-start(f32[56,128]{1,0:T(8,128)S(1)} %add.20), channel_id=1, source_target_pairs={{0,32},{8,40},{16,48},{24,56},{32,0},{40,8},{48,16},{56,24},{64,96... | collective-permute-start | bytes 86024 | tf_op jit(solution)/shard_map/ppermute | solution.py:329
  147.9 7.8 %collective-permute-start.7 = (f32[56,128]{1,0:T(8,128)S(1)}, f32[56,128]{1,0:T(8,128)S(1)}, u32[]{:S(2)}, u32[]{:S(2)}) collective-permute-start(f32[56,128]{1,0:T(8,128)S(1)} %add.21), channel_id=1, source_target_pairs={{0,64},{8,72},{16,80},{24,88},{32,96},{40,104},{48,112},{56,120},{... | collective-permute-start | bytes 86024 | tf_op jit(solution)/shard_map/ppermute | solution.py:329
  (21 other events, 38.5 us)
Sparse Core Ops, SparseCore 0:
  20.8 47.3 all-gather.4
  69.9 53.8 all-gather.2

commit v2 on v1

--- a/solution.py
+++ b/solution.py
@@ -8,10 +8,12 @@
 HDIM = 64
 LANES = 128
 KCONV = 4
+CHUNKS = 8
+FORWARD_ARGS = 13
 EPS = 1e-05
 F32 = jnp.float32
 BF16 = jnp.bfloat16
-VMEM_LIMIT = 48 * 1024 * 1024
+MIB = 1024 * 1024
 
 
 def split2(value):
@@ -106,11 +108,25 @@
     return jnp.concatenate([jnp.where(left, value, zero), jnp.where(left, zero, value)], axis=0)
 
 
+def staged_forward(count_ref, *refs):
+    count = FORWARD_ARGS
+    inputs, outputs, held, sems = refs[:count], refs[count : -count - 1], refs[-count - 1 : -1], refs[-1]
+    copies = [
+        pltpu.make_async_copy(source, target, sems.at[i])
+        for i, (source, target) in enumerate(zip(inputs, held))
+    ]
+    for copy in copies:
+        copy.start()
+    for copy in copies:
+        copy.wait()
+    forward_kernel(count_ref, *held, *outputs)
+
+
 def forward_kernel(
     count_ref, z_ref, x_ref, b_ref, c_ref, dt_ref, seg_ref, cx_ref, cb_ref, cc_ref, al_ref, bias_ref, skip_ref, gain_ref,
     norm_ref, xc_ref, dsx_ref, ssm_ref, gate_ref, dgate_ref, bcc_ref, small_ref, cumt_ref, rms_ref,
 ):
-    heads = dt_ref.shape[1]
+    heads = dt_ref.shape[0]
     tiles = x_ref.shape[1] // LANES
     seg_rows, seg_cols, masks = shift_masks(seg_ref[...])
     rows, cols = iota(0), iota(1)
@@ -125,7 +141,7 @@
     scores = dot_nt(c_conv, b_conv)
     bcc_ref[4] = scores.T
 
-    raw = dt_ref[...].astype(F32) + bias_ref[...]
+    raw = dt_ref[...].astype(F32).T + bias_ref[...]
     step = jnp.maximum(raw, 0.0) + jnp.log1p(jnp.exp(-jnp.abs(raw)))
     decay = -jnp.exp(al_ref[...]) * step
     lower = jnp.where(rows >= cols, 1.0, 0.0).astype(BF16)
@@ -173,10 +189,19 @@
 
 
 def backward_kernel(
-    count_ref, up_ref, x_ref, b_ref, c_ref, seg_ref, cx_ref, cb_ref, cc_ref, al_ref, skip_ref, gain_ref,
+    count_ref, rows_ref, w_ref, x_ref, b_ref, c_ref, seg_ref, cx_ref, cb_ref, cc_ref, al_ref, skip_ref, gain_ref,
     xc_ref, dsx_ref, ssm_ref, gate_ref, dgate_ref, bcc_ref, small_ref, cumt_ref, rms_ref,
-    gz_ref, gx_ref, gb_ref, gc_ref, gdt_ref, par_ref,
+    gz_ref, gx_ref, gb_ref, gc_ref, gdt_ref, par_ref, w_vmem, up_ref, sems,
 ):
+    depth = w_ref.shape[0] // CHUNKS
+    copies = [
+        pltpu.make_async_copy(
+            w_ref.at[pl.ds(i * depth, depth)], w_vmem.at[pl.ds(i * depth, depth)], sems.at[i]
+        )
+        for i in range(CHUNKS)
+    ]
+    for copy in copies:
+        copy.start()
     heads = small_ref.shape[2]
     tiles = x_ref.shape[1] // LANES
     seg_rows, seg_cols, masks = shift_masks(seg_ref[...])
@@ -190,6 +215,16 @@
     expander = head_expander(heads)
     step_wide = dot_exact(split3(step), expander)
     skip_wide = dot_exact(split3(jnp.broadcast_to(skip_ref[...], (8, heads))), expander)
+
+    place = count_ref[1]
+    for i, copy in enumerate(copies):
+        part = slice(i * depth, (i + 1) * depth)
+        left = jnp.concatenate(
+            [rows_ref[lax.bitwise_xor(place, j), :, part] for j in range(rows_ref.shape[0])], axis=0
+        )
+        copy.wait()
+        product = jnp.dot(left, w_vmem[part, :], preferred_element_type=F32)
+        up_ref[...] = product if i == 0 else up_ref[...] + product
 
     dots = jnp.zeros((LANES, LANES), F32)
     for tile in range(tiles):
@@ -265,7 +300,7 @@
     d_decay = sums[:, 0:heads]
     d_step = sums[:, heads : 2 * heads] - jnp.exp(al_ref[...]) * d_decay
     d_raw = d_step * slope
-    gdt_ref[...] = d_raw.astype(BF16)
+    gdt_ref[...] = d_raw.T.astype(BF16)
     par_ref[48:49, 0:heads] = jnp.sum(d_decay * decay, axis=0, keepdims=True)
     par_ref[49:50, 0:heads] = jnp.sum(d_raw, axis=0, keepdims=True)
     par_ref[50:51, 0:heads] = jnp.sum(sums[:, 2 * heads : 3 * heads], axis=0, keepdims=True)
@@ -303,11 +338,45 @@
     skip_ref[...] = total[50:51, 0:heads]
 
 
-def call(kernel, operands, outs, flops, smem_first=True):
+def weight_kernel(meta_ref, col_ref, own_ref, *refs):
+    *blocks, out_ref = refs
+    place, chip, core = meta_ref[1], meta_ref[2], meta_ref[3]
+    chips = col_ref.shape[0] // 2
+    reach = chips // 2
+
+    def columns(shard):
+        return [col_ref[shard, lax.bitwise_xor(place, j)] for j in range(col_ref.shape[1])]
+
+    def product(pieces, block):
+        return lax.dot_general(
+            jnp.concatenate(pieces, axis=0), block, (((0,), (0,)), ((), ())), preferred_element_type=F32
+        )
+
+    def pair(which):
+        return columns(2 * which) + columns(2 * which + 1)
+
+    total = product(pair(chip), own_ref[...])
+    toward = 1 - 2 * core
+    for k in range(1, reach):
+        back = lax.rem(chip - toward * k + chips, chips)
+        ahead = lax.rem(chip + toward * k + chips, chips)
+        total = total + product(pair(back), blocks[k - 1][...])
+        total = total + product(pair(ahead), blocks[reach + k - 1][...])
+    far = 2 * lax.rem(chip + reach, chips)
+    total = total + product(columns(far + core), blocks[reach - 1][...])
+    total = total + product(columns(far + 1 - core), blocks[2 * reach - 1][...])
+    out_ref[...] = total.astype(out_ref.dtype)
+
+
+def call(kernel, operands, outs, flops, smem=1, hbm=(), scratch=(), fixed=(), limit=32):
     vmem = pl.BlockSpec(memory_space=pltpu.VMEM)
-    specs = [vmem] * len(operands)
-    if smem_first:
-        specs[0] = pl.BlockSpec(memory_space=pltpu.SMEM)
+    specs = [pl.BlockSpec()] * len(operands)
+    for i in range(smem):
+        specs[i] = pl.BlockSpec(memory_space=pltpu.SMEM)
+    for i in hbm:
+        specs[i] = pl.BlockSpec(memory_space=pl.ANY)
+    for i in fixed:
+        specs[i] = vmem
     size = sum(a.size * a.dtype.itemsize for a in operands) + sum(
         a.size * a.dtype.itemsize for a in outs
     )
@@ -316,7 +385,8 @@
         out_shape=outs,
         in_specs=specs,
         out_specs=[vmem] * len(outs),
-        compiler_params=pltpu.CompilerParams(vmem_limit_bytes=VMEM_LIMIT),
+        scratch_shapes=scratch,
+        compiler_params=pltpu.CompilerParams(vmem_limit_bytes=limit * MIB),
         cost_estimate=pl.CostEstimate(flops=flops, bytes_accessed=size, transcendentals=0),
     )(*operands)
 
@@ -330,15 +400,25 @@
 
 
 def gather_tensor(block, axis):
-    me = lax.axis_index("tensor")
-    held = jnp.expand_dims(block, axis)
-    for bit in (1, 2, 4):
-        other = swap(held, "tensor", bit, 8)
-        first = (me & bit) == 0
-        held = jnp.concatenate(
-            [jnp.where(first, held, other), jnp.where(first, other, held)], axis=axis
-        )
-    return held
+    held = jnp.expand_dims(block, (axis, axis + 1, axis + 2))
+    for bit, where in ((4, axis), (1, axis + 2), (2, axis + 1)):
+        held = jnp.concatenate([held, swap(held, "tensor", bit, 8)], axis=where)
+    return held.reshape(block.shape[:axis] + (8,) + block.shape[axis:])
+
+
+def gather_chips(block, core, dp):
+    chips, size = dp // 2, block.shape[0]
+    other = swap(block, "dp", 1, dp)
+    first = core == 0
+    pair = jnp.concatenate([jnp.where(first, block, other), jnp.where(first, other, block)], axis=0)
+    ring = [(2 * z, 2 * ((z + 1) % chips)) for z in range(chips)]
+    ring += [(2 * z + 1, 2 * ((z - 1) % chips) + 1) for z in range(chips)]
+    got, current = [], pair
+    for _ in range(chips // 2 - 1):
+        current = lax.ppermute(current, "dp", ring)
+        got.append(current)
+    got.append(lax.ppermute(jnp.where(first, current[:size], current[size:]), "dp", ring))
+    return pair, *got, *[swap(value, "dp", 1, dp) for value in got]
 
 
 def body(
@@ -347,42 +427,58 @@
 ):
     length, width = z_act.shape
     heads = dt_act.shape[1]
-    features = d_out.shape[1]
+    own, features = d_out.shape
     dp = lax.axis_size("dp")
+    shard = lax.axis_index("dp")
+    core = shard % 2
+    meta = jnp.stack([counts[0], lax.axis_index("tensor"), shard // 2, core]).astype(jnp.int32)
     seg_row = segment.reshape(1, length)
     a_log, dt_bias, d_skip = (v.reshape(1, heads) for v in (a_log, dt_bias, d_skip))
     gain = norm_gain.reshape(1, width)
 
     w_all = lax.all_gather(w_out, "dp", axis=0, tiled=True)
 
-    own = d_out.shape[0]
-    rows = gather_tensor(d_out, 0).reshape(length, features)
+    rows = gather_tensor(d_out, 0)
     pieces = d_out.reshape(own, dp, features // dp).transpose(1, 0, 2)
     pieces = lax.all_to_all(pieces, "dp", 0, 0, tiled=False)
-    columns = gather_tensor(pieces, 1).reshape(dp * length, features // dp)
+    columns = gather_tensor(pieces, 1)
 
     wide = shape((length, width))
+    operands = (
+        meta, z_act, x_act, b_act, c_act, dt_act.T, seg_row, conv_x, conv_b, conv_c, a_log, dt_bias, d_skip, gain,
+    )
     normed, *saved = call(
-        forward_kernel,
-        (counts, z_act, x_act, b_act, c_act, dt_act, seg_row, conv_x, conv_b, conv_c, a_log, dt_bias, d_skip, gain),
+        staged_forward,
+        operands,
         [
             shape((length, width), BF16), wide, wide, wide, wide, wide,
             shape((5, LANES, LANES)), shape((4, length, heads)), shape((heads, length)), shape((LANES, LANES)),
         ],
         300_000_000,
-    )
-    normed_all = lax.all_gather(normed, "dp", axis=0, tiled=True)
-
-    upstream = jnp.dot(rows, w_all, preferred_element_type=F32)
+        hbm=range(1, 1 + FORWARD_ARGS),
+        limit=56,
+        scratch=[pltpu.VMEM(a.shape, a.dtype) for a in operands[1:]] + [pltpu.SemaphoreType.DMA((FORWARD_ARGS,))],
+    )
+    blocks = gather_chips(normed, core, dp)
+
+    operands = (
+        meta, rows, w_all, x_act, b_act, c_act, seg_row, conv_x, conv_b, conv_c, a_log, d_skip, gain, *saved,
+    )
     *act_grads, packed = call(
         backward_kernel,
-        (counts, upstream, x_act, b_act, c_act, seg_row, conv_x, conv_b, conv_c, a_log, d_skip, gain, *saved),
+        operands,
         [
             shape((length, width), BF16), shape((length, width), BF16), shape((length, LANES), BF16),
-            shape((length, LANES), BF16), shape((length, heads), BF16), shape((56, LANES)),
+            shape((length, LANES), BF16), shape((heads, length), BF16), shape((56, LANES)),
         ],
-        600_000_000,
-    )
+        1_700_000_000,
+        hbm=(2,),
+        fixed=(1, *range(len(operands) - len(saved), len(operands))),
+        scratch=[
+            pltpu.VMEM((features, width), BF16), pltpu.VMEM((length, width), F32), pltpu.SemaphoreType.DMA((CHUNKS,)),
+        ],
+    )
+    act_grads[4] = act_grads[4].T
     packed = packed + swap(packed, "dp", 1, dp)
     packed = packed + swap(packed, "rep", 1, 2)
     for bit in (2, 4, 8):
@@ -395,12 +491,16 @@
             shape((1, heads)), shape((1, heads)), shape((1, heads)), shape((1, width)),
         ],
         1000,
-        smem_first=False,
-    )
-
-    share = lax.dot_general(
-        columns, normed_all, (((0,), (0,)), ((), ())), preferred_element_type=F32
-    ).astype(BF16)
+        smem=0,
+    )
+
+    share = call(
+        weight_kernel,
+        (meta, columns, *blocks),
+        [shape((features // dp, width), BF16)],
+        1_100_000_000,
+        fixed=range(1, 2 + len(blocks)),
+    )[0]
     weight_grad = share.astype(F32) + swap(share, "rep", 1, 2).astype(F32)
     return (
         *act_grads,

time: 165 us -> 163 us (0.988)
  blocking collectives: 0 us -> 27.6 us
  waiting for transfers between devices: 81.5 us -> 67.4 us
  matrix products: 9.76 us -> 0 us
  starting transfers between devices: 24.7 us -> 15.5 us
  Pallas kernels: 8.06 us -> 15.7 us
  other arithmetic: 11.5 us -> 6.1 us
    all_gather x1, waiting for transfers between devices: 31.3 us -> 0.02 us  [body(): w_all = lax.all_gather(w_out, 'dp', axis=0, tiled=True)]
    all_to_all x0 -> x1, blocking collectives: none -> 27.6 us  [body(): pieces = lax.all_to_all(pieces, 'dp', 0, 0, tiled=False)]
    ppermute x0 -> x4, waiting for transfers between devices: none -> 18.6 us  [the longest x3 18.6 us: gather_chips(): current = lax.ppermute(current, 'dp', ring)]
    dot_general x2 -> x0, matrix products: 9.76 us -> none  [the longest x1 5.03 us: body(): upstream = jnp.dot(rows, w_all, preferred_element_type=F32)]
    all_to_all x1 -> x0, waiting for transfers between devices: 9.12 us -> none  [body(): pieces = lax.all_to_all(pieces, 'dp', 0, 0, tiled=False)]
    all_to_all x1 -> x0, starting transfers between devices: 8.62 us -> none  [body(): pieces = lax.all_to_all(pieces, 'dp', 0, 0, tiled=False)]
    ppermute x12 -> x17, waiting for transfers between devices: 40.4 us -> 48.1 us  [swap(): return lax.ppermute(value, axis, [(i, i ^ bit) for i in range(size)])]
    pallas_call x3 -> x4, Pallas kernels: 8.06 us -> 15.7 us  [call(): pl.pallas_call(kernel, out_shape=outs, in_specs=specs, out_specs=[vmem] *...]
  transfers between devices with their start and end apart: 15 -> 22, of which waited for: 11 -> 14; matrix products, arithmetic and copies ran while one was open for 14% -> 3% of each run, Pallas kernels for 3% -> 9%
where the time goes in v2:
time: 163 us
  waiting for transfers between devices  67.4 us (41%)
  blocking collectives  27.6 us (17%)
  Pallas kernels  15.7 us (10%)
  starting transfers between devices  15.5 us (10%)
  local copies, waits for them, and re-layouts  15.2 us (9%)
  between operations  15 us (9%)
  other arithmetic  6.1 us (4%)
    ppermute x17, waiting for transfers between devices, swap(): return lax.ppermute(value, axis, [(i, i ^ bit) for i in range(size)])  48.1 us
    all_to_all x1, blocking collectives, body(): pieces = lax.all_to_all(pieces, 'dp', 0, 0, tiled=False)  27.6 us
    ppermute x3, waiting for transfers between devices, gather_chips(): current = lax.ppermute(current, 'dp', ring)  18.6 us
    pallas_call x4, Pallas kernels, call(): pl.pallas_call(kernel, out_shape=outs, in_specs=specs, out_specs=[vmem] *...  15.7 us
    unnamed x46, local copies, waits for them, and re-layouts  14.3 us
    ppermute x17, starting transfers between devices, swap(): return lax.ppermute(value, axis, [(i, i ^ bit) for i in range(size)])  13.4 us
  transfers between devices with their start and end apart: 22, of which 14 were waited for; matrix products, arithmetic and copies ran while one was open for 3% of the time, Pallas kernels for 9%

profile of v2, /device:TPU:2, one launch (start us, length us, event | category | flops | bytes accessed | tf_op | source)
XLA Modules:
  0.0 162.5 jit_solution(8884703596329332744)
XLA Ops:
  9.2 5.2 %shard_map.255 = (bf16[128,1024]{1,0:T(8,128)(2,1)}, f32[128,1024]{1,0:T(8,128)}, f32[128,1024]{1,0:T(8,128)}, f32[128,1024]{1,0:T(8,128)}, f32[128,1024]{1,0:T(...) custom-call(s32[4]{0:T(128)} %pad_add_fusion.count_ref.meta_ref, ...), custom_call_target="tpu_custom_call" | custom-call | flops 300000000 | bytes 3936976 | tf_op jit(solution)/shard_map/pallas_call | solution.py:383
  14.5 1.7 %collective-permute-done.11 = bf16[128,1024]{1,0:T(8,128)(2,1)S(1)} collective-permute-done((bf16[128,1024]{1,0:T(8,128)(2,1)}, bf16[128,1024]{1,0:T(8,128)(2,1)S(1)}, u32[]{:S(2)}, u32[]{:S(2)}) %collective-permute-start.11) | collective-permute-done | bytes 262176 | tf_op jit(solution)/shard_map/ppermute | solution.py:399
  17.3 2.0 %collective-permute-start.12 = (bf16[256,1024]{1,0:T(8,128)(2,1)S(1)}, bf16[256,1024]{1,0:T(8,128)(2,1)S(1)}, u32[]{:S(2)}, u32[]{:S(2)}) collective-permute-start(bf16[256,1024]{1,0:T(8,128)(2,1)S(1)} %pad_maximum_fusion.4.own_ref), channel_id=1, source_target_pairs={{0,16},{16,32},{32,48},{48,64},{64,80},{80,96},{96,112},{112,0},{8... | collective-permute-start | bytes 1572872 | tf_op jit(solution)/shard_map/ppermute | solution.py:418
  19.3 16.4 %collective-permute-done.12.refs_0_ = bf16[256,1024]{1,0:T(8,128)(2,1)S(1)} collective-permute-done((bf16[256,1024]{1,0:T(8,128)(2,1)S(1)}, bf16[256,1024]{1,0:T(8,128)(2,1)S(1)}, u32[]{:S(2)}, u32[]{:S(2)}) %collective-permute-start.12) | collective-permute-done | bytes 524320 | tf_op jit(solution)/shard_map/ppermute | solution.py:418
  36.6 27.6 %all_to_all.5 = bf16[16,16,256]{2,1,0:T(8,128)(2,1)S(1)} all-to-all(bf16[16,16,256]{2,1,0:T(8,128)(2,1)S(1)} %bitcast.44), channel_id=1, replica_groups=mesh['rep'=2,'dp'=16,'tensor'=8] {'dp'}, dimensions={0} | all-to-all | bytes 262144 | tf_op jit(solution)/shard_map/all_to_all | solution.py:443
  64.2 2.2 %collective-permute-start.8 = (bf16[16,1,1,1,16,256]{5,4,3,2,1,0:T(8,128)(2,1)S(1)}, bf16[16,1,1,1,16,256]{5,4,3,2,1,0:T(8,128)(2,1)S(1)}, u32[]{:S(2)}, u32[]{:S(2)}) collective-permute-start(bf16[16,1,1,1,16,256]{5,4,3,2,1,0:T(8,128)(2,1)S(1)} %bitcast.40), channel_id=1, source_target_pairs={{0,4},{1,5},{2,6},{3,7},{4,0},{5,1},{6,2},{7,3},{8,12},{9,13},{10,... | collective-permute-start | bytes 393224 | tf_op jit(solution)/shard_map/ppermute | solution.py:399
  66.5 1.3 collective-permute-start
  67.8 4.3 %collective-permute-done.8 = bf16[16,1,1,1,16,256]{5,4,3,2,1,0:T(8,128)(2,1)S(1)} collective-permute-done((bf16[16,1,1,1,16,256]{5,4,3,2,1,0:T(8,128)(2,1)S(1)}, bf16[16,1,1,1,16,256]{5,4,3,2,1,0:T(8,128)(2,1)S(1)}, u32[]{:S(2)}, u32[]{:S(2)}) %collective-permute-start.8) | collective-permute-done | bytes 131104 | tf_op jit(solution)/shard_map/ppermute | solution.py:399
  72.1 3.7 %collective-permute-start.9 = (bf16[16,2,1,1,16,256]{5,4,3,2,1,0:T(8,128)(2,1)S(1)}, bf16[16,2,1,1,16,256]{5,4,3,2,1,0:T(8,128)(2,1)S(1)}, u32[]{:S(2)}, u32[]{:S(2)}) collective-permute-start(bf16[16,2,1,1,16,256]{5,4,3,2,1,0:T(8,128)(2,1)S(1)} %pad_maximum_fusion.6), channel_id=1, source_target_pairs={{0,1},{1,0},{2,3},{3,2},{4,5},{5,4},{6,7},{7,6},{8,9},{9,8},{10,11... | collective-permute-start | bytes 786440 | tf_op jit(solution)/shard_map/ppermute | solution.py:399
  76.8 2.7 %collective-permute-start.1 = (bf16[2,1,1,16,4096]{4,3,2,1,0:T(8,128)(2,1)S(1)}, bf16[2,1,1,16,4096]{4,3,2,1,0:T(8,128)(2,1)S(1)}, u32[]{:S(2)}, u32[]{:S(2)}) collective-permute-start(bf16[2,1,1,16,4096]{4,3,2,1,0:T(8,128)(2,1)S(1)} %pad_maximum_fusion.5), channel_id=1, source_target_pairs={{0,1},{1,0},{2,3},{3,2},{4,5},{5,4},{6,7},{7,6},{8,9},{9,8},{10,11... | collective-permute-start | bytes 786440 | tf_op jit(solution)/shard_map/ppermute | solution.py:399
  79.5 3.4 %collective-permute-done.9 = bf16[16,2,1,1,16,256]{5,4,3,2,1,0:T(8,128)(2,1)S(1)} collective-permute-done((bf16[16,2,1,1,16,256]{5,4,3,2,1,0:T(8,128)(2,1)S(1)}, bf16[16,2,1,1,16,256]{5,4,3,2,1,0:T(8,128)(2,1)S(1)}, u32[]{:S(2)}, u32[]{:S(2)}) %collective-permute-start.9) | collective-permute-done | bytes 262176 | tf_op jit(solution)/shard_map/ppermute | solution.py:399
  84.0 2.2 %collective-permute-done.14.refs_2_ = bf16[256,1024]{1,0:T(8,128)(2,1)S(1)} collective-permute-done((bf16[256,1024]{1,0:T(8,128)(2,1)S(1)}, bf16[256,1024]{1,0:T(8,128)(2,1)S(1)}, u32[]{:S(2)}, u32[]{:S(2)}) %collective-permute-start.14) | collective-permute-done | bytes 524320 | tf_op jit(solution)/shard_map/ppermute | solution.py:418
  86.3 1.9 %collective-permute-done.1 = bf16[2,1,1,16,4096]{4,3,2,1,0:T(8,128)(2,1)S(1)} collective-permute-done((bf16[2,1,1,16,4096]{4,3,2,1,0:T(8,128)(2,1)S(1)}, bf16[2,1,1,16,4096]{4,3,2,1,0:T(8,128)(2,1)S(1)}, u32[]{:S(2)}, u32[]{:S(2)}) %collective-permute-start.1) | collective-permute-done | bytes 262176 | tf_op jit(solution)/shard_map/ppermute | solution.py:399
  89.2 7.2 %collective-permute-done.10 = bf16[16,2,1,2,16,256]{5,4,3,2,1,0:T(8,128)(2,1)S(1)} collective-permute-done((bf16[16,2,1,2,16,256]{5,4,3,2,1,0:T(8,128)(2,1)S(1)}, bf16[16,2,1,2,16,256]{5,4,3,2,1,0:T(8,128)(2,1)S(1)}, u32[]{:S(2)}, u32[]{:S(2)}) %collective-permute-start.10) | collective-permute-done | bytes 524320 | tf_op jit(solution)/shard_map/ppermute | solution.py:399
  96.8 1.4 collective-permute-done.19.refs_7_
  98.2 2.0 %shard_map.258 = bf16[256,1024]{1,0:T(8,128)(2,1)S(1)} custom-call(s32[4]{0:T(128)S(1)} %copy-done.14, bf16[16,8,16,256]{3,2,1,0:T(8,128)(2,1)S(1)} %bitcast.25, bf16[256,1024]{1,0:T(8,128)(2,1)S(1)} %pad_maximum_fusion.4.own_ref, bf16[256,1024]{1,0:T(8,128)(2,1)S(1)} %collective-permute-done.12.refs_0_, ...), custom_call_target="tpu_custom_call" | custom-call | flops 1100000000 | bytes 5767184 | tf_op jit(solution)/shard_map/pallas_call | solution.py:383
  101.4 7.3 %collective-permute-done.2 = bf16[2,1,2,16,4096]{4,3,2,1,0:T(8,128)(2,1)S(1)} collective-permute-done((bf16[2,1,2,16,4096]{4,3,2,1,0:T(8,128)(2,1)S(1)}, bf16[2,1,2,16,4096]{4,3,2,1,0:T(8,128)(2,1)S(1)}, u32[]{:S(2)}, u32[]{:S(2)}) %collective-permute-start.2) | collective-permute-done | bytes 524320 | tf_op jit(solution)/shard_map/ppermute | solution.py:399
  109.0 3.4 %copy-done = bf16[4096,1024]{1,0:T(8,128)(2,1)S(1)} copy-done((bf16[4096,1024]{1,0:T(8,128)(2,1)S(1)}, bf16[4096,1024]{1,0:T(8,128)(2,1)}, u32[]{:S(2)}) %copy-start) | copy-done | bytes 8388632
  123.2 7.9 %shard_map.256 = (bf16[128,1024]{1,0:T(8,128)(2,1)}, bf16[128,1024]{1,0:T(8,128)(2,1)}, bf16[128,128]{1,0:T(8,128)(2,1)}, bf16[128,128]{1,0:T(8,128)(2,1)}, bf16...) custom-call(s32[4]{0:T(128)S(1)} %copy-done.15, bf16[8,16,4096]{2,1,0:T(8,128)(2,1)S(1)} %bitcast.26, ...), custom_call_target="tpu_custom_call" | custom-call | flops 1700000000 | bytes 13468304 | tf_op jit(solution)/shard_map/pallas_call | solution.py:383
  133.2 3.2 %collective-permute-done.4 = f32[56,128]{1,0:T(8,128)S(1)} collective-permute-done((f32[56,128]{1,0:T(8,128)S(1)}, f32[56,128]{1,0:T(8,128)S(1)}, u32[]{:S(2)}, u32[]{:S(2)}) %collective-permute-start.4) | collective-permute-done | bytes 28704 | tf_op jit(solution)/shard_map/ppermute | solution.py:399
  136.4 3.9 %collective-permute-done.5 = f32[56,128]{1,0:T(8,128)S(1)} collective-permute-done((f32[56,128]{1,0:T(8,128)S(1)}, f32[56,128]{1,0:T(8,128)S(1)}, u32[]{:S(2)}, u32[]{:S(2)}) %collective-permute-start.5) | collective-permute-done | bytes 28704 | tf_op jit(solution)/shard_map/ppermute | solution.py:399
  140.2 4.8 %collective-permute-done.6 = f32[56,128]{1,0:T(8,128)S(1)} collective-permute-done((f32[56,128]{1,0:T(8,128)S(1)}, f32[56,128]{1,0:T(8,128)S(1)}, u32[]{:S(2)}, u32[]{:S(2)}) %collective-permute-start.6) | collective-permute-done | bytes 28704 | tf_op jit(solution)/shard_map/ppermute | solution.py:399
  145.1 7.8 %collective-permute-done.7 = f32[56,128]{1,0:T(8,128)S(1)} collective-permute-done((f32[56,128]{1,0:T(8,128)S(1)}, f32[56,128]{1,0:T(8,128)S(1)}, u32[]{:S(2)}, u32[]{:S(2)}) %collective-permute-start.7) | collective-permute-done | bytes 28704 | tf_op jit(solution)/shard_map/ppermute | solution.py:399
  152.9 2.2 %convert_add_fusion = f32[256,1024]{1,0:T(8,128)} fusion(bf16[256,1024]{1,0:T(8,128)(2,1)} %collective-permute-done.20, bf16[256,1024]{1,0:T(8,128)(2,1)S(1)} %shard_map.258), kind=kLoop, calls=%fused_computation.2 | loop fusion | flops 786432 | bytes 2097152 | tf_op jit(solution)/shard_map/add | solution.py:504
  (89 shorter events, 21.9 us)
Async XLA Ops:
  7.2 101.7 %all-gather.2.cloned.1.call-start = ((), (), s32[]{:S(2)}) async-start(), calls=%async_computation.1 | async-start | bytes 8912896 | tf_op jit(solution)/shard_map/all_gather | solution.py:439
  14.4 94.6 %copy-start.1 = (f32[128,1024]{1,0:T(8,128)S(1)}, f32[128,1024]{1,0:T(8,128)}, u32[]{:S(2)}) copy-start(f32[128,1024]{1,0:T(8,128)} %get-tuple-element.36.xc_ref) | copy-start | bytes 1572868
  14.4 94.6 %copy-start.2 = (f32[128,1024]{1,0:T(8,128)S(1)}, f32[128,1024]{1,0:T(8,128)}, u32[]{:S(2)}) copy-start(f32[128,1024]{1,0:T(8,128)} %get-tuple-element.37.dsx_ref) | copy-start | bytes 1572868
  14.4 1.8 %collective-permute-start.11 = (bf16[128,1024]{1,0:T(8,128)(2,1)}, bf16[128,1024]{1,0:T(8,128)(2,1)S(1)}, u32[]{:S(2)}, u32[]{:S(2)}) collective-permute-start(bf16[128,1024]{1,0:T(8,128)(2,1)} %get-tuple-element.58), channel_id=1, source_target_pairs={{0,8},{8,0},{16,24},{24,16},{32,40},{40,32},{48,56},{56,48},{64,72... | collective-permute-start | bytes 786440 | tf_op jit(solution)/shard_map/ppermute | solution.py:399
  17.3 18.4 %collective-permute-start.12 = (bf16[256,1024]{1,0:T(8,128)(2,1)S(1)}, bf16[256,1024]{1,0:T(8,128)(2,1)S(1)}, u32[]{:S(2)}, u32[]{:S(2)}) collective-permute-start(bf16[256,1024]{1,0:T(8,128)(2,1)S(1)} %pad_maximum_fusion.4.own_ref), channel_id=1, source_target_pairs={{0,16},{16,32},{32,48},{48,64},{64,80},{80,96},{96,112},{112,0},{8... | collective-permute-start | bytes 1572872 | tf_op jit(solution)/shard_map/ppermute | solution.py:418
  35.7 40.1 %collective-permute-start.13 = (bf16[256,1024]{1,0:T(8,128)(2,1)S(1)}, bf16[256,1024]{1,0:T(8,128)(2,1)S(1)}, u32[]{:S(2)}, u32[]{:S(2)}) collective-permute-start(bf16[256,1024]{1,0:T(8,128)(2,1)S(1)} %collective-permute-done.12.refs_0_), channel_id=1, source_target_pairs={{0,16},{16,32},{32,48},{48,64},{64,80},{80,96},{96,112},{112,0},{8... | collective-permute-start | bytes 1572872 | tf_op jit(solution)/shard_map/ppermute | solution.py:418
  64.2 7.8 %collective-permute-start.8 = (bf16[16,1,1,1,16,256]{5,4,3,2,1,0:T(8,128)(2,1)S(1)}, bf16[16,1,1,1,16,256]{5,4,3,2,1,0:T(8,128)(2,1)S(1)}, u32[]{:S(2)}, u32[]{:S(2)}) collective-permute-start(bf16[16,1,1,1,16,256]{5,4,3,2,1,0:T(8,128)(2,1)S(1)} %bitcast.40), channel_id=1, source_target_pairs={{0,4},{1,5},{2,6},{3,7},{4,0},{5,1},{6,2},{7,3},{8,12},{9,13},{10,... | collective-permute-start | bytes 393224 | tf_op jit(solution)/shard_map/ppermute | solution.py:399
  66.5 9.3 %collective-permute-start = (bf16[1,1,1,16,4096]{4,3,2,1,0:T(8,128)(2,1)}, bf16[1,1,1,16,4096]{4,3,2,1,0:T(8,128)(2,1)S(1)}, u32[]{:S(2)}, u32[]{:S(2)}) collective-permute-start(bf16[1,1,1,16,4096]{4,3,2,1,0:T(8,128)(2,1)} %bitcast.36), channel_id=1, source_target_pairs={{0,4},{1,5},{2,6},{3,7},{4,0},{5,1},{6,2},{7,3},{8,12},{9,13},{10,... | collective-permute-start | bytes 393224 | tf_op jit(solution)/shard_map/ppermute | solution.py:399
  72.1 10.8 %collective-permute-start.9 = (bf16[16,2,1,1,16,256]{5,4,3,2,1,0:T(8,128)(2,1)S(1)}, bf16[16,2,1,1,16,256]{5,4,3,2,1,0:T(8,128)(2,1)S(1)}, u32[]{:S(2)}, u32[]{:S(2)}) collective-permute-start(bf16[16,2,1,1,16,256]{5,4,3,2,1,0:T(8,128)(2,1)S(1)} %pad_maximum_fusion.6), channel_id=1, source_target_pairs={{0,1},{1,0},{2,3},{3,2},{4,5},{5,4},{6,7},{7,6},{8,9},{9,8},{10,11... | collective-permute-start | bytes 786440 | tf_op jit(solution)/shard_map/ppermute | solution.py:399
  75.8 10.4 %collective-permute-start.14 = (bf16[256,1024]{1,0:T(8,128)(2,1)S(1)}, bf16[256,1024]{1,0:T(8,128)(2,1)S(1)}, u32[]{:S(2)}, u32[]{:S(2)}) collective-permute-start(bf16[256,1024]{1,0:T(8,128)(2,1)S(1)} %collective-permute-done.13.refs_1_), channel_id=1, source_target_pairs={{0,16},{16,32},{32,48},{48,64},{64,80},{80,96},{96,112},{112,0},{8... | collective-permute-start | bytes 1572872 | tf_op jit(solution)/shard_map/ppermute | solution.py:418
  76.8 11.5 %collective-permute-start.1 = (bf16[2,1,1,16,4096]{4,3,2,1,0:T(8,128)(2,1)S(1)}, bf16[2,1,1,16,4096]{4,3,2,1,0:T(8,128)(2,1)S(1)}, u32[]{:S(2)}, u32[]{:S(2)}) collective-permute-start(bf16[2,1,1,16,4096]{4,3,2,1,0:T(8,128)(2,1)S(1)} %pad_maximum_fusion.5), channel_id=1, source_target_pairs={{0,1},{1,0},{2,3},{3,2},{4,5},{5,4},{6,7},{7,6},{8,9},{9,8},{10,11... | collective-permute-start | bytes 786440 | tf_op jit(solution)/shard_map/ppermute | solution.py:399
  83.0 13.4 %collective-permute-start.10 = (bf16[16,2,1,2,16,256]{5,4,3,2,1,0:T(8,128)(2,1)S(1)}, bf16[16,2,1,2,16,256]{5,4,3,2,1,0:T(8,128)(2,1)S(1)}, u32[]{:S(2)}, u32[]{:S(2)}) collective-permute-start(bf16[16,2,1,2,16,256]{5,4,3,2,1,0:T(8,128)(2,1)S(1)} %pad_maximum_fusion.3), channel_id=1, source_target_pairs={{0,2},{1,3},{2,0},{3,1},{4,6},{5,7},{6,4},{7,5},{8,10},{9,11},{10,... | collective-permute-start | bytes 1572872 | tf_op jit(solution)/shard_map/ppermute | solution.py:399
  83.5 13.3 %collective-permute-start.16 = (bf16[256,1024]{1,0:T(8,128)(2,1)S(1)}, bf16[256,1024]{1,0:T(8,128)(2,1)S(1)}, u32[]{:S(2)}, u32[]{:S(2)}) collective-permute-start(bf16[256,1024]{1,0:T(8,128)(2,1)S(1)} %collective-permute-done.12.refs_0_), channel_id=1, source_target_pairs={{0,8},{8,0},{16,24},{24,16},{32,40},{40,32},{48,56},{56,48},{64,72... | collective-permute-start | bytes 1572872 | tf_op jit(solution)/shard_map/ppermute | solution.py:399
  83.5 13.3 %collective-permute-start.17 = (bf16[256,1024]{1,0:T(8,128)(2,1)S(1)}, bf16[256,1024]{1,0:T(8,128)(2,1)S(1)}, u32[]{:S(2)}, u32[]{:S(2)}) collective-permute-start(bf16[256,1024]{1,0:T(8,128)(2,1)S(1)} %collective-permute-done.13.refs_1_), channel_id=1, source_target_pairs={{0,8},{8,0},{16,24},{24,16},{32,40},{40,32},{48,56},{56,48},{64,72... | collective-permute-start | bytes 1572872 | tf_op jit(solution)/shard_map/ppermute | solution.py:399
  86.2 10.5 %collective-permute-start.15 = (bf16[128,1024]{1,0:T(8,128)(2,1)S(1)}, bf16[128,1024]{1,0:T(8,128)(2,1)S(1)}, u32[]{:S(2)}, u32[]{:S(2)}) collective-permute-start(bf16[128,1024]{1,0:T(8,128)(2,1)S(1)} %slice_select_fusion), channel_id=1, source_target_pairs={{0,16},{16,32},{32,48},{48,64},{64,80},{80,96},{96,112},{112,0},{8... | collective-permute-start | bytes 786440 | tf_op jit(solution)/shard_map/ppermute | solution.py:420
  88.2 10.0 %collective-permute-start.18 = (bf16[256,1024]{1,0:T(8,128)(2,1)S(1)}, bf16[256,1024]{1,0:T(8,128)(2,1)S(1)}, u32[]{:S(2)}, u32[]{:S(2)}) collective-permute-start(bf16[256,1024]{1,0:T(8,128)(2,1)S(1)} %collective-permute-done.14.refs_2_), channel_id=1, source_target_pairs={{0,8},{8,0},{16,24},{24,16},{32,40},{40,32},{48,56},{56,48},{64,72... | collective-permute-start | bytes 1572872 | tf_op jit(solution)/shard_map/ppermute | solution.py:399
  96.4 12.4 %collective-permute-start.2 = (bf16[2,1,2,16,4096]{4,3,2,1,0:T(8,128)(2,1)S(1)}, bf16[2,1,2,16,4096]{4,3,2,1,0:T(8,128)(2,1)S(1)}, u32[]{:S(2)}, u32[]{:S(2)}) collective-permute-start(bf16[2,1,2,16,4096]{4,3,2,1,0:T(8,128)(2,1)S(1)} %pad_maximum_fusion.2), channel_id=1, source_target_pairs={{0,2},{1,3},{2,0},{3,1},{4,6},{5,7},{6,4},{7,5},{8,10},{9,11},{10,... | collective-permute-start | bytes 1572872 | tf_op jit(solution)/shard_map/ppermute | solution.py:399
  96.7 1.5 collective-permute-start.19
  100.2 52.7 %collective-permute-start.20 = (bf16[256,1024]{1,0:T(8,128)(2,1)S(1)}, bf16[256,1024]{1,0:T(8,128)(2,1)}, u32[]{:S(2)}, u32[]{:S(2)}) collective-permute-start(bf16[256,1024]{1,0:T(8,128)(2,1)S(1)} %shard_map.258), channel_id=1, source_target_pairs={{0,128},{128,0},{1,129},{129,1},{2,130},{130,2},{3,131},{131,3},{4... | collective-permute-start | bytes 1572872 | tf_op jit(solution)/shard_map/ppermute | solution.py:399
  131.2 1.3 collective-permute-start.3
  132.5 3.9 %collective-permute-start.4 = (f32[56,128]{1,0:T(8,128)S(1)}, f32[56,128]{1,0:T(8,128)S(1)}, u32[]{:S(2)}, u32[]{:S(2)}) collective-permute-start(f32[56,128]{1,0:T(8,128)S(1)} %add.24), channel_id=1, source_target_pairs={{0,128},{128,0},{1,129},{129,1},{2,130},{130,2},{3,131},{131,3},{4... | collective-permute-start | bytes 86024 | tf_op jit(solution)/shard_map/ppermute | solution.py:399
  136.4 3.9 %collective-permute-start.5 = (f32[56,128]{1,0:T(8,128)S(1)}, f32[56,128]{1,0:T(8,128)S(1)}, u32[]{:S(2)}, u32[]{:S(2)}) collective-permute-start(f32[56,128]{1,0:T(8,128)S(1)} %add.25), channel_id=1, source_target_pairs={{0,16},{8,24},{16,0},{24,8},{32,48},{40,56},{48,32},{56,40},{64,80... | collective-permute-start | bytes 86024 | tf_op jit(solution)/shard_map/ppermute | solution.py:399
  140.2 4.8 %collective-permute-start.6 = (f32[56,128]{1,0:T(8,128)S(1)}, f32[56,128]{1,0:T(8,128)S(1)}, u32[]{:S(2)}, u32[]{:S(2)}) collective-permute-start(f32[56,128]{1,0:T(8,128)S(1)} %add.26), channel_id=1, source_target_pairs={{0,32},{8,40},{16,48},{24,56},{32,0},{40,8},{48,16},{56,24},{64,96... | collective-permute-start | bytes 86024 | tf_op jit(solution)/shard_map/ppermute | solution.py:399
  145.1 7.8 %collective-permute-start.7 = (f32[56,128]{1,0:T(8,128)S(1)}, f32[56,128]{1,0:T(8,128)S(1)}, u32[]{:S(2)}, u32[]{:S(2)}) collective-permute-start(f32[56,128]{1,0:T(8,128)S(1)} %add.27), channel_id=1, source_target_pairs={{0,64},{8,72},{16,80},{24,88},{32,96},{40,104},{48,112},{56,120},{... | collective-permute-start | bytes 86024 | tf_op jit(solution)/shard_map/ppermute | solution.py:399
  (21 other events, 575.8 us)
Sparse Core Ops, SparseCore 0:
  9.8 69.9 all-gather.1

commit v3 on v1

--- a/solution.py
+++ b/solution.py
@@ -11,7 +11,9 @@
 EPS = 1e-05
 F32 = jnp.float32
 BF16 = jnp.bfloat16
-VMEM_LIMIT = 48 * 1024 * 1024
+VMEM_LIMIT = 56 * 1024 * 1024
+SHARDS = 16
+PIECES = ((0, 0), (0, 1), (3, 0), (3, 1), (1, 0), (1, 1), (2, 0), (2, 1))
 
 
 def split2(value):
@@ -106,11 +108,51 @@
     return jnp.concatenate([jnp.where(left, value, zero), jnp.where(left, zero, value)], axis=0)
 
 
+def picked(dims, half):
+    axis = len(dims) - 4 if len(dims) > 3 else 0
+    span = dims[axis] // 2
+    return (slice(None),) * axis + (pl.ds(half * span, span),), (*dims[:axis], span, *dims[axis + 1 :])
+
+
+def staged(kernel, count, half):
+    def run(meta_ref, *refs):
+        inputs, rest = refs[:count], refs[count:]
+        outputs, held, sems = rest[: -count - 1], rest[-count - 1 : -1], rest[-1]
+        copies = []
+        for i, (source, target) in enumerate(zip(inputs, held)):
+            if half is not None:
+                source = source.at[picked(source.shape, half)[0]]
+            copies.append(pltpu.make_async_copy(source, target, sems.at[i]))
+        for copy in copies:
+            copy.start()
+        if half is not None:
+            kernel(meta_ref, copies, *held, *outputs)
+        else:
+            wait(copies)
+            kernel(meta_ref, *held, *outputs)
+
+    return run
+
+
+def wait(copies):
+    for copy in copies:
+        copy.wait()
+
+
+def place_pieces(meta_ref, refs, target):
+    near, up, down, far0, far1 = refs
+    pieces = [near.at[0], near.at[1], up.at[0], up.at[1], down.at[0], down.at[1], far0, far1]
+    along, across = meta_ref[1], meta_ref[2]
+    for piece, (far_x, far_y) in zip(pieces, PIECES):
+        index = lax.rem(along + far_x, 4) * 2 + lax.bitwise_xor(across, far_y)
+        target[:, :, pl.ds(pl.multiple_of(index * 16, 16), 16), :] = piece[...]
+
+
 def forward_kernel(
     count_ref, z_ref, x_ref, b_ref, c_ref, dt_ref, seg_ref, cx_ref, cb_ref, cc_ref, al_ref, bias_ref, skip_ref, gain_ref,
     norm_ref, xc_ref, dsx_ref, ssm_ref, gate_ref, dgate_ref, bcc_ref, small_ref, cumt_ref, rms_ref,
 ):
-    heads = dt_ref.shape[1]
+    heads = dt_ref.shape[0]
     tiles = x_ref.shape[1] // LANES
     seg_rows, seg_cols, masks = shift_masks(seg_ref[...])
     rows, cols = iota(0), iota(1)
@@ -125,7 +167,7 @@
     scores = dot_nt(c_conv, b_conv)
     bcc_ref[4] = scores.T
 
-    raw = dt_ref[...].astype(F32) + bias_ref[...]
+    raw = dt_ref[...].astype(F32).T + bias_ref[...]
     step = jnp.maximum(raw, 0.0) + jnp.log1p(jnp.exp(-jnp.abs(raw)))
     decay = -jnp.exp(al_ref[...]) * step
     lower = jnp.where(rows >= cols, 1.0, 0.0).astype(BF16)
@@ -172,7 +214,47 @@
         norm_ref[:, span] = (normed * alive).astype(BF16)
 
 
-def backward_kernel(
+def upstream_kernel(meta_ref, copies, near, up, down, far0, far1, *refs):
+    *weights, own_ref, other_ref, rows_ref, sum_ref = refs
+    wait(copies[:5])
+    place_pieces(meta_ref, (near, up, down, far0, far1), rows_ref)
+    order = ring_order(meta_ref)
+    for i in range(0, len(weights), 2):
+        wait(copies[5 + i : 7 + i])
+        left = [
+            jnp.concatenate([rows_ref[who, order[i]], rows_ref[who, order[i + 1]]], axis=1) for who in range(2)
+        ]
+        product = jnp.dot(
+            jnp.concatenate(left, axis=0),
+            jnp.concatenate([weights[i][...], weights[i + 1][...]], axis=0),
+            preferred_element_type=F32,
+        )
+        sum_ref[...] = product if i == 0 else sum_ref[...] + product
+    length = own_ref.shape[0]
+    own_ref[...] = sum_ref[:length, :]
+    other_ref[...] = sum_ref[length:, :].astype(BF16)
+
+
+def backward_kernel(meta_ref, own_ref, other_ref, *refs):
+    *rest, up_ref = refs
+    up_ref[...] = own_ref[...] + other_ref[...].astype(F32)
+    pull_back(meta_ref, up_ref, *rest)
+
+
+def ring_order(meta_ref):
+    chip, core = meta_ref[3], meta_ref[4]
+    other = 1 - core
+    toward = 1 - 2 * core
+    order = [2 * chip + core, 2 * chip + other]
+    for k in (1, 2, 3):
+        back = 2 * lax.rem(chip - toward * k + 8, 8)
+        ahead = 2 * lax.rem(chip + toward * k + 8, 8)
+        order += [back + core, back + other, ahead + other, ahead + core]
+    far = 2 * lax.rem(chip + 4, 8)
+    return order + [far + core, far + other]
+
+
+def pull_back(
     count_ref, up_ref, x_ref, b_ref, c_ref, seg_ref, cx_ref, cb_ref, cc_ref, al_ref, skip_ref, gain_ref,
     xc_ref, dsx_ref, ssm_ref, gate_ref, dgate_ref, bcc_ref, small_ref, cumt_ref, rms_ref,
     gz_ref, gx_ref, gb_ref, gc_ref, gdt_ref, par_ref,
@@ -265,7 +347,7 @@
     d_decay = sums[:, 0:heads]
     d_step = sums[:, heads : 2 * heads] - jnp.exp(al_ref[...]) * d_decay
     d_raw = d_step * slope
-    gdt_ref[...] = d_raw.astype(BF16)
+    gdt_ref[...] = d_raw.T.astype(BF16)
     par_ref[48:49, 0:heads] = jnp.sum(d_decay * decay, axis=0, keepdims=True)
     par_ref[49:50, 0:heads] = jnp.sum(d_raw, axis=0, keepdims=True)
     par_ref[50:51, 0:heads] = jnp.sum(sums[:, 2 * heads : 3 * heads], axis=0, keepdims=True)
@@ -303,24 +385,54 @@
     skip_ref[...] = total[50:51, 0:heads]
 
 
-def call(kernel, operands, outs, flops, smem_first=True):
-    vmem = pl.BlockSpec(memory_space=pltpu.VMEM)
-    specs = [vmem] * len(operands)
-    if smem_first:
-        specs[0] = pl.BlockSpec(memory_space=pltpu.SMEM)
+def weight_kernel(meta_ref, copies, near, up, down, far0, far1, *refs):
+    *blocks, out_ref, col_ref = refs
+    wait(copies[:5])
+    place_pieces(meta_ref, (near, up, down, far0, far1), col_ref)
+    order = ring_order(meta_ref)
+    total = None
+    for i in range(0, len(blocks), 2):
+        wait(copies[5 + i : 7 + i])
+        product = lax.dot_general(
+            jnp.concatenate(
+                [jnp.concatenate([col_ref[0, k], col_ref[1, k]], axis=1) for k in order[i : i + 2]], axis=0
+            ),
+            jnp.concatenate([blocks[i][...], blocks[i + 1][...]], axis=0),
+            (((0,), (0,)), ((), ())),
+            preferred_element_type=F32,
+        )
+        total = product if i == 0 else total + product
+    out_ref[...] = total.astype(out_ref.dtype)
+
+
+def call(kernel, operands, outs, flops, scratch=(), half=None):
+    others = operands[1:]
     size = sum(a.size * a.dtype.itemsize for a in operands) + sum(
         a.size * a.dtype.itemsize for a in outs
     )
+    held = [a.shape if half is None else picked(a.shape, half)[1] for a in others]
     return pl.pallas_call(
-        kernel,
+        staged(kernel, len(others), half),
         out_shape=outs,
-        in_specs=specs,
-        out_specs=[vmem] * len(outs),
+        in_specs=[pl.BlockSpec(memory_space=pltpu.SMEM)] + [pl.BlockSpec(memory_space=pl.ANY)] * len(others),
+        out_specs=[pl.BlockSpec(memory_space=pltpu.VMEM)] * len(outs),
+        scratch_shapes=[
+            *scratch,
+            *[pltpu.VMEM(dims, a.dtype) for dims, a in zip(held, others)],
+            pltpu.SemaphoreType.DMA((len(others),)),
+        ],
         compiler_params=pltpu.CompilerParams(vmem_limit_bytes=VMEM_LIMIT),
         cost_estimate=pl.CostEstimate(flops=flops, bytes_accessed=size, transcendentals=0),
     )(*operands)
 
 
+def unpack(packed, outs):
+    vmem = pl.BlockSpec(memory_space=pltpu.VMEM)
+    return pl.pallas_call(
+        unpack_kernel, out_shape=outs, in_specs=[vmem], out_specs=[vmem] * len(outs)
+    )(packed)
+
+
 def shape(dims, dtype=F32):
     return jax.ShapeDtypeStruct(dims, dtype)
 
@@ -329,16 +441,24 @@
     return lax.ppermute(value, axis, [(i, i ^ bit) for i in range(size)])
 
 
-def gather_tensor(block, axis):
-    me = lax.axis_index("tensor")
-    held = jnp.expand_dims(block, axis)
-    for bit in (1, 2, 4):
-        other = swap(held, "tensor", bit, 8)
-        first = (me & bit) == 0
-        held = jnp.concatenate(
-            [jnp.where(first, held, other), jnp.where(first, other, held)], axis=axis
-        )
-    return held
+def along_x(value, by):
+    return lax.ppermute(value, "tensor", [(i, (i + 2 * by) % 8) for i in range(8)])
+
+
+def gather_near(block):
+    return jnp.stack([block, swap(block, "tensor", 1, 8)])
+
+
+def gather_next(near):
+    return along_x(near, 1), along_x(near, -1)
+
+
+def gather_far(up, down):
+    return along_x(up[0], 1), along_x(down[1], -1)
+
+
+def tie(*values):
+    return lax.optimization_barrier(values)
 
 
 def body(
@@ -347,61 +467,107 @@
 ):
     length, width = z_act.shape
     heads = dt_act.shape[1]
-    features = d_out.shape[1]
+    own, features = d_out.shape
     dp = lax.axis_size("dp")
+    shard = lax.axis_index("dp")
+    place = lax.axis_index("tensor")
+    core = lax.bitwise_and(shard, 1)
+    meta = jnp.stack(
+        [counts[0], lax.shift_right_logical(place, 1), lax.bitwise_and(place, 1), lax.shift_right_logical(shard, 1), core]
+    )
+    chips = dp // 2
+    ring = [(2 * z, 2 * ((z + 1) % chips)) for z in range(chips)]
+    ring += [(2 * z + 1, 2 * ((z - 1) % chips) + 1) for z in range(chips)]
     seg_row = segment.reshape(1, length)
     a_log, dt_bias, d_skip = (v.reshape(1, heads) for v in (a_log, dt_bias, d_skip))
     gain = norm_gain.reshape(1, width)
-
-    w_all = lax.all_gather(w_out, "dp", axis=0, tiled=True)
-
-    own = d_out.shape[0]
-    rows = gather_tensor(d_out, 0).reshape(length, features)
-    pieces = d_out.reshape(own, dp, features // dp).transpose(1, 0, 2)
-    pieces = lax.all_to_all(pieces, "dp", 0, 0, tiled=False)
-    columns = gather_tensor(pieces, 1).reshape(dp * length, features // dp)
+    replica = lax.axis_index("rep")
+    lower = replica == 0
+    half = w_out.shape[0] // 2
+    w_half = jnp.where(lower, w_out[:half], w_out[half:])
+    pieces = d_out.reshape(own, dp, 2, half).transpose(2, 1, 0, 3)
+    theirs = swap(jnp.where(lower, pieces[1], pieces[0]), "rep", 1, 2)
+    mine = jnp.where(lower, pieces[0], pieces[1])
+    turned = lax.all_to_all(pieces, "dp", 1, 1, tiled=False)
+    pieces = jnp.concatenate([mine[None], theirs[None], turned], axis=0)
+
+    def step(value):
+        return lax.ppermute(value, "dp", ring)
+
+    def across(*values):
+        return [swap(value, "dp", 1, dp) for value in values]
 
     wide = shape((length, width))
     normed, *saved = call(
         forward_kernel,
-        (counts, z_act, x_act, b_act, c_act, dt_act, seg_row, conv_x, conv_b, conv_c, a_log, dt_bias, d_skip, gain),
+        (meta, z_act, x_act, b_act, c_act, dt_act.T, seg_row, conv_x, conv_b, conv_c, a_log, dt_bias, d_skip, gain),
         [
             shape((length, width), BF16), wide, wide, wide, wide, wide,
             shape((5, LANES, LANES)), shape((4, length, heads)), shape((heads, length)), shape((LANES, LANES)),
         ],
-        300_000_000,
-    )
-    normed_all = lax.all_gather(normed, "dp", axis=0, tiled=True)
-
-    upstream = jnp.dot(rows, w_all, preferred_element_type=F32)
+        5_000_000_000,
+    )
+    one = jnp.concatenate([w_half, normed], axis=0)
+    (two,) = across(one)
+    blocks = [one, two]
+    one, two = step(one), step(two)
+    near = gather_near(pieces)
+
+    blocks += [one, two, *across(one, two)]
+    one, two = step(one), step(two)
+    up, down = gather_next(near)
+
+    blocks += [one, two, *across(one, two)]
+    one, two = step(one), step(two)
+    far = gather_far(up, down)
+    blocks += [one, two, *across(one, two)]
+    one = step(one)
+    blocks += [one, *across(one)]
+
+    upstream, other = call(
+        upstream_kernel,
+        (meta, near, up, down, *far, *blocks),
+        [shape((length, width)), shape((length, width), BF16)],
+        4_000_000_000,
+        half=0,
+        scratch=[pltpu.VMEM((2, dp, length, half), BF16), pltpu.VMEM((2 * length, width), F32)],
+    )
+    other = swap(other, "rep", 1, 2)
     *act_grads, packed = call(
         backward_kernel,
-        (counts, upstream, x_act, b_act, c_act, seg_row, conv_x, conv_b, conv_c, a_log, d_skip, gain, *saved),
+        (
+            meta, upstream, other,
+            x_act, b_act, c_act, seg_row, conv_x, conv_b, conv_c, a_log, d_skip, gain, *saved,
+        ),
         [
             shape((length, width), BF16), shape((length, width), BF16), shape((length, LANES), BF16),
-            shape((length, LANES), BF16), shape((length, heads), BF16), shape((56, LANES)),
+            shape((length, LANES), BF16), shape((heads, length), BF16), shape((56, LANES)),
         ],
-        600_000_000,
-    )
-    packed = packed + swap(packed, "dp", 1, dp)
+        10_000_000_000,
+        scratch=[pltpu.VMEM((length, width), F32)],
+    )
+    act_grads[4] = act_grads[4].T
+    share = call(
+        weight_kernel,
+        (meta, near, up, down, *far, *blocks),
+        [shape((features // dp, width), BF16)],
+        5_000_000_000,
+        half=1,
+        scratch=[pltpu.VMEM((2, dp, length, half), BF16)],
+    )[0]
+    weight_grad = share.astype(F32) + swap(share, "rep", 1, 2).astype(F32)
+    for bit in (1, 2, 4):
+        packed = packed + swap(packed, "dp", bit, dp)
     packed = packed + swap(packed, "rep", 1, 2)
-    for bit in (2, 4, 8):
-        packed = packed + swap(packed, "dp", bit, dp)
-    sums = call(
-        unpack_kernel,
-        (packed,),
+    packed = packed + swap(packed, "dp", 8, dp)
+    sums = unpack(
+        packed,
         [
             shape(conv_x.shape), shape(conv_b.shape), shape(conv_c.shape),
             shape((1, heads)), shape((1, heads)), shape((1, heads)), shape((1, width)),
         ],
-        1000,
-        smem_first=False,
-    )
-
-    share = lax.dot_general(
-        columns, normed_all, (((0,), (0,)), ((), ())), preferred_element_type=F32
-    ).astype(BF16)
-    weight_grad = share.astype(F32) + swap(share, "rep", 1, 2).astype(F32)
+    )
+
     return (
         *act_grads,
         sums[0], sums[1], sums[2],

time: 165 us -> 122 us (0.74)
  waiting for transfers between devices: 81.5 us -> 54.3 us
  Pallas kernels: 8.06 us -> 24.1 us
  between operations: 15 us -> 1.72 us
  local copies, waits for them, and re-layouts: 14.1 us -> 3.08 us
  matrix products: 9.76 us -> 0 us
  starting transfers between devices: 24.7 us -> 32.3 us
  other arithmetic: 11.5 us -> 4.75 us
    all_gather x2 -> x0, waiting for transfers between devices: 31.3 us -> none  [the longest x1 31.3 us: body(): w_all = lax.all_gather(w_out, 'dp', axis=0, tiled=True)]
    ppermute x0 -> x11, waiting for transfers between devices: none -> 23.5 us  [the longest x4 17.4 us: along_x(): lax.ppermute(value, 'tensor', [(i, (i + 2 * by) % 8) for i in range(8)])]
    pallas_call x3 -> x5, Pallas kernels: 8.06 us -> 24.1 us  [the longest x4 22.7 us: call(): pl.pallas_call(staged(kernel, len(others), half), out_shape=outs, in_spec...]
    ppermute x12 -> x17, waiting for transfers between devices: 40.4 us -> 27.1 us  [swap(): return lax.ppermute(value, axis, [(i, i ^ bit) for i in range(size)])]
    unnamed x63 -> x48, local copies, waits for them, and re-layouts: 13.4 us -> 1.61 us
    ppermute x0 -> x11, starting transfers between devices: none -> 11.1 us  [the longest x7 6.06 us: step(): return lax.ppermute(value, 'dp', ring)]
    dot_general x2 -> x0, matrix products: 9.76 us -> none  [the longest x1 5.03 us: body(): upstream = jnp.dot(rows, w_all, preferred_element_type=F32)]
    all_to_all x1, waiting for transfers between devices: 9.12 us -> 3.59 us  [body(): turned = lax.all_to_all(pieces, 'dp', 1, 1, tiled=False)]
  transfers between devices with their start and end apart: 15 -> 29, of which waited for: 11 -> 15; matrix products, arithmetic and copies ran while one was open for 14% -> 2% of each run, Pallas kernels for 3% -> 12%
where the time goes in v3:
time: 122 us; the launch traced here: 120 us
  waiting for transfers between devices  54.3 us (45%)
  starting transfers between devices  32.3 us (26%)
  Pallas kernels  24.1 us (20%)
  other arithmetic  4.75 us (4%)
  local copies, waits for them, and re-layouts  3.08 us (3%)
  between operations  1.72 us (1%)
    ppermute x17, waiting for transfers between devices, swap(): return lax.ppermute(value, axis, [(i, i ^ bit) for i in range(size)])  27.1 us
    pallas_call x4, Pallas kernels, call(): pl.pallas_call(staged(kernel, len(others), half), out_shape=outs, in_spec...  22.7 us
    ppermute x4, waiting for transfers between devices, along_x(): lax.ppermute(value, 'tensor', [(i, (i + 2 * by) % 8) for i in range(8)])  17.4 us
    ppermute x17, starting transfers between devices, swap(): return lax.ppermute(value, axis, [(i, i ^ bit) for i in range(size)])  16.9 us
    ppermute x7, waiting for transfers between devices, step(): return lax.ppermute(value, 'dp', ring)  6.16 us
    ppermute x7, starting transfers between devices, step(): return lax.ppermute(value, 'dp', ring)  6.06 us
    ppermute x4, starting transfers between devices, along_x(): lax.ppermute(value, 'tensor', [(i, (i + 2 * by) % 8) for i in range(8)])  5.02 us
    all_to_all x1, starting transfers between devices, body(): turned = lax.all_to_all(pieces, 'dp', 1, 1, tiled=False)  4.29 us
  transfers between devices with their start and end apart: 29, of which 15 were waited for; matrix products, arithmetic and copies ran while one was open for 2% of the time, Pallas kernels for 12%

profile of v3, /device:TPU:2, one launch (start us, length us, event | category | flops | bytes accessed | tf_op | source)
XLA Modules:
  0.0 120.2 jit_solution(7848270189575355220)
XLA Ops:
  3.0 5.0 %shard_map.255 = (bf16[128,1024]{1,0:T(8,128)(2,1)}, f32[128,1024]{1,0:T(8,128)}, f32[128,1024]{1,0:T(8,128)}, f32[128,1024]{1,0:T(8,128)}, f32[128,1024]{1,0:T(...) custom-call(s32[5]{0:T(128)} %stack.28.meta_ref, ...), custom_call_target="tpu_custom_call" | custom-call | flops 5000000000 | bytes 3936980 | tf_op jit(solution)/shard_map/pallas_call | solution.py:414
  9.1 2.0 %collective-permute-start.7 = (bf16[256,1024]{1,0:T(8,128)(2,1)S(1)}, bf16[256,1024]{1,0:T(8,128)(2,1)S(1)}, u32[]{:S(2)}, u32[]{:S(2)}) collective-permute-start(bf16[256,1024]{1,0:T(8,128)(2,1)S(1)} %pad_maximum_fusion.1.refs_5_), channel_id=1, source_target_pairs={{0,16},{16,32},{32,48},{48,64},{64,80},{80,96},{96,112},{112,0},{8... | collective-permute-start | bytes 1572872 | tf_op jit(solution)/shard_map/ppermute | solution.py:495
  11.1 3.5 %collective-permute-start.6 = (bf16[256,1024]{1,0:T(8,128)(2,1)S(1)}, bf16[256,1024]{1,0:T(8,128)(2,1)S(1)}, u32[]{:S(2)}, u32[]{:S(2)}) collective-permute-start(bf16[256,1024]{1,0:T(8,128)(2,1)S(1)} %pad_maximum_fusion.1.refs_5_), channel_id=1, source_target_pairs={{0,8},{8,0},{16,24},{24,16},{32,40},{40,32},{48,56},{56,48},{64,72... | collective-permute-start | bytes 1572872 | tf_op jit(solution)/shard_map/ppermute | solution.py:441
  15.3 4.3 %all-to-all-start = ((bf16[2,16,16,128]{3,2,0,1:T(8,128)(2,1)}), bf16[2,16,16,128]{3,2,0,1:T(8,128)(2,1)S(1)}, u32[]{:S(2)}, u32[]{:S(2)}) async-start(bf16[2,16,16,128]{3,2,0,1:T(8,128)(2,1)} %bitcast.29), calls=%async_computation | async-start | bytes 262144 | tf_op jit(solution)/shard_map/all_to_all | solution.py:491
  19.7 1.7 %collective-permute-start = (bf16[16,16,128]{2,1,0:T(8,128)(2,1)S(1)}, bf16[16,16,128]{2,1,0:T(8,128)(2,1)S(1)}, u32[]{:S(2)}, u32[]{:S(2)}) collective-permute-start(bf16[16,16,128]{2,1,0:T(8,128)(2,1)S(1)} %get-tuple-element.66), channel_id=1, source_target_pairs={{0,128},{128,0},{1,129},{129,1},{2,130},{130,2},{3,131},{131,3},{4... | collective-permute-start | bytes 196616 | tf_op jit(solution)/shard_map/ppermute | solution.py:441
  24.8 3.6 %all-to-all-done = bf16[2,16,16,128]{3,2,0,1:T(8,128)(2,1)S(1)} async-done(((bf16[2,16,16,128]{3,2,0,1:T(8,128)(2,1)}), bf16[2,16,16,128]{3,2,0,1:T(8,128)(2,1)S(1)}, u32[]{:S(2)}, u32[]{:S(2)}) %all-to-all-start) | async-done | bytes 131104 | tf_op jit(solution)/shard_map/all_to_all | solution.py:491
  28.5 3.3 %collective-permute-start.1 = (bf16[4,16,16,128]{3,2,1,0:T(8,128)(2,1)S(1)}, bf16[4,16,16,128]{3,2,1,0:T(8,128)(2,1)S(1)}, u32[]{:S(2)}, u32[]{:S(2)}) collective-permute-start(bf16[4,16,16,128]{3,2,1,0:T(8,128)(2,1)S(1)} %get-tuple-element.64), channel_id=1, source_target_pairs={{0,1},{1,0},{2,3},{3,2},{4,5},{5,4},{6,7},{7,6},{8,9},{9,8},{10,11... | collective-permute-start | bytes 786440 | tf_op jit(solution)/shard_map/ppermute | solution.py:441
  31.7 7.4 %collective-permute-done.1 = bf16[4,16,16,128]{3,2,1,0:T(8,128)(2,1)S(1)} collective-permute-done((bf16[4,16,16,128]{3,2,1,0:T(8,128)(2,1)S(1)}, bf16[4,16,16,128]{3,2,1,0:T(8,128)(2,1)S(1)}, u32[]{:S(2)}, u32[]{:S(2)}) %collective-permute-start.1) | collective-permute-done | bytes 262176 | tf_op jit(solution)/shard_map/ppermute | solution.py:441
  42.5 10.6 %collective-permute-done.3.refs_2_ = bf16[2,4,16,16,128]{4,3,2,1,0:T(8,128)(2,1)S(1)} collective-permute-done((bf16[2,4,16,16,128]{4,3,2,1,0:T(8,128)(2,1)S(1)}, bf16[2,4,16,16,128]{4,3,2,1,0:T(8,128)(2,1)S(1)}, u32[]{:S(2)}, u32[]{:S(2)}) %collective-permute-start.3) | collective-permute-done | bytes 524320 | tf_op jit(solution)/shard_map/ppermute | solution.py:445
  53.4 2.4 %collective-permute-done.12.refs_12_ = bf16[256,1024]{1,0:T(8,128)(2,1)S(1)} collective-permute-done((bf16[256,1024]{1,0:T(8,128)(2,1)S(1)}, bf16[256,1024]{1,0:T(8,128)(2,1)S(1)}, u32[]{:S(2)}, u32[]{:S(2)}) %collective-permute-start.12) | collective-permute-done | bytes 524320 | tf_op jit(solution)/shard_map/ppermute | solution.py:495
  55.9 2.8 %collective-permute-start.5 = (bf16[4,16,16,128]{3,2,1,0:T(8,128)(2,1)S(1)}, bf16[4,16,16,128]{3,2,1,0:T(8,128)(2,1)S(1)}, u32[]{:S(2)}, u32[]{:S(2)}) collective-permute-start(bf16[4,16,16,128]{3,2,1,0:T(8,128)(2,1)S(1)} %slice_bitcast_fusion), channel_id=1, source_target_pairs={{0,6},{1,7},{2,0},{3,1},{4,2},{5,3},{6,4},{7,5},{8,14},{9,15},{10,... | collective-permute-start | bytes 786440 | tf_op jit(solution)/shard_map/ppermute | solution.py:445
  58.9 4.4 %collective-permute-done.5.refs_4_ = bf16[4,16,16,128]{3,2,1,0:T(8,128)(2,1)S(1)} collective-permute-done((bf16[4,16,16,128]{3,2,1,0:T(8,128)(2,1)S(1)}, bf16[4,16,16,128]{3,2,1,0:T(8,128)(2,1)S(1)}, u32[]{:S(2)}, u32[]{:S(2)}) %collective-permute-start.5) | collective-permute-done | bytes 262176 | tf_op jit(solution)/shard_map/ppermute | solution.py:445
  63.3 2.3 %collective-permute-done.4.refs_3_ = bf16[4,16,16,128]{3,2,1,0:T(8,128)(2,1)S(1)} collective-permute-done((bf16[4,16,16,128]{3,2,1,0:T(8,128)(2,1)S(1)}, bf16[4,16,16,128]{3,2,1,0:T(8,128)(2,1)S(1)}, u32[]{:S(2)}, u32[]{:S(2)}) %collective-permute-start.4) | collective-permute-done | bytes 262176 | tf_op jit(solution)/shard_map/ppermute | solution.py:445
  66.3 3.0 %collective-permute-done.16.refs_16_ = bf16[256,1024]{1,0:T(8,128)(2,1)S(1)} collective-permute-done((bf16[256,1024]{1,0:T(8,128)(2,1)S(1)}, bf16[256,1024]{1,0:T(8,128)(2,1)S(1)}, u32[]{:S(2)}, u32[]{:S(2)}) %collective-permute-start.16) | collective-permute-done | bytes 524320 | tf_op jit(solution)/shard_map/ppermute | solution.py:495
  69.3 1.8 %collective-permute-done.18.refs_18_ = bf16[256,1024]{1,0:T(8,128)(2,1)S(1)} collective-permute-done((bf16[256,1024]{1,0:T(8,128)(2,1)S(1)}, bf16[256,1024]{1,0:T(8,128)(2,1)S(1)}, u32[]{:S(2)}, u32[]{:S(2)}) %collective-permute-start.18) | collective-permute-done | bytes 524320 | tf_op jit(solution)/shard_map/ppermute | solution.py:441
  72.1 4.7 %shard_map.256 = (f32[128,1024]{1,0:T(8,128)}, bf16[128,1024]{1,0:T(8,128)(2,1)}) custom-call(s32[5]{0:T(128)} %stack.28.meta_ref, bf16[2,4,16,16,128]{4,3,2,1,0:T(8,128)(2,1)} %copy-done.1, bf16[2,4,16,16,128]{4,3,2,1,0:T(8,128)(2,1)} %copy-done.4, bf16[2,4,16,16,128]{4,3,2,1,0:T(8,128)(2,1)} %copy-done.3, bf16[4,16,16,128]{3,2,1,0:T(8,128)(2,1)} %copy-done.22, ...), custom_call_target="tpu_custom_call" | custom-call | flops 4000000000 | bytes 11272212 | tf_op jit(solution)/shard_map/pallas_call | solution.py:414
  78.4 4.9 %shard_map.259 = bf16[256,1024]{1,0:T(8,128)(2,1)} custom-call(s32[5]{0:T(128)} %stack.28.meta_ref, bf16[2,4,16,16,128]{4,3,2,1,0:T(8,128)(2,1)} %copy-done.1, bf16[2,4,16,16,128]{4,3,2,1,0:T(8,128)(2,1)} %copy-done.4, bf16[2,4,16,16,128]{4,3,2,1,0:T(8,128)(2,1)} %copy-done.3, bf16[4,16,16,128]{3,2,1,0:T(8,128)(2,1)} %copy-done.22, ...), custom_call_target="tpu_custom_call" | custom-call | flops 5000000000 | bytes 11010068 | tf_op jit(solution)/shard_map/pallas_call | solution.py:414
  86.1 8.1 %shard_map.257 = (bf16[128,1024]{1,0:T(8,128)(2,1)}, bf16[128,1024]{1,0:T(8,128)(2,1)}, bf16[128,128]{1,0:T(8,128)(2,1)}, bf16[128,128]{1,0:T(8,128)(2,1)}, bf16[16,128]{1,0:T(8,128)(2,1)}, /*index=5*/f32[56,128]{1,0:T(8,128)}) custom-call(s32[5]{0:T(128)} %stack.28.meta_ref, f32[128,1024]{1,0:T(8,128)} %get-tuple-element.39.refs_0_, ...), custom_call_target="tpu_custom_call" | custom-call | flops 10000000000 | bytes 4817556 | tf_op jit(solution)/shard_map/pallas_call | solution.py:414
  96.7 3.9 %collective-permute-done.23 = f32[56,128]{1,0:T(8,128)S(1)} collective-permute-done((f32[56,128]{1,0:T(8,128)S(1)}, f32[56,128]{1,0:T(8,128)S(1)}, u32[]{:S(2)}, u32[]{:S(2)}) %collective-permute-start.23) | collective-permute-done | bytes 28704 | tf_op jit(solution)/shard_map/ppermute | solution.py:441
  101.8 3.5 %collective-permute-done.24 = f32[56,128]{1,0:T(8,128)S(1)} collective-permute-done((f32[56,128]{1,0:T(8,128)S(1)}, f32[56,128]{1,0:T(8,128)S(1)}, u32[]{:S(2)}, u32[]{:S(2)}) %collective-permute-start.24) | collective-permute-done | bytes 28704 | tf_op jit(solution)/shard_map/ppermute | solution.py:441
  105.3 2.0 %collective-permute-start.25 = (f32[56,128]{1,0:T(8,128)S(1)}, f32[56,128]{1,0:T(8,128)S(1)}, u32[]{:S(2)}, u32[]{:S(2)}) collective-permute-start(f32[56,128]{1,0:T(8,128)S(1)} %add.20), channel_id=1, source_target_pairs={{0,128},{128,0},{1,129},{129,1},{2,130},{130,2},{3,131},{131,3},{4... | collective-permute-start | bytes 86024 | tf_op jit(solution)/shard_map/ppermute | solution.py:441
  107.3 1.9 %collective-permute-done.25 = f32[56,128]{1,0:T(8,128)S(1)} collective-permute-done((f32[56,128]{1,0:T(8,128)S(1)}, f32[56,128]{1,0:T(8,128)S(1)}, u32[]{:S(2)}, u32[]{:S(2)}) %collective-permute-start.25) | collective-permute-done | bytes 28704 | tf_op jit(solution)/shard_map/ppermute | solution.py:441
  109.2 2.1 %collective-permute-start.26 = (f32[56,128]{1,0:T(8,128)S(1)}, f32[56,128]{1,0:T(8,128)S(1)}, u32[]{:S(2)}, u32[]{:S(2)}) collective-permute-start(f32[56,128]{1,0:T(8,128)S(1)} %add.21), channel_id=1, source_target_pairs={{0,64},{8,72},{16,80},{24,88},{32,96},{40,104},{48,112},{56,120},{... | collective-permute-start | bytes 86024 | tf_op jit(solution)/shard_map/ppermute | solution.py:441
  111.4 5.6 %collective-permute-done.26 = f32[56,128]{1,0:T(8,128)S(1)} collective-permute-done((f32[56,128]{1,0:T(8,128)S(1)}, f32[56,128]{1,0:T(8,128)S(1)}, u32[]{:S(2)}, u32[]{:S(2)}) %collective-permute-start.26) | collective-permute-done | bytes 28704 | tf_op jit(solution)/shard_map/ppermute | solution.py:441
  (104 shorter events, 23.6 us)
Async XLA Ops:
  9.1 13.1 %collective-permute-start.7 = (bf16[256,1024]{1,0:T(8,128)(2,1)S(1)}, bf16[256,1024]{1,0:T(8,128)(2,1)S(1)}, u32[]{:S(2)}, u32[]{:S(2)}) collective-permute-start(bf16[256,1024]{1,0:T(8,128)(2,1)S(1)} %pad_maximum_fusion.1.refs_5_), channel_id=1, source_target_pairs={{0,16},{16,32},{32,48},{48,64},{64,80},{80,96},{96,112},{112,0},{8... | collective-permute-start | bytes 1572872 | tf_op jit(solution)/shard_map/ppermute | solution.py:495
  11.1 12.3 %collective-permute-start.6 = (bf16[256,1024]{1,0:T(8,128)(2,1)S(1)}, bf16[256,1024]{1,0:T(8,128)(2,1)S(1)}, u32[]{:S(2)}, u32[]{:S(2)}) collective-permute-start(bf16[256,1024]{1,0:T(8,128)(2,1)S(1)} %pad_maximum_fusion.1.refs_5_), channel_id=1, source_target_pairs={{0,8},{8,0},{16,24},{24,16},{32,40},{40,32},{48,56},{56,48},{64,72... | collective-permute-start | bytes 1572872 | tf_op jit(solution)/shard_map/ppermute | solution.py:441
  15.3 13.0 %all-to-all-start = ((bf16[2,16,16,128]{3,2,0,1:T(8,128)(2,1)}), bf16[2,16,16,128]{3,2,0,1:T(8,128)(2,1)S(1)}, u32[]{:S(2)}, u32[]{:S(2)}) async-start(bf16[2,16,16,128]{3,2,0,1:T(8,128)(2,1)} %bitcast.29), calls=%async_computation | async-start | bytes 262144 | tf_op jit(solution)/shard_map/all_to_all | solution.py:491
  19.7 5.1 %collective-permute-start = (bf16[16,16,128]{2,1,0:T(8,128)(2,1)S(1)}, bf16[16,16,128]{2,1,0:T(8,128)(2,1)S(1)}, u32[]{:S(2)}, u32[]{:S(2)}) collective-permute-start(bf16[16,16,128]{2,1,0:T(8,128)(2,1)S(1)} %get-tuple-element.66), channel_id=1, source_target_pairs={{0,128},{128,0},{1,129},{129,1},{2,130},{130,2},{3,131},{131,3},{4... | collective-permute-start | bytes 196616 | tf_op jit(solution)/shard_map/ppermute | solution.py:441
  22.2 17.6 %collective-permute-start.11 = (bf16[256,1024]{1,0:T(8,128)(2,1)S(1)}, bf16[256,1024]{1,0:T(8,128)(2,1)S(1)}, u32[]{:S(2)}, u32[]{:S(2)}) collective-permute-start(bf16[256,1024]{1,0:T(8,128)(2,1)S(1)} %collective-permute-done.7.refs_7_), channel_id=1, source_target_pairs={{0,16},{16,32},{32,48},{48,64},{64,80},{80,96},{96,112},{112,0},{8... | collective-permute-start | bytes 1572872 | tf_op jit(solution)/shard_map/ppermute | solution.py:495
  23.3 16.8 %collective-permute-start.8 = (bf16[256,1024]{1,0:T(8,128)(2,1)S(1)}, bf16[256,1024]{1,0:T(8,128)(2,1)S(1)}, u32[]{:S(2)}, u32[]{:S(2)}) collective-permute-start(bf16[256,1024]{1,0:T(8,128)(2,1)S(1)} %collective-permute-done.6.refs_6_), channel_id=1, source_target_pairs={{0,16},{16,32},{32,48},{48,64},{64,80},{80,96},{96,112},{112,0},{8... | collective-permute-start | bytes 1572872 | tf_op jit(solution)/shard_map/ppermute | solution.py:495
  28.5 10.7 %collective-permute-start.1 = (bf16[4,16,16,128]{3,2,1,0:T(8,128)(2,1)S(1)}, bf16[4,16,16,128]{3,2,1,0:T(8,128)(2,1)S(1)}, u32[]{:S(2)}, u32[]{:S(2)}) collective-permute-start(bf16[4,16,16,128]{3,2,1,0:T(8,128)(2,1)S(1)} %get-tuple-element.64), channel_id=1, source_target_pairs={{0,1},{1,0},{2,3},{3,2},{4,5},{5,4},{6,7},{7,6},{8,9},{9,8},{10,11... | collective-permute-start | bytes 786440 | tf_op jit(solution)/shard_map/ppermute | solution.py:441
  39.2 13.9 %collective-permute-start.3 = (bf16[2,4,16,16,128]{4,3,2,1,0:T(8,128)(2,1)S(1)}, bf16[2,4,16,16,128]{4,3,2,1,0:T(8,128)(2,1)S(1)}, u32[]{:S(2)}, u32[]{:S(2)}) collective-permute-start(bf16[2,4,16,16,128]{4,3,2,1,0:T(8,128)(2,1)S(1)} %pad_maximum_fusion.refs_0_), channel_id=1, source_target_pairs={{0,6},{1,7},{2,0},{3,1},{4,2},{5,3},{6,4},{7,5},{8,14},{9,15},{10,... | collective-permute-start | bytes 1572872 | tf_op jit(solution)/shard_map/ppermute | solution.py:445
  39.8 13.3 %collective-permute-start.15 = (bf16[256,1024]{1,0:T(8,128)(2,1)S(1)}, bf16[256,1024]{1,0:T(8,128)(2,1)S(1)}, u32[]{:S(2)}, u32[]{:S(2)}) collective-permute-start(bf16[256,1024]{1,0:T(8,128)(2,1)S(1)} %collective-permute-done.11.refs_11_), channel_id=1, source_target_pairs={{0,16},{16,32},{32,48},{48,64},{64,80},{80,96},{96,112},{112,0},{8... | collective-permute-start | bytes 1572872 | tf_op jit(solution)/shard_map/ppermute | solution.py:495
  40.1 15.7 %collective-permute-start.12 = (bf16[256,1024]{1,0:T(8,128)(2,1)S(1)}, bf16[256,1024]{1,0:T(8,128)(2,1)S(1)}, u32[]{:S(2)}, u32[]{:S(2)}) collective-permute-start(bf16[256,1024]{1,0:T(8,128)(2,1)S(1)} %collective-permute-done.8.refs_8_), channel_id=1, source_target_pairs={{0,16},{16,32},{32,48},{48,64},{64,80},{80,96},{96,112},{112,0},{8... | collective-permute-start | bytes 1572872 | tf_op jit(solution)/shard_map/ppermute | solution.py:495
  41.0 14.9 %collective-permute-start.2 = (bf16[2,4,16,16,128]{4,3,2,1,0:T(8,128)(2,1)S(1)}, bf16[2,4,16,16,128]{4,3,2,1,0:T(8,128)(2,1)S(1)}, u32[]{:S(2)}, u32[]{:S(2)}) collective-permute-start(bf16[2,4,16,16,128]{4,3,2,1,0:T(8,128)(2,1)S(1)} %pad_maximum_fusion.refs_0_), channel_id=1, source_target_pairs={{0,2},{1,3},{2,4},{3,5},{4,6},{5,7},{6,0},{7,1},{8,10},{9,11},{10,... | collective-permute-start | bytes 1572872 | tf_op jit(solution)/shard_map/ppermute | solution.py:445
  42.5 16.3 %collective-permute-start.9 = (bf16[256,1024]{1,0:T(8,128)(2,1)S(1)}, bf16[256,1024]{1,0:T(8,128)(2,1)S(1)}, u32[]{:S(2)}, u32[]{:S(2)}) collective-permute-start(bf16[256,1024]{1,0:T(8,128)(2,1)S(1)} %collective-permute-done.7.refs_7_), channel_id=1, source_target_pairs={{0,8},{8,0},{16,24},{24,16},{32,40},{40,32},{48,56},{56,48},{64,72... | collective-permute-start | bytes 1572872 | tf_op jit(solution)/shard_map/ppermute | solution.py:441
  53.1 12.5 %collective-permute-start.13 = (bf16[256,1024]{1,0:T(8,128)(2,1)S(1)}, bf16[256,1024]{1,0:T(8,128)(2,1)S(1)}, u32[]{:S(2)}, u32[]{:S(2)}) collective-permute-start(bf16[256,1024]{1,0:T(8,128)(2,1)S(1)} %collective-permute-done.11.refs_11_), channel_id=1, source_target_pairs={{0,8},{8,0},{16,24},{24,16},{32,40},{40,32},{48,56},{56,48},{64,72... | collective-permute-start | bytes 1572872 | tf_op jit(solution)/shard_map/ppermute | solution.py:441
  53.1 13.0 %collective-permute-start.19 = (bf16[256,1024]{1,0:T(8,128)(2,1)S(1)}, bf16[256,1024]{1,0:T(8,128)(2,1)S(1)}, u32[]{:S(2)}, u32[]{:S(2)}) collective-permute-start(bf16[256,1024]{1,0:T(8,128)(2,1)S(1)} %collective-permute-done.15.refs_15_), channel_id=1, source_target_pairs={{0,16},{16,32},{32,48},{48,64},{64,80},{80,96},{96,112},{112,0},{8... | collective-permute-start | bytes 1572872 | tf_op jit(solution)/shard_map/ppermute | solution.py:495
  55.8 13.4 %collective-permute-start.16 = (bf16[256,1024]{1,0:T(8,128)(2,1)S(1)}, bf16[256,1024]{1,0:T(8,128)(2,1)S(1)}, u32[]{:S(2)}, u32[]{:S(2)}) collective-permute-start(bf16[256,1024]{1,0:T(8,128)(2,1)S(1)} %collective-permute-done.12.refs_12_), channel_id=1, source_target_pairs={{0,16},{16,32},{32,48},{48,64},{64,80},{80,96},{96,112},{112,0},{8... | collective-permute-start | bytes 1572872 | tf_op jit(solution)/shard_map/ppermute | solution.py:495
  55.9 7.4 %collective-permute-start.5 = (bf16[4,16,16,128]{3,2,1,0:T(8,128)(2,1)S(1)}, bf16[4,16,16,128]{3,2,1,0:T(8,128)(2,1)S(1)}, u32[]{:S(2)}, u32[]{:S(2)}) collective-permute-start(bf16[4,16,16,128]{3,2,1,0:T(8,128)(2,1)S(1)} %slice_bitcast_fusion), channel_id=1, source_target_pairs={{0,6},{1,7},{2,0},{3,1},{4,2},{5,3},{6,4},{7,5},{8,14},{9,15},{10,... | collective-permute-start | bytes 786440 | tf_op jit(solution)/shard_map/ppermute | solution.py:445
  58.8 6.9 %collective-permute-start.4 = (bf16[4,16,16,128]{3,2,1,0:T(8,128)(2,1)S(1)}, bf16[4,16,16,128]{3,2,1,0:T(8,128)(2,1)S(1)}, u32[]{:S(2)}, u32[]{:S(2)}) collective-permute-start(bf16[4,16,16,128]{3,2,1,0:T(8,128)(2,1)S(1)} %slice_bitcast_fusion.1), channel_id=1, source_target_pairs={{0,2},{1,3},{2,4},{3,5},{4,6},{5,7},{6,0},{7,1},{8,10},{9,11},{10,... | collective-permute-start | bytes 786440 | tf_op jit(solution)/shard_map/ppermute | solution.py:445
  63.3 5.9 %collective-permute-start.10 = (bf16[256,1024]{1,0:T(8,128)(2,1)S(1)}, bf16[256,1024]{1,0:T(8,128)(2,1)S(1)}, u32[]{:S(2)}, u32[]{:S(2)}) collective-permute-start(bf16[256,1024]{1,0:T(8,128)(2,1)S(1)} %collective-permute-done.8.refs_8_), channel_id=1, source_target_pairs={{0,8},{8,0},{16,24},{24,16},{32,40},{40,32},{48,56},{56,48},{64,72... | collective-permute-start | bytes 1572872 | tf_op jit(solution)/shard_map/ppermute | solution.py:441
  76.8 8.6 %collective-permute-start.21 = (bf16[128,1024]{1,0:T(8,128)(2,1)}, bf16[128,1024]{1,0:T(8,128)(2,1)S(1)}, u32[]{:S(2)}, u32[]{:S(2)}) collective-permute-start(bf16[128,1024]{1,0:T(8,128)(2,1)} %get-tuple-element.40), channel_id=1, source_target_pairs={{0,128},{128,0},{1,129},{129,1},{2,130},{130,2},{3,131},{131,3},{4... | collective-permute-start | bytes 786440 | tf_op jit(solution)/shard_map/ppermute | solution.py:441
  83.3 35.7 %collective-permute-start.27 = (bf16[256,1024]{1,0:T(8,128)(2,1)}, bf16[256,1024]{1,0:T(8,128)(2,1)S(1)}, u32[]{:S(2)}, u32[]{:S(2)}) collective-permute-start(bf16[256,1024]{1,0:T(8,128)(2,1)} %shard_map.259), channel_id=1, source_target_pairs={{0,128},{128,0},{1,129},{129,1},{2,130},{130,2},{3,131},{131,3},{4... | collective-permute-start | bytes 1572872 | tf_op jit(solution)/shard_map/ppermute | solution.py:441
  96.7 3.9 %collective-permute-start.23 = (f32[56,128]{1,0:T(8,128)S(1)}, f32[56,128]{1,0:T(8,128)S(1)}, u32[]{:S(2)}, u32[]{:S(2)}) collective-permute-start(f32[56,128]{1,0:T(8,128)S(1)} %add.18), channel_id=1, source_target_pairs={{0,16},{8,24},{16,0},{24,8},{32,48},{40,56},{48,32},{56,40},{64,80... | collective-permute-start | bytes 86024 | tf_op jit(solution)/shard_map/ppermute | solution.py:441
  100.6 4.8 %collective-permute-start.24 = (f32[56,128]{1,0:T(8,128)S(1)}, f32[56,128]{1,0:T(8,128)S(1)}, u32[]{:S(2)}, u32[]{:S(2)}) collective-permute-start(f32[56,128]{1,0:T(8,128)S(1)} %add.19), channel_id=1, source_target_pairs={{0,32},{8,40},{16,48},{24,56},{32,0},{40,8},{48,16},{56,24},{64,96... | collective-permute-start | bytes 86024 | tf_op jit(solution)/shard_map/ppermute | solution.py:441
  105.3 3.9 %collective-permute-start.25 = (f32[56,128]{1,0:T(8,128)S(1)}, f32[56,128]{1,0:T(8,128)S(1)}, u32[]{:S(2)}, u32[]{:S(2)}) collective-permute-start(f32[56,128]{1,0:T(8,128)S(1)} %add.20), channel_id=1, source_target_pairs={{0,128},{128,0},{1,129},{129,1},{2,130},{130,2},{3,131},{131,3},{4... | collective-permute-start | bytes 86024 | tf_op jit(solution)/shard_map/ppermute | solution.py:441
  109.2 7.8 %collective-permute-start.26 = (f32[56,128]{1,0:T(8,128)S(1)}, f32[56,128]{1,0:T(8,128)S(1)}, u32[]{:S(2)}, u32[]{:S(2)}) collective-permute-start(f32[56,128]{1,0:T(8,128)S(1)} %add.21), channel_id=1, source_target_pairs={{0,64},{8,72},{16,80},{24,88},{32,96},{40,104},{48,112},{56,120},{... | collective-permute-start | bytes 86024 | tf_op jit(solution)/shard_map/ppermute | solution.py:441
  (29 other events, 284.2 us)

commit v4 on v3

--- a/solution.py
+++ b/solution.py
@@ -108,24 +108,17 @@
     return jnp.concatenate([jnp.where(left, value, zero), jnp.where(left, zero, value)], axis=0)
 
 
-def picked(dims, half):
-    axis = len(dims) - 4 if len(dims) > 3 else 0
-    span = dims[axis] // 2
-    return (slice(None),) * axis + (pl.ds(half * span, span),), (*dims[:axis], span, *dims[axis + 1 :])
-
-
-def staged(kernel, count, half):
+def staged(kernel, count, lazy):
     def run(meta_ref, *refs):
         inputs, rest = refs[:count], refs[count:]
         outputs, held, sems = rest[: -count - 1], rest[-count - 1 : -1], rest[-1]
-        copies = []
-        for i, (source, target) in enumerate(zip(inputs, held)):
-            if half is not None:
-                source = source.at[picked(source.shape, half)[0]]
-            copies.append(pltpu.make_async_copy(source, target, sems.at[i]))
+        copies = [
+            pltpu.make_async_copy(source, target, sems.at[i])
+            for i, (source, target) in enumerate(zip(inputs, held))
+        ]
         for copy in copies:
             copy.start()
-        if half is not None:
+        if lazy:
             kernel(meta_ref, copies, *held, *outputs)
         else:
             wait(copies)
@@ -218,17 +211,10 @@
     *weights, own_ref, other_ref, rows_ref, sum_ref = refs
     wait(copies[:5])
     place_pieces(meta_ref, (near, up, down, far0, far1), rows_ref)
-    order = ring_order(meta_ref)
-    for i in range(0, len(weights), 2):
-        wait(copies[5 + i : 7 + i])
-        left = [
-            jnp.concatenate([rows_ref[who, order[i]], rows_ref[who, order[i + 1]]], axis=1) for who in range(2)
-        ]
-        product = jnp.dot(
-            jnp.concatenate(left, axis=0),
-            jnp.concatenate([weights[i][...], weights[i + 1][...]], axis=0),
-            preferred_element_type=F32,
-        )
+    for i, (block, shards) in enumerate(zip(weights, ring_order(meta_ref))):
+        copies[5 + i].wait()
+        left = [jnp.concatenate([rows_ref[who, k] for k in shards], axis=1) for who in range(2)]
+        product = jnp.dot(jnp.concatenate(left, axis=0), block[...], preferred_element_type=F32)
         sum_ref[...] = product if i == 0 else sum_ref[...] + product
     length = own_ref.shape[0]
     own_ref[...] = sum_ref[:length, :]
@@ -245,13 +231,13 @@
     chip, core = meta_ref[3], meta_ref[4]
     other = 1 - core
     toward = 1 - 2 * core
-    order = [2 * chip + core, 2 * chip + other]
+    order = [(2 * chip + core, 2 * chip + other)]
     for k in (1, 2, 3):
         back = 2 * lax.rem(chip - toward * k + 8, 8)
         ahead = 2 * lax.rem(chip + toward * k + 8, 8)
-        order += [back + core, back + other, ahead + other, ahead + core]
+        order += [(back + core, back + other), (ahead + other, ahead + core)]
     far = 2 * lax.rem(chip + 4, 8)
-    return order + [far + core, far + other]
+    return order + [(far + core,), (far + other,)]
 
 
 def pull_back(
@@ -385,40 +371,37 @@
     skip_ref[...] = total[50:51, 0:heads]
 
 
-def weight_kernel(meta_ref, copies, near, up, down, far0, far1, *refs):
-    *blocks, out_ref, col_ref = refs
-    wait(copies[:5])
-    place_pieces(meta_ref, (near, up, down, far0, far1), col_ref)
-    order = ring_order(meta_ref)
-    total = None
-    for i in range(0, len(blocks), 2):
-        wait(copies[5 + i : 7 + i])
+def weight_kernel(meta_ref, copies, near, up, down, far0, far1, own_ref, other_ref, keep_ref, give_ref, rows_ref):
+    wait(copies)
+    place_pieces(meta_ref, (near, up, down, far0, far1), rows_ref)
+    chip, core = meta_ref[3], meta_ref[4]
+    toward = 1 - 2 * core
+    tokens = jnp.concatenate([own_ref[...], other_ref[...]], axis=0)
+    for k in range(8):
+        kept = 2 * lax.rem(chip + toward * k + 8, 8) + core
+        given = 2 * lax.rem(chip - toward * k + 8, 8) + 1 - core
+        left = [jnp.concatenate([rows_ref[who, kept], rows_ref[who, given]], axis=1) for who in range(2)]
         product = lax.dot_general(
-            jnp.concatenate(
-                [jnp.concatenate([col_ref[0, k], col_ref[1, k]], axis=1) for k in order[i : i + 2]], axis=0
-            ),
-            jnp.concatenate([blocks[i][...], blocks[i + 1][...]], axis=0),
-            (((0,), (0,)), ((), ())),
-            preferred_element_type=F32,
-        )
-        total = product if i == 0 else total + product
-    out_ref[...] = total.astype(out_ref.dtype)
-
-
-def call(kernel, operands, outs, flops, scratch=(), half=None):
+            jnp.concatenate(left, axis=0), tokens, (((0,), (0,)), ((), ())), preferred_element_type=F32
+        )
+        depth = keep_ref.shape[1]
+        keep_ref[k] = product[:depth]
+        give_ref[k] = product[depth:].astype(BF16)
+
+
+def call(kernel, operands, outs, flops, scratch=(), lazy=False):
     others = operands[1:]
     size = sum(a.size * a.dtype.itemsize for a in operands) + sum(
         a.size * a.dtype.itemsize for a in outs
     )
-    held = [a.shape if half is None else picked(a.shape, half)[1] for a in others]
     return pl.pallas_call(
-        staged(kernel, len(others), half),
+        staged(kernel, len(others), lazy),
         out_shape=outs,
         in_specs=[pl.BlockSpec(memory_space=pltpu.SMEM)] + [pl.BlockSpec(memory_space=pl.ANY)] * len(others),
         out_specs=[pl.BlockSpec(memory_space=pltpu.VMEM)] * len(outs),
         scratch_shapes=[
             *scratch,
-            *[pltpu.VMEM(dims, a.dtype) for dims, a in zip(held, others)],
+            *[pltpu.VMEM(a.shape, a.dtype) for a in others],
             pltpu.SemaphoreType.DMA((len(others),)),
         ],
         compiler_params=pltpu.CompilerParams(vmem_limit_bytes=VMEM_LIMIT),
@@ -457,8 +440,8 @@
     return along_x(up[0], 1), along_x(down[1], -1)
 
 
-def tie(*values):
-    return lax.optimization_barrier(values)
+def after(value, *others):
+    return lax.optimization_barrier((value, *others))[0]
 
 
 def body(
@@ -488,11 +471,11 @@
     pieces = d_out.reshape(own, dp, 2, half).transpose(2, 1, 0, 3)
     theirs = swap(jnp.where(lower, pieces[1], pieces[0]), "rep", 1, 2)
     mine = jnp.where(lower, pieces[0], pieces[1])
-    turned = lax.all_to_all(pieces, "dp", 1, 1, tiled=False)
-    pieces = jnp.concatenate([mine[None], theirs[None], turned], axis=0)
-
     def step(value):
         return lax.ppermute(value, "dp", ring)
+
+    def back(value):
+        return lax.ppermute(value, "dp", [(j, i) for i, j in ring])
 
     def across(*values):
         return [swap(value, "dp", 1, dp) for value in values]
@@ -507,32 +490,51 @@
         ],
         5_000_000_000,
     )
-    one = jnp.concatenate([w_half, normed], axis=0)
-    (two,) = across(one)
-    blocks = [one, two]
-    one, two = step(one), step(two)
-    near = gather_near(pieces)
-
-    blocks += [one, two, *across(one, two)]
-    one, two = step(one), step(two)
-    up, down = gather_next(near)
-
-    blocks += [one, two, *across(one, two)]
-    one, two = step(one), step(two)
-    far = gather_far(up, down)
-    blocks += [one, two, *across(one, two)]
-    one = step(one)
-    blocks += [one, *across(one)]
+
+    def pair_up(block):
+        return jnp.concatenate([block, *across(block)], axis=0)
+
+    def passed(rounds, single):
+        held = [rounds[0]]
+        for pair in rounds[1:]:
+            held += [pair, *across(pair)]
+        return held + [single, *across(single)]
+
+    weights = [pair_up(w_half)]
+    for _ in range(3):
+        weights.append(step(weights[-1]))
+    near = gather_near(after(jnp.stack([mine, theirs]), weights[0]))
+    up, down = gather_next(after(near, weights[1]))
+    rows = (near, up, down, *gather_far(after(up, weights[2]), down))
+
+    keep, give = call(
+        weight_kernel,
+        (meta, *rows, after(normed, weights[3]), swap(normed, "rep", 1, 2)),
+        [shape((chips, half, width)), shape((chips, half, width), BF16)],
+        5_000_000_000,
+        lazy=True,
+        scratch=[pltpu.VMEM((2, dp, length, half), BF16)],
+    )
+    weights = passed(weights, step(weights[-1][:half]))
+    (given,) = across(give)
+
+    def term(k):
+        return keep[k] + given[k].astype(F32)
 
     upstream, other = call(
         upstream_kernel,
-        (meta, near, up, down, *far, *blocks),
+        (meta, *rows, *weights),
         [shape((length, width)), shape((length, width), BF16)],
         4_000_000_000,
-        half=0,
+        lazy=True,
         scratch=[pltpu.VMEM((2, dp, length, half), BF16), pltpu.VMEM((2 * length, width), F32)],
     )
+    one, two = term(4), term(5)
+    one = step(one.astype(BF16)).astype(F32) + term(3)
+    two = back(two.astype(BF16)).astype(F32) + term(6)
+    one, two = after(one, other), after(two, other)
     other = swap(other, "rep", 1, 2)
+
     *act_grads, packed = call(
         backward_kernel,
         (
@@ -547,18 +549,20 @@
         scratch=[pltpu.VMEM((length, width), F32)],
     )
     act_grads[4] = act_grads[4].T
-    share = call(
-        weight_kernel,
-        (meta, near, up, down, *far, *blocks),
-        [shape((features // dp, width), BF16)],
-        5_000_000_000,
-        half=1,
-        scratch=[pltpu.VMEM((2, dp, length, half), BF16)],
-    )[0]
-    weight_grad = share.astype(F32) + swap(share, "rep", 1, 2).astype(F32)
-    for bit in (1, 2, 4):
-        packed = packed + swap(packed, "dp", bit, dp)
+    one = step(one.astype(BF16)).astype(F32) + term(2)
+    two = back(two.astype(BF16)).astype(F32) + term(7)
+    one, two = after(one, packed), after(two, packed)
+    one = step(one.astype(BF16)).astype(F32) + term(1)
+    two = back(two.astype(BF16)).astype(F32)
+    packed = packed + swap(packed, "dp", 1, dp)
+    packed = packed + swap(packed, "dp", 2, dp)
+    total = (term(0) + two + step(after(one, packed).astype(BF16)).astype(F32)).astype(BF16)
     packed = packed + swap(packed, "rep", 1, 2)
+    packed = packed + swap(packed, "dp", 4, dp)
+    partner = swap(after(total, packed), "rep", 1, 2)
+    weight_grad = jnp.concatenate(
+        [jnp.where(lower, total, partner), jnp.where(lower, partner, total)], axis=0
+    ).astype(F32)
     packed = packed + swap(packed, "dp", 8, dp)
     sums = unpack(
         packed,

time: 122 us -> 114 us (0.934)
  waiting for transfers between devices: 54.3 us -> 42.4 us
  starting transfers between devices: 32.3 us -> 34.3 us
  local copies, waits for them, and re-layouts: 3.08 us -> 4.47 us
  Pallas kernels: 24.1 us -> 25.4 us
    ppermute x4, waiting for transfers between devices: 17.4 us -> 0.01 us  [along_x(): lax.ppermute(value, 'tensor', [(i, (i + 2 * by) % 8) for i in range(8)])]
    ppermute x7 -> x8, waiting for transfers between devices: 6.16 us -> 19.2 us  [step(): return lax.ppermute(value, 'dp', ring)]
    ppermute x0 -> x3, starting transfers between devices: none -> 9.52 us  [back(): return lax.ppermute(value, 'dp', [(j, i) for i, j in ring])]
    all_to_all x1 -> x0, starting transfers between devices: 4.29 us -> none  [body(): turned = lax.all_to_all(pieces, 'dp', 1, 1, tiled=False)]
    ppermute x17 -> x16, waiting for transfers between devices: 27.1 us -> 23.1 us  [swap(): return lax.ppermute(value, axis, [(i, i ^ bit) for i in range(size)])]
    ppermute x7 -> x8, starting transfers between devices: 6.06 us -> 2.42 us  [step(): return lax.ppermute(value, 'dp', ring)]
    all_to_all x1 -> x0, waiting for transfers between devices: 3.59 us -> none  [body(): turned = lax.all_to_all(pieces, 'dp', 1, 1, tiled=False)]
    convert_element_type x0 -> x3, other arithmetic: none -> 2.67 us  [the longest x1 1.44 us: body(): two = back(two.astype(BF16)).astype(F32) + term(6)]
  transfers between devices with their start and end apart: 29 -> 31, of which waited for: 15 -> 13; matrix products, arithmetic and copies ran while one was open for 2% -> 3% of each run, Pallas kernels for 12% -> 17%
where the time goes in v4:
time: 114 us; the launch traced here: 113 us
  waiting for transfers between devices  42.4 us (37%)
  starting transfers between devices  34.3 us (30%)
  Pallas kernels  25.4 us (22%)
  other arithmetic  5.08 us (4%)
  local copies, waits for them, and re-layouts  4.47 us (4%)
  between operations  1.69 us (1%)
    pallas_call x4, Pallas kernels, call(): pl.pallas_call(staged(kernel, len(others), lazy), out_shape=outs, in_spec...  24 us
    ppermute x16, waiting for transfers between devices, swap(): return lax.ppermute(value, axis, [(i, i ^ bit) for i in range(size)])  23.1 us
    ppermute x8, waiting for transfers between devices, step(): return lax.ppermute(value, 'dp', ring)  19.2 us
    ppermute x16, starting transfers between devices, swap(): return lax.ppermute(value, axis, [(i, i ^ bit) for i in range(size)])  18 us
    ppermute x3, starting transfers between devices, back(): return lax.ppermute(value, 'dp', [(j, i) for i, j in ring])  9.52 us
    ppermute x4, starting transfers between devices, along_x(): lax.ppermute(value, 'tensor', [(i, (i + 2 * by) % 8) for i in range(8)])  4.28 us
    unnamed x26, local copies, waits for them, and re-layouts  2.8 us
    ppermute x8, starting transfers between devices, step(): return lax.ppermute(value, 'dp', ring)  2.42 us
  transfers between devices with their start and end apart: 31, of which 13 were waited for; matrix products, arithmetic and copies ran while one was open for 3% of the time, Pallas kernels for 17%

profile of v4, /device:TPU:2, one launch (start us, length us, event | category | flops | bytes accessed | tf_op | source)
XLA Modules:
  0.0 113.3 jit_solution(6601402447886621783)
XLA Ops:
  3.4 2.0 %collective-permute-start.3 = (bf16[256,1024]{1,0:T(8,128)(2,1)S(1)}, bf16[256,1024]{1,0:T(8,128)(2,1)}, u32[]{:S(2)}, u32[]{:S(2)}) collective-permute-start(bf16[256,1024]{1,0:T(8,128)(2,1)S(1)} %pad_maximum_fusion.refs_5_), channel_id=1, source_target_pairs={{0,16},{16,32},{32,48},{48,64},{64,80},{80,96},{96,112},{112,0},{8... | collective-permute-start | bytes 1572872 | tf_op jit(solution)/shard_map/ppermute | solution.py:475
  5.4 1.7 %collective-permute-start = (bf16[16,16,128]{2,1,0:T(8,128)(2,1)S(1)}, bf16[16,16,128]{2,1,0:T(8,128)(2,1)S(1)}, u32[]{:S(2)}, u32[]{:S(2)}) collective-permute-start(bf16[16,16,128]{2,1,0:T(8,128)(2,1)S(1)} %get-tuple-element.96), channel_id=1, source_target_pairs={{0,128},{128,0},{1,129},{129,1},{2,130},{130,2},{3,131},{131,3},{4... | collective-permute-start | bytes 196616 | tf_op jit(solution)/shard_map/ppermute | solution.py:424
  7.1 2.7 %collective-permute-done = bf16[16,16,128]{2,1,0:T(8,128)(2,1)S(1)} collective-permute-done((bf16[16,16,128]{2,1,0:T(8,128)(2,1)S(1)}, bf16[16,16,128]{2,1,0:T(8,128)(2,1)S(1)}, u32[]{:S(2)}, u32[]{:S(2)}) %collective-permute-start) | collective-permute-done | bytes 65568 | tf_op jit(solution)/shard_map/ppermute | solution.py:424
  9.8 3.3 %collective-permute-start.2 = (bf16[2,16,16,128]{3,2,1,0:T(8,128)(2,1)S(1)}, bf16[2,16,16,128]{3,2,1,0:T(8,128)(2,1)S(1)}, u32[]{:S(2)}, u32[]{:S(2)}) collective-permute-start(bf16[2,16,16,128]{3,2,1,0:T(8,128)(2,1)S(1)} %pad_maximum_fusion.2), channel_id=1, source_target_pairs={{0,1},{1,0},{2,3},{3,2},{4,5},{5,4},{6,7},{7,6},{8,9},{9,8},{10,11... | collective-permute-start | bytes 393224 | tf_op jit(solution)/shard_map/ppermute | solution.py:424
  14.3 2.3 %collective-permute-done.3.refs_6_ = bf16[256,1024]{1,0:T(8,128)(2,1)} collective-permute-done((bf16[256,1024]{1,0:T(8,128)(2,1)S(1)}, bf16[256,1024]{1,0:T(8,128)(2,1)}, u32[]{:S(2)}, u32[]{:S(2)}) %collective-permute-start.3) | collective-permute-done | bytes 524320 | tf_op jit(solution)/shard_map/ppermute | solution.py:475
  18.7 5.0 %shard_map.256 = (bf16[128,1024]{1,0:T(8,128)(2,1)}, f32[128,1024]{1,0:T(8,128)}, f32[128,1024]{1,0:T(8,128)}, f32[128,1024]{1,0:T(8,128)}, f32[128,1024]{1,0:T(...) custom-call(s32[5]{0:T(128)} %stack.35.meta_ref, ...), custom_call_target="tpu_custom_call" | custom-call | flops 5000000000 | bytes 3936980 | tf_op jit(solution)/shard_map/pallas_call | solution.py:397
  23.8 1.7 %collective-permute-start.21 = (bf16[128,1024]{1,0:T(8,128)(2,1)}, bf16[128,1024]{1,0:T(8,128)(2,1)S(1)}, u32[]{:S(2)}, u32[]{:S(2)}) collective-permute-start(bf16[128,1024]{1,0:T(8,128)(2,1)} %get-tuple-element.78.refs_5_), channel_id=1, source_target_pairs={{0,128},{128,0},{1,129},{129,1},{2,130},{130,2},{3,131},{131,3},{4... | collective-permute-start | bytes 786440 | tf_op jit(solution)/shard_map/ppermute | solution.py:424
  25.5 1.8 %collective-permute-done.6.refs_8_ = bf16[256,1024]{1,0:T(8,128)(2,1)} collective-permute-done((bf16[256,1024]{1,0:T(8,128)(2,1)}, bf16[256,1024]{1,0:T(8,128)(2,1)}, u32[]{:S(2)}, u32[]{:S(2)}) %collective-permute-start.6) | collective-permute-done | bytes 524320 | tf_op jit(solution)/shard_map/ppermute | solution.py:475
  29.5 8.4 %collective-permute-done.11.refs_10_ = bf16[256,1024]{1,0:T(8,128)(2,1)S(1)} collective-permute-done((bf16[256,1024]{1,0:T(8,128)(2,1)}, bf16[256,1024]{1,0:T(8,128)(2,1)S(1)}, u32[]{:S(2)}, u32[]{:S(2)}) %collective-permute-start.11) | collective-permute-done | bytes 524320 | tf_op jit(solution)/shard_map/ppermute | solution.py:475
  39.3 6.1 %shard_map.259 = (f32[8,128,1024]{2,1,0:T(8,128)}, bf16[8,128,1024]{2,1,0:T(8,128)(2,1)}) custom-call(s32[5]{0:T(128)} %stack.35.meta_ref, bf16[2,2,16,16,128]{4,3,2,1,0:T(8,128)(2,1)} %copy-done.2, bf16[2,2,16,16,128]{4,3,2,1,0:T(8,128)(2,1)} %copy-done.5, bf16[2,2,16,16,128]{4,3,2,1,0:T(8,128)(2,1)} %copy-done.4, bf16[2,16,16,128]{3,2,1,0:T(8,128)(2,1)} %copy-done.12, ...), custom_call_target="tpu_custom_call" | custom-call | flops 5000000000 | bytes 7864340 | tf_op jit(solution)/shard_map/pallas_call | solution.py:397
  46.2 1.8 %collective-permute-start.10 = (bf16[256,1024]{1,0:T(8,128)(2,1)}, bf16[256,1024]{1,0:T(8,128)(2,1)}, u32[]{:S(2)}, u32[]{:S(2)}) collective-permute-start(bf16[256,1024]{1,0:T(8,128)(2,1)} %collective-permute-done.6.refs_8_), channel_id=1, source_target_pairs={{0,8},{8,0},{16,24},{24,16},{32,40},{40,32},{48,56},{56,48},{64,72... | collective-permute-start | bytes 1572872 | tf_op jit(solution)/shard_map/ppermute | solution.py:424
  48.0 5.8 %collective-permute-done.13.refs_12_ = bf16[128,1024]{1,0:T(8,128)(2,1)S(1)} collective-permute-done((bf16[128,1024]{1,0:T(8,128)(2,1)S(1)}, bf16[128,1024]{1,0:T(8,128)(2,1)S(1)}, u32[]{:S(2)}, u32[]{:S(2)}) %collective-permute-start.13) | collective-permute-done | bytes 262176 | tf_op jit(solution)/shard_map/ppermute | solution.py:475
  56.1 4.9 %shard_map.255 = (f32[128,1024]{1,0:T(8,128)}, bf16[128,1024]{1,0:T(8,128)(2,1)}) custom-call(s32[5]{0:T(128)} %stack.35.meta_ref, bf16[2,2,16,16,128]{4,3,2,1,0:T(8,128)(2,1)} %copy-done.2, bf16[2,2,16,16,128]{4,3,2,1,0:T(8,128)(2,1)} %copy-done.5, bf16[2,2,16,16,128]{4,3,2,1,0:T(8,128)(2,1)} %copy-done.4, bf16[2,16,16,128]{3,2,1,0:T(8,128)(2,1)} %copy-done.12, ...), custom_call_target="tpu_custom_call" | custom-call | flops 4000000000 | bytes 6029332 | tf_op jit(solution)/shard_map/pallas_call | solution.py:397
  61.0 1.7 %collective-permute-start.15 = (bf16[128,1024]{1,0:T(8,128)(2,1)}, bf16[128,1024]{1,0:T(8,128)(2,1)S(1)}, u32[]{:S(2)}, u32[]{:S(2)}) collective-permute-start(bf16[128,1024]{1,0:T(8,128)(2,1)} %get-tuple-element.54), channel_id=1, source_target_pairs={{0,128},{128,0},{1,129},{129,1},{2,130},{130,2},{3,131},{131,3},{4... | collective-permute-start | bytes 786440 | tf_op jit(solution)/shard_map/ppermute | solution.py:424
  62.6 3.1 %collective-permute-start.23 = (bf16[128,1024]{1,0:T(8,128)(2,1)S(1)}, bf16[128,1024]{1,0:T(8,128)(2,1)S(1)}, u32[]{:S(2)}, u32[]{:S(2)}) collective-permute-start(bf16[128,1024]{1,0:T(8,128)(2,1)S(1)} %get-tuple-element.91), channel_id=1, source_target_pairs={{16,0},{32,16},{48,32},{64,48},{80,64},{96,80},{112,96},{0,112},{1... | collective-permute-start | bytes 786440 | tf_op jit(solution)/shard_map/ppermute | solution.py:478
  65.9 4.2 %collective-permute-done.15.refs_1_ = bf16[128,1024]{1,0:T(8,128)(2,1)S(1)} collective-permute-done((bf16[128,1024]{1,0:T(8,128)(2,1)}, bf16[128,1024]{1,0:T(8,128)(2,1)S(1)}, u32[]{:S(2)}, u32[]{:S(2)}) %collective-permute-start.15) | collective-permute-done | bytes 262176 | tf_op jit(solution)/shard_map/ppermute | solution.py:424
  70.8 8.0 %shard_map.257 = (bf16[128,1024]{1,0:T(8,128)(2,1)}, bf16[128,1024]{1,0:T(8,128)(2,1)}, bf16[128,128]{1,0:T(8,128)(2,1)}, bf16[128,128]{1,0:T(8,128)(2,1)}, bf16[16,128]{1,0:T(8,128)(2,1)}, /*index=5*/f32[56,128]{1,0:T(8,128)}) custom-call(s32[5]{0:T(128)} %stack.35.meta_ref, f32[128,1024]{1,0:T(8,128)} %get-tuple-element.53.refs_0_, ...), custom_call_target="tpu_custom_call" | custom-call | flops 10000000000 | bytes 4817556 | tf_op jit(solution)/shard_map/pallas_call | solution.py:397
  79.2 3.2 %collective-permute-start.24 = (bf16[128,1024]{1,0:T(8,128)(2,1)S(1)}, bf16[128,1024]{1,0:T(8,128)(2,1)S(1)}, u32[]{:S(2)}, u32[]{:S(2)}) collective-permute-start(bf16[128,1024]{1,0:T(8,128)(2,1)S(1)} %get-tuple-element.81), channel_id=1, source_target_pairs={{16,0},{32,16},{48,32},{64,48},{80,64},{96,80},{112,96},{0,112},{1... | collective-permute-start | bytes 786440 | tf_op jit(solution)/shard_map/ppermute | solution.py:478
  83.6 4.2 %collective-permute-done.17 = f32[56,128]{1,0:T(8,128)S(1)} collective-permute-done((f32[56,128]{1,0:T(8,128)S(1)}, f32[56,128]{1,0:T(8,128)S(1)}, u32[]{:S(2)}, u32[]{:S(2)}) %collective-permute-start.17) | collective-permute-done | bytes 28704 | tf_op jit(solution)/shard_map/ppermute | solution.py:424
  89.0 3.2 %collective-permute-start.25 = (bf16[128,1024]{1,0:T(8,128)(2,1)S(1)}, bf16[128,1024]{1,0:T(8,128)(2,1)S(1)}, u32[]{:S(2)}, u32[]{:S(2)}) collective-permute-start(bf16[128,1024]{1,0:T(8,128)(2,1)S(1)} %get-tuple-element.82), channel_id=1, source_target_pairs={{16,0},{32,16},{48,32},{64,48},{80,64},{96,80},{112,96},{0,112},{1... | collective-permute-start | bytes 786440 | tf_op jit(solution)/shard_map/ppermute | solution.py:478
  93.4 2.7 %collective-permute-done.18 = f32[56,128]{1,0:T(8,128)S(1)} collective-permute-done((f32[56,128]{1,0:T(8,128)S(1)}, f32[56,128]{1,0:T(8,128)S(1)}, u32[]{:S(2)}, u32[]{:S(2)}) %collective-permute-start.18) | collective-permute-done | bytes 28704 | tf_op jit(solution)/shard_map/ppermute | solution.py:424
  96.4 4.5 %collective-permute-done.19 = f32[56,128]{1,0:T(8,128)S(1)} collective-permute-done((f32[56,128]{1,0:T(8,128)S(1)}, f32[56,128]{1,0:T(8,128)S(1)}, u32[]{:S(2)}, u32[]{:S(2)}) %collective-permute-start.19) | collective-permute-done | bytes 28704 | tf_op jit(solution)/shard_map/ppermute | solution.py:424
  102.3 4.6 %collective-permute-start.20 = (f32[56,128]{1,0:T(8,128)S(1)}, f32[56,128]{1,0:T(8,128)S(1)}, u32[]{:S(2)}, u32[]{:S(2)}) collective-permute-start(f32[56,128]{1,0:T(8,128)S(1)} %add.83), channel_id=1, source_target_pairs={{0,64},{8,72},{16,80},{24,88},{32,96},{40,104},{48,112},{56,120},{... | collective-permute-start | bytes 86024 | tf_op jit(solution)/shard_map/ppermute | solution.py:424
  106.9 3.2 %collective-permute-done.20 = f32[56,128]{1,0:T(8,128)S(1)} collective-permute-done((f32[56,128]{1,0:T(8,128)S(1)}, f32[56,128]{1,0:T(8,128)S(1)}, u32[]{:S(2)}, u32[]{:S(2)}) %collective-permute-start.20) | collective-permute-done | bytes 28704 | tf_op jit(solution)/shard_map/ppermute | solution.py:424
  (92 shorter events, 21.7 us)
Async XLA Ops:
  3.4 13.2 %collective-permute-start.3 = (bf16[256,1024]{1,0:T(8,128)(2,1)S(1)}, bf16[256,1024]{1,0:T(8,128)(2,1)}, u32[]{:S(2)}, u32[]{:S(2)}) collective-permute-start(bf16[256,1024]{1,0:T(8,128)(2,1)S(1)} %pad_maximum_fusion.refs_5_), channel_id=1, source_target_pairs={{0,16},{16,32},{32,48},{48,64},{64,80},{80,96},{96,112},{112,0},{8... | collective-permute-start | bytes 1572872 | tf_op jit(solution)/shard_map/ppermute | solution.py:475
  9.8 6.8 %collective-permute-start.2 = (bf16[2,16,16,128]{3,2,1,0:T(8,128)(2,1)S(1)}, bf16[2,16,16,128]{3,2,1,0:T(8,128)(2,1)S(1)}, u32[]{:S(2)}, u32[]{:S(2)}) collective-permute-start(bf16[2,16,16,128]{3,2,1,0:T(8,128)(2,1)S(1)} %pad_maximum_fusion.2), channel_id=1, source_target_pairs={{0,1},{1,0},{2,3},{3,2},{4,5},{5,4},{6,7},{7,6},{8,9},{9,8},{10,11... | collective-permute-start | bytes 393224 | tf_op jit(solution)/shard_map/ppermute | solution.py:424
  16.6 10.7 %collective-permute-start.6 = (bf16[256,1024]{1,0:T(8,128)(2,1)}, bf16[256,1024]{1,0:T(8,128)(2,1)}, u32[]{:S(2)}, u32[]{:S(2)}) collective-permute-start(bf16[256,1024]{1,0:T(8,128)(2,1)} %collective-permute-done.3.refs_6_), channel_id=1, source_target_pairs={{0,16},{16,32},{32,48},{48,64},{64,80},{80,96},{96,112},{112,0},{8... | collective-permute-start | bytes 1572872 | tf_op jit(solution)/shard_map/ppermute | solution.py:475
  16.6 10.7 %collective-permute-start.5 = (bf16[2,2,16,16,128]{4,3,2,1,0:T(8,128)(2,1)S(1)}, bf16[2,2,16,16,128]{4,3,2,1,0:T(8,128)(2,1)S(1)}, u32[]{:S(2)}, u32[]{:S(2)}) collective-permute-start(bf16[2,2,16,16,128]{4,3,2,1,0:T(8,128)(2,1)S(1)} %pad_maximum_fusion.1.refs_0_), channel_id=1, source_target_pairs={{0,6},{1,7},{2,0},{3,1},{4,2},{5,3},{6,4},{7,5},{8,14},{9,15},{10,... | collective-permute-start | bytes 786440 | tf_op jit(solution)/shard_map/ppermute | solution.py:428
  17.3 11.3 %collective-permute-start.4 = (bf16[2,2,16,16,128]{4,3,2,1,0:T(8,128)(2,1)S(1)}, bf16[2,2,16,16,128]{4,3,2,1,0:T(8,128)(2,1)S(1)}, u32[]{:S(2)}, u32[]{:S(2)}) collective-permute-start(bf16[2,2,16,16,128]{4,3,2,1,0:T(8,128)(2,1)S(1)} %pad_maximum_fusion.1.refs_0_), channel_id=1, source_target_pairs={{0,2},{1,3},{2,4},{3,5},{4,6},{5,7},{6,0},{7,1},{8,10},{9,11},{10,... | collective-permute-start | bytes 786440 | tf_op jit(solution)/shard_map/ppermute | solution.py:428
  23.8 14.1 %collective-permute-start.21 = (bf16[128,1024]{1,0:T(8,128)(2,1)}, bf16[128,1024]{1,0:T(8,128)(2,1)S(1)}, u32[]{:S(2)}, u32[]{:S(2)}) collective-permute-start(bf16[128,1024]{1,0:T(8,128)(2,1)} %get-tuple-element.78.refs_5_), channel_id=1, source_target_pairs={{0,128},{128,0},{1,129},{129,1},{2,130},{130,2},{3,131},{131,3},{4... | collective-permute-start | bytes 786440 | tf_op jit(solution)/shard_map/ppermute | solution.py:424
  27.3 10.6 %collective-permute-start.11 = (bf16[256,1024]{1,0:T(8,128)(2,1)}, bf16[256,1024]{1,0:T(8,128)(2,1)S(1)}, u32[]{:S(2)}, u32[]{:S(2)}) collective-permute-start(bf16[256,1024]{1,0:T(8,128)(2,1)} %collective-permute-done.6.refs_8_), channel_id=1, source_target_pairs={{0,16},{16,32},{32,48},{48,64},{64,80},{80,96},{96,112},{112,0},{8... | collective-permute-start | bytes 1572872 | tf_op jit(solution)/shard_map/ppermute | solution.py:475
  27.3 10.6 %collective-permute-start.8 = (bf16[2,16,16,128]{3,2,1,0:T(8,128)(2,1)S(1)}, bf16[2,16,16,128]{3,2,1,0:T(8,128)(2,1)S(1)}, u32[]{:S(2)}, u32[]{:S(2)}) collective-permute-start(bf16[2,16,16,128]{3,2,1,0:T(8,128)(2,1)S(1)} %slice_bitcast_fusion), channel_id=1, source_target_pairs={{0,6},{1,7},{2,0},{3,1},{4,2},{5,3},{6,4},{7,5},{8,14},{9,15},{10,... | collective-permute-start | bytes 393224 | tf_op jit(solution)/shard_map/ppermute | solution.py:428
  28.5 9.4 %collective-permute-start.7 = (bf16[2,16,16,128]{3,2,1,0:T(8,128)(2,1)S(1)}, bf16[2,16,16,128]{3,2,1,0:T(8,128)(2,1)S(1)}, u32[]{:S(2)}, u32[]{:S(2)}) collective-permute-start(bf16[2,16,16,128]{3,2,1,0:T(8,128)(2,1)S(1)} %slice_bitcast_fusion.1), channel_id=1, source_target_pairs={{0,2},{1,3},{2,4},{3,5},{4,6},{5,7},{6,0},{7,1},{8,10},{9,11},{10,... | collective-permute-start | bytes 393224 | tf_op jit(solution)/shard_map/ppermute | solution.py:428
  45.5 8.3 %collective-permute-start.22 = (bf16[8,128,1024]{2,1,0:T(8,128)(2,1)}, bf16[8,128,1024]{2,1,0:T(8,128)(2,1)S(1)}, u32[]{:S(2)}, u32[]{:S(2)}) collective-permute-start(bf16[8,128,1024]{2,1,0:T(8,128)(2,1)} %get-tuple-element.80), channel_id=1, source_target_pairs={{0,8},{8,0},{16,24},{24,16},{32,40},{40,32},{48,56},{56,48},{64,72... | collective-permute-start | bytes 6291464 | tf_op jit(solution)/shard_map/ppermute | solution.py:424
  45.6 9.7 %collective-permute-start.9 = (bf16[256,1024]{1,0:T(8,128)(2,1)}, bf16[256,1024]{1,0:T(8,128)(2,1)}, u32[]{:S(2)}, u32[]{:S(2)}) collective-permute-start(bf16[256,1024]{1,0:T(8,128)(2,1)} %collective-permute-done.3.refs_6_), channel_id=1, source_target_pairs={{0,8},{8,0},{16,24},{24,16},{32,40},{40,32},{48,56},{56,48},{64,72... | collective-permute-start | bytes 1572872 | tf_op jit(solution)/shard_map/ppermute | solution.py:424
  46.1 7.7 %collective-permute-start.13 = (bf16[128,1024]{1,0:T(8,128)(2,1)S(1)}, bf16[128,1024]{1,0:T(8,128)(2,1)S(1)}, u32[]{:S(2)}, u32[]{:S(2)}) collective-permute-start(bf16[128,1024]{1,0:T(8,128)(2,1)S(1)} %slice.97), channel_id=1, source_target_pairs={{0,16},{16,32},{32,48},{48,64},{64,80},{80,96},{96,112},{112,0},{8... | collective-permute-start | bytes 786440 | tf_op jit(solution)/shard_map/ppermute | solution.py:475
  46.2 9.1 %collective-permute-start.10 = (bf16[256,1024]{1,0:T(8,128)(2,1)}, bf16[256,1024]{1,0:T(8,128)(2,1)}, u32[]{:S(2)}, u32[]{:S(2)}) collective-permute-start(bf16[256,1024]{1,0:T(8,128)(2,1)} %collective-permute-done.6.refs_8_), channel_id=1, source_target_pairs={{0,8},{8,0},{16,24},{24,16},{32,40},{40,32},{48,56},{56,48},{64,72... | collective-permute-start | bytes 1572872 | tf_op jit(solution)/shard_map/ppermute | solution.py:424
  48.0 7.4 %collective-permute-start.12 = (bf16[256,1024]{1,0:T(8,128)(2,1)S(1)}, bf16[256,1024]{1,0:T(8,128)(2,1)}, u32[]{:S(2)}, u32[]{:S(2)}) collective-permute-start(bf16[256,1024]{1,0:T(8,128)(2,1)S(1)} %collective-permute-done.11.refs_10_), channel_id=1, source_target_pairs={{0,8},{8,0},{16,24},{24,16},{32,40},{40,32},{48,56},{56,48},{64,72... | collective-permute-start | bytes 1572872 | tf_op jit(solution)/shard_map/ppermute | solution.py:424
  55.2 10.5 %collective-permute-start.26 = (bf16[128,1024]{1,0:T(8,128)(2,1)S(1)}, bf16[128,1024]{1,0:T(8,128)(2,1)S(1)}, u32[]{:S(2)}, u32[]{:S(2)}) collective-permute-start(bf16[128,1024]{1,0:T(8,128)(2,1)S(1)} %get-tuple-element.92), channel_id=1, source_target_pairs={{0,16},{16,32},{32,48},{48,64},{64,80},{80,96},{96,112},{112,0},{8... | collective-permute-start | bytes 786440 | tf_op jit(solution)/shard_map/ppermute | solution.py:475
  61.0 9.2 %collective-permute-start.15 = (bf16[128,1024]{1,0:T(8,128)(2,1)}, bf16[128,1024]{1,0:T(8,128)(2,1)S(1)}, u32[]{:S(2)}, u32[]{:S(2)}) collective-permute-start(bf16[128,1024]{1,0:T(8,128)(2,1)} %get-tuple-element.54), channel_id=1, source_target_pairs={{0,128},{128,0},{1,129},{129,1},{2,130},{130,2},{3,131},{131,3},{4... | collective-permute-start | bytes 786440 | tf_op jit(solution)/shard_map/ppermute | solution.py:424
  62.6 16.2 %collective-permute-start.23 = (bf16[128,1024]{1,0:T(8,128)(2,1)S(1)}, bf16[128,1024]{1,0:T(8,128)(2,1)S(1)}, u32[]{:S(2)}, u32[]{:S(2)}) collective-permute-start(bf16[128,1024]{1,0:T(8,128)(2,1)S(1)} %get-tuple-element.91), channel_id=1, source_target_pairs={{16,0},{32,16},{48,32},{64,48},{80,64},{96,80},{112,96},{0,112},{1... | collective-permute-start | bytes 786440 | tf_op jit(solution)/shard_map/ppermute | solution.py:478
  65.8 13.0 %collective-permute-start.27 = (bf16[128,1024]{1,0:T(8,128)(2,1)S(1)}, bf16[128,1024]{1,0:T(8,128)(2,1)S(1)}, u32[]{:S(2)}, u32[]{:S(2)}) collective-permute-start(bf16[128,1024]{1,0:T(8,128)(2,1)S(1)} %bitcast_add_fusion.2), channel_id=1, source_target_pairs={{0,16},{16,32},{32,48},{48,64},{64,80},{80,96},{96,112},{112,0},{8... | collective-permute-start | bytes 786440 | tf_op jit(solution)/shard_map/ppermute | solution.py:475
  79.1 9.6 %collective-permute-start.28 = (bf16[128,1024]{1,0:T(8,128)(2,1)S(1)}, bf16[128,1024]{1,0:T(8,128)(2,1)S(1)}, u32[]{:S(2)}, u32[]{:S(2)}) collective-permute-start(bf16[128,1024]{1,0:T(8,128)(2,1)S(1)} %get-tuple-element.84), channel_id=1, source_target_pairs={{0,16},{16,32},{32,48},{48,64},{64,80},{80,96},{96,112},{112,0},{8... | collective-permute-start | bytes 786440 | tf_op jit(solution)/shard_map/ppermute | solution.py:475
  79.2 9.5 %collective-permute-start.24 = (bf16[128,1024]{1,0:T(8,128)(2,1)S(1)}, bf16[128,1024]{1,0:T(8,128)(2,1)S(1)}, u32[]{:S(2)}, u32[]{:S(2)}) collective-permute-start(bf16[128,1024]{1,0:T(8,128)(2,1)S(1)} %get-tuple-element.81), channel_id=1, source_target_pairs={{16,0},{32,16},{48,32},{64,48},{80,64},{96,80},{112,96},{0,112},{1... | collective-permute-start | bytes 786440 | tf_op jit(solution)/shard_map/ppermute | solution.py:478
  88.9 12.0 %collective-permute-start.29 = (bf16[128,1024]{1,0:T(8,128)(2,1)S(1)}, bf16[128,1024]{1,0:T(8,128)(2,1)S(1)}, u32[]{:S(2)}, u32[]{:S(2)}) collective-permute-start(bf16[128,1024]{1,0:T(8,128)(2,1)S(1)} %get-tuple-element.85), channel_id=1, source_target_pairs={{0,16},{16,32},{32,48},{48,64},{64,80},{80,96},{96,112},{112,0},{8... | collective-permute-start | bytes 786440 | tf_op jit(solution)/shard_map/ppermute | solution.py:475
  89.0 11.9 %collective-permute-start.25 = (bf16[128,1024]{1,0:T(8,128)(2,1)S(1)}, bf16[128,1024]{1,0:T(8,128)(2,1)S(1)}, u32[]{:S(2)}, u32[]{:S(2)}) collective-permute-start(bf16[128,1024]{1,0:T(8,128)(2,1)S(1)} %get-tuple-element.82), channel_id=1, source_target_pairs={{16,0},{32,16},{48,32},{64,48},{80,64},{96,80},{112,96},{0,112},{1... | collective-permute-start | bytes 786440 | tf_op jit(solution)/shard_map/ppermute | solution.py:478
  101.1 11.1 %collective-permute-start.30 = (bf16[128,1024]{1,0:T(8,128)(2,1)S(1)}, bf16[128,1024]{1,0:T(8,128)(2,1)S(1)}, u32[]{:S(2)}, u32[]{:S(2)}) collective-permute-start(bf16[128,1024]{1,0:T(8,128)(2,1)S(1)} %fusion.1), channel_id=1, source_target_pairs={{0,128},{128,0},{1,129},{129,1},{2,130},{130,2},{3,131},{131,3},{4... | collective-permute-start | bytes 786440 | tf_op jit(solution)/shard_map/ppermute | solution.py:424
  102.3 7.8 %collective-permute-start.20 = (f32[56,128]{1,0:T(8,128)S(1)}, f32[56,128]{1,0:T(8,128)S(1)}, u32[]{:S(2)}, u32[]{:S(2)}) collective-permute-start(f32[56,128]{1,0:T(8,128)S(1)} %add.83), channel_id=1, source_target_pairs={{0,64},{8,72},{16,80},{24,88},{32,96},{40,104},{48,112},{56,120},{... | collective-permute-start | bytes 86024 | tf_op jit(solution)/shard_map/ppermute | solution.py:424
  (20 other events, 98.6 us)

commit v5 on v4

--- a/solution.py
+++ b/solution.py
@@ -353,10 +353,10 @@
         par_ref[44 + tap : 45 + tap, :] = tap_grads[tap]
 
 
-def unpack_kernel(par_ref, cx_ref, cb_ref, cc_ref, al_ref, bias_ref, skip_ref, gain_ref):
+def unpack_kernel(par_ref, far_ref, cx_ref, cb_ref, cc_ref, al_ref, bias_ref, skip_ref, gain_ref):
     heads = al_ref.shape[1]
     tiles = cx_ref.shape[1] // LANES
-    total = par_ref[...]
+    total = par_ref[...] + far_ref[...]
     for tap in range(KCONV):
         for tile in range(tiles):
             cx_ref[tap : tap + 1, tile * LANES : (tile + 1) * LANES] = total[
@@ -409,11 +409,11 @@
     )(*operands)
 
 
-def unpack(packed, outs):
+def unpack(packed, far, outs):
     vmem = pl.BlockSpec(memory_space=pltpu.VMEM)
     return pl.pallas_call(
-        unpack_kernel, out_shape=outs, in_specs=[vmem], out_specs=[vmem] * len(outs)
-    )(packed)
+        unpack_kernel, out_shape=outs, in_specs=[vmem] * 2, out_specs=[vmem] * len(outs)
+    )(packed, far)
 
 
 def shape(dims, dtype=F32):
@@ -563,9 +563,10 @@
     weight_grad = jnp.concatenate(
         [jnp.where(lower, total, partner), jnp.where(lower, partner, total)], axis=0
     ).astype(F32)
-    packed = packed + swap(packed, "dp", 8, dp)
+    far = swap(packed, "dp", 8, dp)
     sums = unpack(
-        packed,
+        after(packed, weight_grad),
+        far,
         [
             shape(conv_x.shape), shape(conv_b.shape), shape(conv_c.shape),
             shape((1, heads)), shape((1, heads)), shape((1, heads)), shape((1, width)),

time: 114 us -> 113 us (level)
    ppermute x3, starting transfers between devices: 9.52 us -> 7.15 us  [back(): return lax.ppermute(value, 'dp', [(j, i) for i, j in ring])]
    ppermute x8, starting transfers between devices: 2.42 us -> 3.59 us  [step(): return lax.ppermute(value, 'dp', ring)]
    unnamed x26 -> x30, local copies, waits for them, and re-layouts: 2.8 us -> 3.39 us
  transfers between devices with their start and end apart: 31 -> 31, of which waited for: 13 -> 14; matrix products, arithmetic and copies ran while one was open for 3% -> 4% of each run, Pallas kernels for 17% -> 16%
where the time goes in v5:
time: 113 us; the launch traced here: 112 us
  waiting for transfers between devices  41.8 us (37%)
  starting transfers between devices  33.4 us (30%)
  Pallas kernels  25.4 us (22%)
  local copies, waits for them, and re-layouts  5.06 us (4%)
  other arithmetic  4.49 us (4%)
  between operations  1.68 us (1%)
    pallas_call x4, Pallas kernels, call(): pl.pallas_call(staged(kernel, len(others), lazy), out_shape=outs, in_spec...  24 us
    ppermute x16, waiting for transfers between devices, swap(): return lax.ppermute(value, axis, [(i, i ^ bit) for i in range(size)])  23.2 us
    ppermute x8, waiting for transfers between devices, step(): return lax.ppermute(value, 'dp', ring)  18.5 us
    ppermute x16, starting transfers between devices, swap(): return lax.ppermute(value, axis, [(i, i ^ bit) for i in range(size)])  18.4 us
    ppermute x3, starting transfers between devices, back(): return lax.ppermute(value, 'dp', [(j, i) for i, j in ring])  7.15 us
    ppermute x4, starting transfers between devices, along_x(): lax.ppermute(value, 'tensor', [(i, (i + 2 * by) % 8) for i in range(8)])  4.28 us
    ppermute x8, starting transfers between devices, step(): return lax.ppermute(value, 'dp', ring)  3.59 us
    unnamed x30, local copies, waits for them, and re-layouts  3.39 us
  transfers between devices with their start and end apart: 31, of which 14 were waited for; matrix products, arithmetic and copies ran while one was open for 4% of the time, Pallas kernels for 16%

profile of v5, /device:TPU:2, one launch (start us, length us, event | category | flops | bytes accessed | tf_op | source)
XLA Modules:
  0.0 111.8 jit_solution(1740357661392735216)
XLA Ops:
  3.4 2.0 %collective-permute-start.3 = (bf16[256,1024]{1,0:T(8,128)(2,1)S(1)}, bf16[256,1024]{1,0:T(8,128)(2,1)}, u32[]{:S(2)}, u32[]{:S(2)}) collective-permute-start(bf16[256,1024]{1,0:T(8,128)(2,1)S(1)} %pad_maximum_fusion.refs_5_), channel_id=1, source_target_pairs={{0,16},{16,32},{32,48},{48,64},{64,80},{80,96},{96,112},{112,0},{8... | collective-permute-start | bytes 1572872 | tf_op jit(solution)/shard_map/ppermute | solution.py:475
  5.4 1.7 %collective-permute-start = (bf16[16,16,128]{2,1,0:T(8,128)(2,1)S(1)}, bf16[16,16,128]{2,1,0:T(8,128)(2,1)S(1)}, u32[]{:S(2)}, u32[]{:S(2)}) collective-permute-start(bf16[16,16,128]{2,1,0:T(8,128)(2,1)S(1)} %get-tuple-element.98), channel_id=1, source_target_pairs={{0,128},{128,0},{1,129},{129,1},{2,130},{130,2},{3,131},{131,3},{4... | collective-permute-start | bytes 196616 | tf_op jit(solution)/shard_map/ppermute | solution.py:424
  7.1 2.7 %collective-permute-done = bf16[16,16,128]{2,1,0:T(8,128)(2,1)S(1)} collective-permute-done((bf16[16,16,128]{2,1,0:T(8,128)(2,1)S(1)}, bf16[16,16,128]{2,1,0:T(8,128)(2,1)S(1)}, u32[]{:S(2)}, u32[]{:S(2)}) %collective-permute-start) | collective-permute-done | bytes 65568 | tf_op jit(solution)/shard_map/ppermute | solution.py:424
  9.8 3.3 %collective-permute-start.2 = (bf16[2,16,16,128]{3,2,1,0:T(8,128)(2,1)S(1)}, bf16[2,16,16,128]{3,2,1,0:T(8,128)(2,1)S(1)}, u32[]{:S(2)}, u32[]{:S(2)}) collective-permute-start(bf16[2,16,16,128]{3,2,1,0:T(8,128)(2,1)S(1)} %pad_maximum_fusion.2), channel_id=1, source_target_pairs={{0,1},{1,0},{2,3},{3,2},{4,5},{5,4},{6,7},{7,6},{8,9},{9,8},{10,11... | collective-permute-start | bytes 393224 | tf_op jit(solution)/shard_map/ppermute | solution.py:424
  14.3 2.3 %collective-permute-done.3.refs_6_ = bf16[256,1024]{1,0:T(8,128)(2,1)} collective-permute-done((bf16[256,1024]{1,0:T(8,128)(2,1)S(1)}, bf16[256,1024]{1,0:T(8,128)(2,1)}, u32[]{:S(2)}, u32[]{:S(2)}) %collective-permute-start.3) | collective-permute-done | bytes 524320 | tf_op jit(solution)/shard_map/ppermute | solution.py:475
  16.6 1.6 %collective-permute-start.4 = (bf16[2,2,16,16,128]{4,3,2,1,0:T(8,128)(2,1)S(1)}, bf16[2,2,16,16,128]{4,3,2,1,0:T(8,128)(2,1)S(1)}, u32[]{:S(2)}, u32[]{:S(2)}) collective-permute-start(bf16[2,2,16,16,128]{4,3,2,1,0:T(8,128)(2,1)S(1)} %pad_maximum_fusion.1.refs_0_), channel_id=1, source_target_pairs={{0,2},{1,3},{2,4},{3,5},{4,6},{5,7},{6,0},{7,1},{8,10},{9,11},{10,... | collective-permute-start | bytes 786440 | tf_op jit(solution)/shard_map/ppermute | solution.py:428
  18.7 5.0 %shard_map.256 = (bf16[128,1024]{1,0:T(8,128)(2,1)}, f32[128,1024]{1,0:T(8,128)}, f32[128,1024]{1,0:T(8,128)}, f32[128,1024]{1,0:T(8,128)}, f32[128,1024]{1,0:T(...) custom-call(s32[5]{0:T(128)} %stack.35.meta_ref, ...), custom_call_target="tpu_custom_call" | custom-call | flops 5000000000 | bytes 3936980 | tf_op jit(solution)/shard_map/pallas_call | solution.py:397
  23.8 1.7 %collective-permute-start.20 = (bf16[128,1024]{1,0:T(8,128)(2,1)}, bf16[128,1024]{1,0:T(8,128)(2,1)S(1)}, u32[]{:S(2)}, u32[]{:S(2)}) collective-permute-start(bf16[128,1024]{1,0:T(8,128)(2,1)} %get-tuple-element.72.refs_5_), channel_id=1, source_target_pairs={{0,128},{128,0},{1,129},{129,1},{2,130},{130,2},{3,131},{131,3},{4... | collective-permute-start | bytes 786440 | tf_op jit(solution)/shard_map/ppermute | solution.py:424
  25.5 1.8 %collective-permute-done.6.refs_8_ = bf16[256,1024]{1,0:T(8,128)(2,1)} collective-permute-done((bf16[256,1024]{1,0:T(8,128)(2,1)}, bf16[256,1024]{1,0:T(8,128)(2,1)}, u32[]{:S(2)}, u32[]{:S(2)}) %collective-permute-start.6) | collective-permute-done | bytes 524320 | tf_op jit(solution)/shard_map/ppermute | solution.py:475
  27.3 1.7 %collective-permute-start.8 = (bf16[2,16,16,128]{3,2,1,0:T(8,128)(2,1)S(1)}, bf16[2,16,16,128]{3,2,1,0:T(8,128)(2,1)S(1)}, u32[]{:S(2)}, u32[]{:S(2)}) collective-permute-start(bf16[2,16,16,128]{3,2,1,0:T(8,128)(2,1)S(1)} %slice_bitcast_fusion), channel_id=1, source_target_pairs={{0,6},{1,7},{2,0},{3,1},{4,2},{5,3},{6,4},{7,5},{8,14},{9,15},{10,... | collective-permute-start | bytes 393224 | tf_op jit(solution)/shard_map/ppermute | solution.py:428
  29.5 8.4 %collective-permute-done.11.refs_10_ = bf16[256,1024]{1,0:T(8,128)(2,1)S(1)} collective-permute-done((bf16[256,1024]{1,0:T(8,128)(2,1)}, bf16[256,1024]{1,0:T(8,128)(2,1)S(1)}, u32[]{:S(2)}, u32[]{:S(2)}) %collective-permute-start.11) | collective-permute-done | bytes 524320 | tf_op jit(solution)/shard_map/ppermute | solution.py:475
  39.3 6.1 %shard_map.258 = (f32[8,128,1024]{2,1,0:T(8,128)}, bf16[8,128,1024]{2,1,0:T(8,128)(2,1)}) custom-call(s32[5]{0:T(128)} %stack.35.meta_ref, bf16[2,2,16,16,128]{4,3,2,1,0:T(8,128)(2,1)} %copy-done.2, bf16[2,2,16,16,128]{4,3,2,1,0:T(8,128)(2,1)} %copy-done.5, bf16[2,2,16,16,128]{4,3,2,1,0:T(8,128)(2,1)} %copy-done.6, bf16[2,16,16,128]{3,2,1,0:T(8,128)(2,1)} %copy-done.14, ...), custom_call_target="tpu_custom_call" | custom-call | flops 5000000000 | bytes 7864340 | tf_op jit(solution)/shard_map/pallas_call | solution.py:397
  46.2 1.8 %collective-permute-start.10 = (bf16[256,1024]{1,0:T(8,128)(2,1)}, bf16[256,1024]{1,0:T(8,128)(2,1)}, u32[]{:S(2)}, u32[]{:S(2)}) collective-permute-start(bf16[256,1024]{1,0:T(8,128)(2,1)} %collective-permute-done.6.refs_8_), channel_id=1, source_target_pairs={{0,8},{8,0},{16,24},{24,16},{32,40},{40,32},{48,56},{56,48},{64,72... | collective-permute-start | bytes 1572872 | tf_op jit(solution)/shard_map/ppermute | solution.py:424
  47.9 5.8 %collective-permute-done.13.refs_12_ = bf16[128,1024]{1,0:T(8,128)(2,1)S(1)} collective-permute-done((bf16[128,1024]{1,0:T(8,128)(2,1)S(1)}, bf16[128,1024]{1,0:T(8,128)(2,1)S(1)}, u32[]{:S(2)}, u32[]{:S(2)}) %collective-permute-start.13) | collective-permute-done | bytes 262176 | tf_op jit(solution)/shard_map/ppermute | solution.py:475
  56.0 4.9 %shard_map.255 = (f32[128,1024]{1,0:T(8,128)}, bf16[128,1024]{1,0:T(8,128)(2,1)}) custom-call(s32[5]{0:T(128)} %stack.35.meta_ref, bf16[2,2,16,16,128]{4,3,2,1,0:T(8,128)(2,1)} %copy-done.2, bf16[2,2,16,16,128]{4,3,2,1,0:T(8,128)(2,1)} %copy-done.5, bf16[2,2,16,16,128]{4,3,2,1,0:T(8,128)(2,1)} %copy-done.6, bf16[2,16,16,128]{3,2,1,0:T(8,128)(2,1)} %copy-done.14, ...), custom_call_target="tpu_custom_call" | custom-call | flops 4000000000 | bytes 6029332 | tf_op jit(solution)/shard_map/pallas_call | solution.py:397
  60.9 1.7 %collective-permute-start.15 = (bf16[128,1024]{1,0:T(8,128)(2,1)}, bf16[128,1024]{1,0:T(8,128)(2,1)S(1)}, u32[]{:S(2)}, u32[]{:S(2)}) collective-permute-start(bf16[128,1024]{1,0:T(8,128)(2,1)} %get-tuple-element.55), channel_id=1, source_target_pairs={{0,128},{128,0},{1,129},{129,1},{2,130},{130,2},{3,131},{131,3},{4... | collective-permute-start | bytes 786440 | tf_op jit(solution)/shard_map/ppermute | solution.py:424
  62.6 3.1 %collective-permute-start.22 = (bf16[128,1024]{1,0:T(8,128)(2,1)S(1)}, bf16[128,1024]{1,0:T(8,128)(2,1)S(1)}, u32[]{:S(2)}, u32[]{:S(2)}) collective-permute-start(bf16[128,1024]{1,0:T(8,128)(2,1)S(1)} %get-tuple-element.93), channel_id=1, source_target_pairs={{16,0},{32,16},{48,32},{64,48},{80,64},{96,80},{112,96},{0,112},{1... | collective-permute-start | bytes 786440 | tf_op jit(solution)/shard_map/ppermute | solution.py:478
  65.9 4.2 %collective-permute-done.15.refs_1_ = bf16[128,1024]{1,0:T(8,128)(2,1)S(1)} collective-permute-done((bf16[128,1024]{1,0:T(8,128)(2,1)}, bf16[128,1024]{1,0:T(8,128)(2,1)S(1)}, u32[]{:S(2)}, u32[]{:S(2)}) %collective-permute-start.15) | collective-permute-done | bytes 262176 | tf_op jit(solution)/shard_map/ppermute | solution.py:424
  70.8 7.9 %shard_map.257 = (bf16[128,1024]{1,0:T(8,128)(2,1)}, bf16[128,1024]{1,0:T(8,128)(2,1)}, bf16[128,128]{1,0:T(8,128)(2,1)}, bf16[128,128]{1,0:T(8,128)(2,1)}, bf16[16,128]{1,0:T(8,128)(2,1)}, /*index=5*/f32[56,128]{1,0:T(8,128)}) custom-call(s32[5]{0:T(128)} %stack.35.meta_ref, f32[128,1024]{1,0:T(8,128)} %get-tuple-element.54.refs_0_, ...), custom_call_target="tpu_custom_call" | custom-call | flops 10000000000 | bytes 4817556 | tf_op jit(solution)/shard_map/pallas_call | solution.py:397
  82.5 5.6 %collective-permute-done.17 = f32[56,128]{1,0:T(8,128)S(1)} collective-permute-done((f32[56,128]{1,0:T(8,128)S(1)}, f32[56,128]{1,0:T(8,128)S(1)}, u32[]{:S(2)}, u32[]{:S(2)}) %collective-permute-start.17) | collective-permute-done | bytes 28704 | tf_op jit(solution)/shard_map/ppermute | solution.py:424
  88.7 3.2 %collective-permute-start.24 = (bf16[128,1024]{1,0:T(8,128)(2,1)S(1)}, bf16[128,1024]{1,0:T(8,128)(2,1)S(1)}, u32[]{:S(2)}, u32[]{:S(2)}) collective-permute-start(bf16[128,1024]{1,0:T(8,128)(2,1)S(1)} %get-tuple-element.76), channel_id=1, source_target_pairs={{16,0},{32,16},{48,32},{64,48},{80,64},{96,80},{112,96},{0,112},{1... | collective-permute-start | bytes 786440 | tf_op jit(solution)/shard_map/ppermute | solution.py:478
  93.1 2.7 %collective-permute-done.18 = f32[56,128]{1,0:T(8,128)S(1)} collective-permute-done((f32[56,128]{1,0:T(8,128)S(1)}, f32[56,128]{1,0:T(8,128)S(1)}, u32[]{:S(2)}, u32[]{:S(2)}) %collective-permute-start.18) | collective-permute-done | bytes 28704 | tf_op jit(solution)/shard_map/ppermute | solution.py:424
  96.0 4.6 %collective-permute-done.19 = f32[56,128]{1,0:T(8,128)S(1)} collective-permute-done((f32[56,128]{1,0:T(8,128)S(1)}, f32[56,128]{1,0:T(8,128)S(1)}, u32[]{:S(2)}, u32[]{:S(2)}) %collective-permute-start.19) | collective-permute-done | bytes 28704 | tf_op jit(solution)/shard_map/ppermute | solution.py:424
  102.0 4.5 %collective-permute-start.30 = (f32[56,128]{1,0:T(8,128)S(1)}, f32[56,128]{1,0:T(8,128)S(1)}, u32[]{:S(2)}, u32[]{:S(2)}) collective-permute-start(f32[56,128]{1,0:T(8,128)S(1)} %add.80.par_ref), channel_id=1, source_target_pairs={{0,64},{8,72},{16,80},{24,88},{32,96},{40,104},{48,112},{56,120},{... | collective-permute-start | bytes 86024 | tf_op jit(solution)/shard_map/ppermute | solution.py:424
  (95 shorter events, 22.0 us)
Async XLA Ops:
  3.4 13.2 %collective-permute-start.3 = (bf16[256,1024]{1,0:T(8,128)(2,1)S(1)}, bf16[256,1024]{1,0:T(8,128)(2,1)}, u32[]{:S(2)}, u32[]{:S(2)}) collective-permute-start(bf16[256,1024]{1,0:T(8,128)(2,1)S(1)} %pad_maximum_fusion.refs_5_), channel_id=1, source_target_pairs={{0,16},{16,32},{32,48},{48,64},{64,80},{80,96},{96,112},{112,0},{8... | collective-permute-start | bytes 1572872 | tf_op jit(solution)/shard_map/ppermute | solution.py:475
  9.8 6.8 %collective-permute-start.2 = (bf16[2,16,16,128]{3,2,1,0:T(8,128)(2,1)S(1)}, bf16[2,16,16,128]{3,2,1,0:T(8,128)(2,1)S(1)}, u32[]{:S(2)}, u32[]{:S(2)}) collective-permute-start(bf16[2,16,16,128]{3,2,1,0:T(8,128)(2,1)S(1)} %pad_maximum_fusion.2), channel_id=1, source_target_pairs={{0,1},{1,0},{2,3},{3,2},{4,5},{5,4},{6,7},{7,6},{8,9},{9,8},{10,11... | collective-permute-start | bytes 393224 | tf_op jit(solution)/shard_map/ppermute | solution.py:424
  16.6 10.7 %collective-permute-start.6 = (bf16[256,1024]{1,0:T(8,128)(2,1)}, bf16[256,1024]{1,0:T(8,128)(2,1)}, u32[]{:S(2)}, u32[]{:S(2)}) collective-permute-start(bf16[256,1024]{1,0:T(8,128)(2,1)} %collective-permute-done.3.refs_6_), channel_id=1, source_target_pairs={{0,16},{16,32},{32,48},{48,64},{64,80},{80,96},{96,112},{112,0},{8... | collective-permute-start | bytes 1572872 | tf_op jit(solution)/shard_map/ppermute | solution.py:475
  16.6 12.3 %collective-permute-start.4 = (bf16[2,2,16,16,128]{4,3,2,1,0:T(8,128)(2,1)S(1)}, bf16[2,2,16,16,128]{4,3,2,1,0:T(8,128)(2,1)S(1)}, u32[]{:S(2)}, u32[]{:S(2)}) collective-permute-start(bf16[2,2,16,16,128]{4,3,2,1,0:T(8,128)(2,1)S(1)} %pad_maximum_fusion.1.refs_0_), channel_id=1, source_target_pairs={{0,2},{1,3},{2,4},{3,5},{4,6},{5,7},{6,0},{7,1},{8,10},{9,11},{10,... | collective-permute-start | bytes 786440 | tf_op jit(solution)/shard_map/ppermute | solution.py:428
  18.2 9.1 %collective-permute-start.5 = (bf16[2,2,16,16,128]{4,3,2,1,0:T(8,128)(2,1)S(1)}, bf16[2,2,16,16,128]{4,3,2,1,0:T(8,128)(2,1)S(1)}, u32[]{:S(2)}, u32[]{:S(2)}) collective-permute-start(bf16[2,2,16,16,128]{4,3,2,1,0:T(8,128)(2,1)S(1)} %pad_maximum_fusion.1.refs_0_), channel_id=1, source_target_pairs={{0,6},{1,7},{2,0},{3,1},{4,2},{5,3},{6,4},{7,5},{8,14},{9,15},{10,... | collective-permute-start | bytes 786440 | tf_op jit(solution)/shard_map/ppermute | solution.py:428
  23.8 14.1 %collective-permute-start.20 = (bf16[128,1024]{1,0:T(8,128)(2,1)}, bf16[128,1024]{1,0:T(8,128)(2,1)S(1)}, u32[]{:S(2)}, u32[]{:S(2)}) collective-permute-start(bf16[128,1024]{1,0:T(8,128)(2,1)} %get-tuple-element.72.refs_5_), channel_id=1, source_target_pairs={{0,128},{128,0},{1,129},{129,1},{2,130},{130,2},{3,131},{131,3},{4... | collective-permute-start | bytes 786440 | tf_op jit(solution)/shard_map/ppermute | solution.py:424
  27.3 10.6 %collective-permute-start.11 = (bf16[256,1024]{1,0:T(8,128)(2,1)}, bf16[256,1024]{1,0:T(8,128)(2,1)S(1)}, u32[]{:S(2)}, u32[]{:S(2)}) collective-permute-start(bf16[256,1024]{1,0:T(8,128)(2,1)} %collective-permute-done.6.refs_8_), channel_id=1, source_target_pairs={{0,16},{16,32},{32,48},{48,64},{64,80},{80,96},{96,112},{112,0},{8... | collective-permute-start | bytes 1572872 | tf_op jit(solution)/shard_map/ppermute | solution.py:475
  27.3 10.6 %collective-permute-start.8 = (bf16[2,16,16,128]{3,2,1,0:T(8,128)(2,1)S(1)}, bf16[2,16,16,128]{3,2,1,0:T(8,128)(2,1)S(1)}, u32[]{:S(2)}, u32[]{:S(2)}) collective-permute-start(bf16[2,16,16,128]{3,2,1,0:T(8,128)(2,1)S(1)} %slice_bitcast_fusion), channel_id=1, source_target_pairs={{0,6},{1,7},{2,0},{3,1},{4,2},{5,3},{6,4},{7,5},{8,14},{9,15},{10,... | collective-permute-start | bytes 393224 | tf_op jit(solution)/shard_map/ppermute | solution.py:428
  29.0 8.9 %collective-permute-start.7 = (bf16[2,16,16,128]{3,2,1,0:T(8,128)(2,1)S(1)}, bf16[2,16,16,128]{3,2,1,0:T(8,128)(2,1)S(1)}, u32[]{:S(2)}, u32[]{:S(2)}) collective-permute-start(bf16[2,16,16,128]{3,2,1,0:T(8,128)(2,1)S(1)} %slice_bitcast_fusion.1), channel_id=1, source_target_pairs={{0,2},{1,3},{2,4},{3,5},{4,6},{5,7},{6,0},{7,1},{8,10},{9,11},{10,... | collective-permute-start | bytes 393224 | tf_op jit(solution)/shard_map/ppermute | solution.py:428
  45.5 8.3 %collective-permute-start.21 = (bf16[8,128,1024]{2,1,0:T(8,128)(2,1)}, bf16[8,128,1024]{2,1,0:T(8,128)(2,1)S(1)}, u32[]{:S(2)}, u32[]{:S(2)}) collective-permute-start(bf16[8,128,1024]{2,1,0:T(8,128)(2,1)} %get-tuple-element.74), channel_id=1, source_target_pairs={{0,8},{8,0},{16,24},{24,16},{32,40},{40,32},{48,56},{56,48},{64,72... | collective-permute-start | bytes 6291464 | tf_op jit(solution)/shard_map/ppermute | solution.py:424
  45.6 9.7 %collective-permute-start.9 = (bf16[256,1024]{1,0:T(8,128)(2,1)}, bf16[256,1024]{1,0:T(8,128)(2,1)}, u32[]{:S(2)}, u32[]{:S(2)}) collective-permute-start(bf16[256,1024]{1,0:T(8,128)(2,1)} %collective-permute-done.3.refs_6_), channel_id=1, source_target_pairs={{0,8},{8,0},{16,24},{24,16},{32,40},{40,32},{48,56},{56,48},{64,72... | collective-permute-start | bytes 1572872 | tf_op jit(solution)/shard_map/ppermute | solution.py:424
  46.1 7.7 %collective-permute-start.13 = (bf16[128,1024]{1,0:T(8,128)(2,1)S(1)}, bf16[128,1024]{1,0:T(8,128)(2,1)S(1)}, u32[]{:S(2)}, u32[]{:S(2)}) collective-permute-start(bf16[128,1024]{1,0:T(8,128)(2,1)S(1)} %slice.97), channel_id=1, source_target_pairs={{0,16},{16,32},{32,48},{48,64},{64,80},{80,96},{96,112},{112,0},{8... | collective-permute-start | bytes 786440 | tf_op jit(solution)/shard_map/ppermute | solution.py:475
  46.2 9.1 %collective-permute-start.10 = (bf16[256,1024]{1,0:T(8,128)(2,1)}, bf16[256,1024]{1,0:T(8,128)(2,1)}, u32[]{:S(2)}, u32[]{:S(2)}) collective-permute-start(bf16[256,1024]{1,0:T(8,128)(2,1)} %collective-permute-done.6.refs_8_), channel_id=1, source_target_pairs={{0,8},{8,0},{16,24},{24,16},{32,40},{40,32},{48,56},{56,48},{64,72... | collective-permute-start | bytes 1572872 | tf_op jit(solution)/shard_map/ppermute | solution.py:424
  47.9 7.4 %collective-permute-start.12 = (bf16[256,1024]{1,0:T(8,128)(2,1)S(1)}, bf16[256,1024]{1,0:T(8,128)(2,1)}, u32[]{:S(2)}, u32[]{:S(2)}) collective-permute-start(bf16[256,1024]{1,0:T(8,128)(2,1)S(1)} %collective-permute-done.11.refs_10_), channel_id=1, source_target_pairs={{0,8},{8,0},{16,24},{24,16},{32,40},{40,32},{48,56},{56,48},{64,72... | collective-permute-start | bytes 1572872 | tf_op jit(solution)/shard_map/ppermute | solution.py:424
  55.2 10.5 %collective-permute-start.25 = (bf16[128,1024]{1,0:T(8,128)(2,1)S(1)}, bf16[128,1024]{1,0:T(8,128)(2,1)S(1)}, u32[]{:S(2)}, u32[]{:S(2)}) collective-permute-start(bf16[128,1024]{1,0:T(8,128)(2,1)S(1)} %get-tuple-element.94), channel_id=1, source_target_pairs={{0,16},{16,32},{32,48},{48,64},{64,80},{80,96},{96,112},{112,0},{8... | collective-permute-start | bytes 786440 | tf_op jit(solution)/shard_map/ppermute | solution.py:475
  60.9 9.2 %collective-permute-start.15 = (bf16[128,1024]{1,0:T(8,128)(2,1)}, bf16[128,1024]{1,0:T(8,128)(2,1)S(1)}, u32[]{:S(2)}, u32[]{:S(2)}) collective-permute-start(bf16[128,1024]{1,0:T(8,128)(2,1)} %get-tuple-element.55), channel_id=1, source_target_pairs={{0,128},{128,0},{1,129},{129,1},{2,130},{130,2},{3,131},{131,3},{4... | collective-permute-start | bytes 786440 | tf_op jit(solution)/shard_map/ppermute | solution.py:424
  62.6 16.2 %collective-permute-start.22 = (bf16[128,1024]{1,0:T(8,128)(2,1)S(1)}, bf16[128,1024]{1,0:T(8,128)(2,1)S(1)}, u32[]{:S(2)}, u32[]{:S(2)}) collective-permute-start(bf16[128,1024]{1,0:T(8,128)(2,1)S(1)} %get-tuple-element.93), channel_id=1, source_target_pairs={{16,0},{32,16},{48,32},{64,48},{80,64},{96,80},{112,96},{0,112},{1... | collective-permute-start | bytes 786440 | tf_op jit(solution)/shard_map/ppermute | solution.py:478
  65.8 13.0 %collective-permute-start.26 = (bf16[128,1024]{1,0:T(8,128)(2,1)S(1)}, bf16[128,1024]{1,0:T(8,128)(2,1)S(1)}, u32[]{:S(2)}, u32[]{:S(2)}) collective-permute-start(bf16[128,1024]{1,0:T(8,128)(2,1)S(1)} %bitcast_add_fusion.2), channel_id=1, source_target_pairs={{0,16},{16,32},{32,48},{48,64},{64,80},{80,96},{96,112},{112,0},{8... | collective-permute-start | bytes 786440 | tf_op jit(solution)/shard_map/ppermute | solution.py:475
  79.0 9.0 %collective-permute-start.23 = (bf16[128,1024]{1,0:T(8,128)(2,1)S(1)}, bf16[128,1024]{1,0:T(8,128)(2,1)S(1)}, u32[]{:S(2)}, u32[]{:S(2)}) collective-permute-start(bf16[128,1024]{1,0:T(8,128)(2,1)S(1)} %get-tuple-element.75), channel_id=1, source_target_pairs={{16,0},{32,16},{48,32},{64,48},{80,64},{96,80},{112,96},{0,112},{1... | collective-permute-start | bytes 786440 | tf_op jit(solution)/shard_map/ppermute | solution.py:478
  79.9 8.5 %collective-permute-start.27 = (bf16[128,1024]{1,0:T(8,128)(2,1)S(1)}, bf16[128,1024]{1,0:T(8,128)(2,1)S(1)}, u32[]{:S(2)}, u32[]{:S(2)}) collective-permute-start(bf16[128,1024]{1,0:T(8,128)(2,1)S(1)} %get-tuple-element.78), channel_id=1, source_target_pairs={{0,16},{16,32},{32,48},{48,64},{64,80},{80,96},{96,112},{112,0},{8... | collective-permute-start | bytes 786440 | tf_op jit(solution)/shard_map/ppermute | solution.py:475
  88.6 12.0 %collective-permute-start.28 = (bf16[128,1024]{1,0:T(8,128)(2,1)S(1)}, bf16[128,1024]{1,0:T(8,128)(2,1)S(1)}, u32[]{:S(2)}, u32[]{:S(2)}) collective-permute-start(bf16[128,1024]{1,0:T(8,128)(2,1)S(1)} %get-tuple-element.79), channel_id=1, source_target_pairs={{0,16},{16,32},{32,48},{48,64},{64,80},{80,96},{96,112},{112,0},{8... | collective-permute-start | bytes 786440 | tf_op jit(solution)/shard_map/ppermute | solution.py:475
  88.7 11.9 %collective-permute-start.24 = (bf16[128,1024]{1,0:T(8,128)(2,1)S(1)}, bf16[128,1024]{1,0:T(8,128)(2,1)S(1)}, u32[]{:S(2)}, u32[]{:S(2)}) collective-permute-start(bf16[128,1024]{1,0:T(8,128)(2,1)S(1)} %get-tuple-element.76), channel_id=1, source_target_pairs={{16,0},{32,16},{48,32},{64,48},{80,64},{96,80},{112,96},{0,112},{1... | collective-permute-start | bytes 786440 | tf_op jit(solution)/shard_map/ppermute | solution.py:478
  100.7 6.6 %collective-permute-start.29 = (bf16[128,1024]{1,0:T(8,128)(2,1)S(1)}, bf16[128,1024]{1,0:T(8,128)(2,1)S(1)}, u32[]{:S(2)}, u32[]{:S(2)}) collective-permute-start(bf16[128,1024]{1,0:T(8,128)(2,1)S(1)} %fusion.1), channel_id=1, source_target_pairs={{0,128},{128,0},{1,129},{129,1},{2,130},{130,2},{3,131},{131,3},{4... | collective-permute-start | bytes 786440 | tf_op jit(solution)/shard_map/ppermute | solution.py:424
  102.0 7.8 %collective-permute-start.30 = (f32[56,128]{1,0:T(8,128)S(1)}, f32[56,128]{1,0:T(8,128)S(1)}, u32[]{:S(2)}, u32[]{:S(2)}) collective-permute-start(f32[56,128]{1,0:T(8,128)S(1)} %add.80.par_ref), channel_id=1, source_target_pairs={{0,64},{8,72},{16,80},{24,88},{32,96},{40,104},{48,112},{56,120},{... | collective-permute-start | bytes 86024 | tf_op jit(solution)/shard_map/ppermute | solution.py:424
  (22 other events, 106.9 us)
